TPU v7x, 512 devices: a whole 4x4x16 slice. The times are simulated.
512 devices in a mesh: depth: 16 (over x_hi, y, core), tile: 32 (over z, x_lo).
Axes of the slice: x: 4 (x_hi: 2, x_lo: 2; x = x_hi * 2 + x_lo), y: 4, z: 16, core: 2. Of those that a mesh axis runs over, the one named last changes fastest.
Arguments:
- volume: float32 [16, 1024, 1024], P('depth', 'tile'), may hold values from 0.05 to 100
- measured: float32 [1024, 1024], P('tile'), may hold values from 0.15 to 0.6
- point_spread: bfloat16 [16, 13, 13], P('depth'), may hold values from 7.390976e-05 to 0.0007362366
- entry_block: int32 [32, 4096], P('tile', 'depth'), may hold values from 0 to 63
- entry_neuron: int32 [32, 4096], P('tile', 'depth'), may hold values from -1 to 8191, as said below
- footprints: bfloat16 [32, 4096, 4, 128], P('tile', 'depth'), may hold values from 0.049804688 to 1
- seed_plane: int32 [8192], replicated, may hold values from 0 to 15
- seed_row: int32 [8192], replicated, may hold values from 0 to 1023
- seed_col: int32 [8192], replicated, may hold values from 0 to 1023
- owner_slot: int32 [8192], replicated, may hold values from 0 to 8191, each once
Outputs:
- estimate: float32 [16, 1024, 1024], P('depth', 'tile')
- demixed: float32 [8192], P(('depth', 'tile'))
Inputs may be any that keep to these rules, and one draw needn't show every extreme that they name: `entry_neuron`: -1 marks an empty slot; on each device the active slots come first, from 85 to 256 of them, and some device has all 256 slots active; neuron ids may repeat.
All inputs are finite; a program needn't handle non-finite values.
Results may differ from a plain program's by a relative error of at most 0.0025.
Values may be sent and summed in bfloat16 or wider, within the bound.
No kernel may reach another device: no remote copies, remote signals or barrier semaphores. Data moves between devices by JAX's collectives and lax.ppermute only.
A program may use at most 64 MiB of HBM per device.

v0:
```python
import jax
import jax.numpy as jnp
from jax import lax
from jax.sharding import PartitionSpec as P

ITERS = 2
RADIUS = 6
BR = 4
CB = 128


def padded_2(cells, sides, width):
    for axis, dim in sides:
        count = lax.axis_size(axis)
        ends = count - 1
        head = lax.slice_in_dim(cells, 0, width, axis=dim)
        tail = lax.slice_in_dim(cells, cells.shape[dim] - width, cells.shape[dim], axis=dim)
        cells = jnp.concatenate(
            [
                lax.ppermute(tail, axis, [(i, (i + 1) % count) for i in range(ends)]),
                cells,
                lax.ppermute(head, axis, [((i + 1) % count, i) for i in range(ends)]),
            ],
            axis=dim,
        )
    return cells


def band_tables(point_spread):
    kernel_size = point_spread.shape[1]
    radius = kernel_size // 2
    inner = jnp.arange(3 * CB)[:, None, None]
    outer = jnp.arange(CB)[None, :, None]
    tapnum = jnp.arange(kernel_size)[None, None, :]
    ahead_hot = (inner - CB - outer + radius == tapnum).astype(jnp.float32)
    behind_hot = (CB + outer + radius - inner == tapnum).astype(jnp.float32)
    spread_f = point_spread.astype(jnp.float32)
    high = lax.Precision.HIGHEST
    ahead = jnp.einsum("pak,jik->paji", spread_f, ahead_hot, precision=high).astype(jnp.bfloat16)
    behind = jnp.einsum("pak,jik->paji", spread_f, behind_hot, precision=high).astype(jnp.bfloat16)
    return (ahead, behind)


def column_blocks(field):
    shape = field.shape
    blocks = field.reshape(shape[:-1] + (shape[-1] // CB, CB))
    widths = [(0, 0)] * (len(shape) - 1)
    before = jnp.pad(blocks, widths + [(1, 0), (0, 0)])[..., :-1, :]
    after = jnp.pad(blocks, widths + [(0, 1), (0, 0)])[..., 1:, :]
    return jnp.concatenate([before, blocks, after], axis=-1)


def project_ahead(padded, ahead, rows_dev):
    stacked = column_blocks(padded)
    kernel_size = ahead.shape[1]
    summed = None
    for tapnum in range(kernel_size):
        term = jnp.einsum(
            "prnj,pji->rni",
            stacked[:, tapnum : tapnum + rows_dev],
            ahead[:, tapnum],
            preferred_element_type=jnp.float32,
        )
        summed = term if summed is None else summed + term
    return summed.reshape(rows_dev, -1)


def project_behind(padded, behind, rows_dev):
    stacked = column_blocks(padded)
    kernel_size = behind.shape[1]
    last = kernel_size - 1
    summed = None
    for tapnum in range(kernel_size):
        begin = last - tapnum
        term = jnp.einsum(
            "rnj,pji->prni",
            stacked[begin : begin + rows_dev],
            behind[:, tapnum],
            preferred_element_type=jnp.float32,
        )
        summed = term if summed is None else summed + term
    return summed.reshape(behind.shape[0], rows_dev, -1)


def body(
    volume,
    measured,
    point_spread,
    entry_block,
    entry_neuron,
    footprints,
    seed_plane,
    seed_row,
    seed_col,
    owner_slot,
):
    planes_dev, rows_dev, columns = volume.shape
    norm = jnp.sum(point_spread.astype(jnp.float32), axis=(1, 2))
    ahead, behind = band_tables(point_spread)
    estimate = volume
    for sweep in range(ITERS):
        rounded = estimate.astype(jnp.bfloat16)
        padded = padded_2(rounded, (("tile", 1),), RADIUS)
        partial_value = project_ahead(padded, ahead, rows_dev)
        plane_sum = lax.psum(partial_value.astype(jnp.bfloat16), "depth").astype(jnp.float32)
        ratio = (measured / plane_sum).astype(jnp.bfloat16)
        ratio_padded = padded_2(ratio, (("tile", 0),), RADIUS)
        backward = project_behind(ratio_padded, behind, rows_dev)
        estimate = estimate * backward / norm[:, None, None]
    row_groups = rows_dev // BR
    col_groups = columns // CB
    blocked = estimate.reshape(planes_dev, row_groups, BR, col_groups, CB).transpose(0, 1, 3, 2, 4)
    blocked = blocked.reshape(planes_dev * row_groups * col_groups, BR, CB)
    block_ids = entry_block[0]
    neuron = entry_neuron[0]
    weights = footprints[0].astype(jnp.float32)
    active = (neuron >= 0).astype(jnp.float32)
    neurons = seed_plane.shape[0]
    slot_pos = owner_slot[jnp.maximum(neuron, 0)]
    picked = blocked[block_ids]
    slot_proj = jnp.sum(weights * picked, axis=(1, 2)) * active
    proj_dense = jnp.zeros((neurons,), jnp.float32).at[slot_pos].add(slot_proj)
    holder = (seed_plane // planes_dev == lax.axis_index("depth")) & (
        seed_row // rows_dev == lax.axis_index("tile")
    )
    seed_value = estimate[seed_plane % planes_dev, seed_row % rows_dev, seed_col] * holder.astype(
        jnp.float32
    )
    seed_dense = jnp.zeros((neurons,), jnp.float32).at[owner_slot].add(seed_value)
    group = lax.axis_size(("depth", "tile"))
    owned_count = neurons // group
    proj_all, seed_all = lax.psum((proj_dense, seed_dense), ("depth", "tile"))
    offset = lax.axis_index(("depth", "tile")) * owned_count
    proj_own = lax.dynamic_slice_in_dim(proj_all, offset, owned_count, 0)
    seed_own = lax.dynamic_slice_in_dim(seed_all, offset, owned_count, 0)
    scaled = weights * (seed_all[slot_pos] * active)[:, None, None]
    block_count = blocked.shape[0]
    selector = (jnp.arange(block_count)[:, None] == block_ids[None, :]).astype(jnp.float32)
    rebuilt = jnp.dot(
        selector,
        scaled.reshape(scaled.shape[0], BR * CB),
        precision=lax.Precision.HIGHEST,
        preferred_element_type=jnp.float32,
    )
    rebuilt = rebuilt.reshape(block_count, BR, CB)
    slot_over = jnp.sum(weights * rebuilt[block_ids], axis=(1, 2)) * active
    over_dense = jnp.zeros((neurons,), jnp.float32).at[slot_pos].add(slot_over)
    over_own = lax.psum_scatter(over_dense, ("depth", "tile"), scatter_dimension=0, tiled=True)
    demixed = seed_own * proj_own / (over_own + 100.0 * seed_own)
    return (estimate, demixed)


def solution(mesh):
    in_specs = (
        P("depth", "tile", None),
        P("tile", None),
        P("depth", None, None),
        P("tile", "depth"),
        P("tile", "depth"),
        P("tile", "depth", None, None),
        P(),
        P(),
        P(),
        P(),
    )
    out_specs = (P("depth", "tile", None), P(("depth", "tile")))
    return jax.shard_map(body, mesh=mesh, in_specs=in_specs, out_specs=out_specs, check_vma=False)
```

profile of v0, /device:TPU:1, one launch (start us, length us, event | category | flops | bytes accessed | tf_op | source)
XLA Modules:
  0.0 1035.0 jit_solution(12849229935386808176)
XLA Ops:
  7.2 0.9 convert_element_type.84
  8.7 4.5 collective-permute-start
  13.3 1.3 collective-permute-start.1
  14.7 1.6 fusion.7
  16.3 2.7 fusion.173
  19.1 0.9 fusion.6
  20.0 3.2 fusion.172
  23.3 1.7 gather_fusion.1
  29.7 148.9 %all-reduce.14.cloned.1.call-done = bf16[32,1024]{1,0:T(8,128)(2,1)} async-done(((bf16[32,1024]{1,0:T(8,128)(2,1)}), bf16[32,1024]{1,0:T(8,128)(2,1)}) %all-reduce.14.cloned.1.call-update) | async-done | bytes 65552 | tf_op jit(solution)/shard_map/psum | solution.py:105
  179.5 2.3 collective-permute-start.2
  181.9 1.3 collective-permute-start.3
  183.8 3.3 collective-permute-done.3
  187.3 1.2 fusion.41
  188.5 1.2 convolution_add_fusion.35
  193.3 4.4 collective-permute-start.4
  197.7 1.3 collective-permute-start.5
  199.0 3.2 collective-permute-done.5
  206.1 144.1 %all-reduce.16.cloned.1.call-done = bf16[32,1024]{1,0:T(8,128)(2,1)} async-done(((bf16[32,1024]{1,0:T(8,128)(2,1)}), bf16[32,1024]{1,0:T(8,128)(2,1)}) %all-reduce.16.cloned.1.call-update) | async-done | bytes 65552 | tf_op jit(solution)/shard_map/psum | solution.py:105
  351.0 2.2 collective-permute-start.6
  353.2 1.5 collective-permute-start.7
  355.0 3.5 collective-permute-done.7
  362.6 65.0 %gather_fusion = f32[8192]{0:T(1024)S(1)} fusion(f32[1,32,1024]{2,1,0:T(8,128)S(1)} %fusion.44, s32[8192]{0:T(1024)S(1)} %fusion.156), kind=kCustom, calls=%fused_computation | custom fusion | bytes 163840 | tf_op jit(solution)/shard_map/gather | solution.py:126
  427.6 43.2 %scatter_custom_fusion = f32[8192]{0:T(1024)S(1)} fusion(s32[8192]{0:T(1024)S(1)} %compare_select_fusion.2, f32[8192]{0:T(1024)S(1)} %and_select_fusion, f32[]{:T(128)} %constant.76.clone.1), kind=kCustom, calls=%fused_computation.290 | custom fusion | flops 8192 | bytes 32772 | tf_op jit(solution)/shard_map/scatter-add | solution.py:129
  470.9 109.2 %psum.30 = f32[8192]{0:T(1024)S(1)} all-reduce(f32[8192]{0:T(1024)S(1)} %scatter_custom_fusion), channel_id=1, replica_groups=mesh['depth'=16,'tile'=32] {'depth','tile'}, use_global_device_ids=true, to_apply=%region_4.5 | all-reduce | flops 8192 | bytes 65536 | tf_op jit(solution)/shard_map/psum | solution.py:132
  580.1 1.7 gather_fusion.3
  582.6 1.0 gather_fusion.4
  583.6 1.0 gather_fusion.2
  584.6 1.0 fusion.12
  585.6 2.7 scatter_custom_fusion.1
  588.3 2.7 scatter_custom_fusion.2
  591.0 436.1 %all-reduce.18.cloned.1.call-done = (f32[8192]{0:T(1024)}, f32[8192]{0:T(1024)}) async-done(((f32[8192]{0:T(1024)}, f32[8192]{0:T(1024)}), (f32[8192]{0:T(1024)}, f32[8192]{0:T(1024)})) %all-reduce.18.cloned.1.call-update) | async-done | bytes 65552
  1027.2 1.3 fusion.170
  (181 shorter events, 19.8 us)
Async XLA Ops:
  7.2 171.5 %all-reduce.14.cloned.1.call-start = ((), (), s32[]{:S(2)}) async-start(), calls=%async_computation | async-start | bytes 131072 | tf_op jit(solution)/shard_map/psum | solution.py:105
  8.7 16.3 %collective-permute-start = (bf16[1,6,1024]{2,1,0:T(8,128)(2,1)}, bf16[1,6,1024]{2,1,0:T(8,128)(2,1)}, u32[]{:S(2)}, u32[]{:S(2)}) collective-permute-start(bf16[1,6,1024]{2,1,0:T(8,128)(2,1)} %get-tuple-element.46), channel_id=1, source_target_pairs={{0,1},{1,2},{2,3},{3,4},{4,5},{5,6},{6,7},{7,8},{8,9},{9,10},{10,1... | collective-permute-start | bytes 36872 | tf_op jit(solution)/shard_map/ppermute | solution.py:20
  13.3 11.8 %collective-permute-start.1 = (bf16[1,6,1024]{2,1,0:T(8,128)(2,1)}, bf16[1,6,1024]{2,1,0:T(8,128)(2,1)}, u32[]{:S(2)}, u32[]{:S(2)}) collective-permute-start(bf16[1,6,1024]{2,1,0:T(8,128)(2,1)} %get-tuple-element.47), channel_id=1, source_target_pairs={{1,0},{2,1},{3,2},{4,3},{5,4},{6,5},{7,6},{8,7},{9,8},{10,9},{11,1... | collective-permute-start | bytes 36872 | tf_op jit(solution)/shard_map/ppermute | solution.py:22
  16.3 2.7 copy-start.26
  19.0 7.5 copy-start.6
  19.0 7.7 copy-start.4
  20.0 3.3 copy-start.1
  20.0 3.2 copy-start.30
  20.0 5.0 copy-start.25
  20.0 5.0 copy-start.27
  27.8 1.9 copy-start.29
  27.9 150.8 %copy-start.8 = (f32[32,1024]{1,0:T(8,128)S(1)}, f32[32,1024]{1,0:T(8,128)}, u32[]{:S(2)}) copy-start(f32[32,1024]{1,0:T(8,128)} %param.11) | copy-start | bytes 393220
  29.7 320.5 %all-reduce.16.cloned.1.call-start = ((), (), s32[]{:S(2)}) async-start(), calls=%async_computation.1 | async-start | bytes 131072 | tf_op jit(solution)/shard_map/psum | solution.py:105
  179.5 10.2 copy-start.21
  179.5 4.2 collective-permute-start.2
  181.9 5.2 collective-permute-start.3
  187.2 3.1 copy-start.19
  188.5 2.2 copy-start.17
  191.3 1.3 copy-start.2
  192.5 10.3 copy-start.7
  193.3 9.8 copy-start.5
  193.3 5.7 collective-permute-start.4
  197.7 4.5 collective-permute-start.5
  204.2 150.6 %copy-start.3 = (bf16[1,256,4,128]{3,2,1,0:T(4,128)(2,1)S(1)}, bf16[1,256,4,128]{3,2,1,0:T(4,128)(2,1)}, u32[]{:S(2)}) copy-start(bf16[1,256,4,128]{3,2,1,0:T(4,128)(2,1)} %param.15) | copy-start | bytes 786436
  205.3 153.3 %copy-start.24 = (bf16[1,1,384,128]{3,1,2,0:T(2,128)(2,1)S(1)}, bf16[1,1,384,128]{3,1,2,0:T(2,128)(2,1)}, u32[]{:S(2)}) copy-start(bf16[1,1,384,128]{3,1,2,0:T(2,128)(2,1)} %get-tuple-element.18) | copy-start | bytes 294916
  206.0 821.2 %all-reduce.18.cloned.1.call-start = ((), (), s32[]{:S(2)}) async-start(), calls=%async_computation.2 | async-start | bytes 131072
  351.0 3.9 collective-permute-start.6
  353.2 5.2 collective-permute-start.7
  354.8 4.1 copy-start.23
  354.9 4.2 copy-start.22
  362.6 219.9 %copy-start = (f32[1,32,1024]{2,1,0:T(8,128)}, f32[1,32,1024]{2,1,0:T(8,128)S(1)}, u32[]{:S(2)}) copy-start(f32[1,32,1024]{2,1,0:T(8,128)S(1)} %fusion.44) | copy-start | bytes 393220
  362.6 65.0 %copy-start.28 = (s32[8192]{0:T(1024)S(1)}, s32[8192]{0:T(1024)}, u32[]{:S(2)}) copy-start(s32[8192]{0:T(1024)} %param.16) | copy-start | bytes 98308
  (10 other events, 10.5 us)
Sparse Core Ops, SparseCore 0:
  29.8 148.7 all-reduce.13
  206.1 144.0 all-reduce.15
  591.1 435.9 all-reduce.17
where the time goes:
time: 1040 us; the launch traced here: 1030 us
  waiting for transfers between devices  739 us (71%)
  blocking collectives  109 us (10%)
  local copies, waits for them, and re-layouts  79.5 us (8%)
  other arithmetic  56.9 us (5%)
  starting transfers between devices  18.9 us (2%)
  matrix products  16.2 us (2%)
  between operations  15.1 us (1%)
    unnamed x4, waiting for transfers between devices  436 us
    psum x2, waiting for transfers between devices, body(): lax.psum(partial_value.astype(jnp.bfloat16), 'depth').astype(jnp.float32)  293 us
    psum x1, blocking collectives, body(): proj_all, seed_all = lax.psum((proj_dense, seed_dense), ('depth', 'tile'))  109 us
    gather x1, local copies, waits for them, and re-layouts, body(): estimate[seed_plane % planes_dev, seed_row % rows_dev, seed_col]  65 us
    scatter-add x1, other arithmetic, body(): jnp.zeros((neurons,), jnp.float32).at[owner_slot].add(seed_value)  43.2 us
  transfers between devices with their start and end apart: 11, of which 6 were waited for; matrix products, arithmetic and copies ran while one was open for 1% of the time, Pallas kernels for 0%

commit v1 on v0

v1 whole, which is shorter than its diff:
```python
import jax
import jax.numpy as jnp
from jax import lax
from jax.experimental import pallas as pl
from jax.experimental.pallas import tpu as pltpu
from jax.sharding import PartitionSpec as P

F32 = jnp.float32
BF16 = jnp.bfloat16
I32 = jnp.int32
KS = 13
RADIUS = 6
ROWS = 32
COLS = 1024
CB = 128
NCB = COLS // CB
DEPTHS = 16
TILES = 32
SLOTS = 256
NEURONS = 8192
HALO = 24
H1 = 48
H2 = 24
VMEM = pl.BlockSpec(memory_space=pltpu.VMEM)
SMEM = pl.BlockSpec(memory_space=pltpu.SMEM)


def call(kernel, outs, n_in, scalars=(), scratch=(), mib=24):
    return pl.pallas_call(
        kernel,
        out_shape=[jax.ShapeDtypeStruct(s, t) for s, t in outs],
        in_specs=[SMEM if i in scalars else VMEM for i in range(n_in)],
        out_specs=[VMEM] * len(outs),
        scratch_shapes=list(scratch),
        compiler_params=pltpu.CompilerParams(vmem_limit_bytes=mib * 2**20),
    )


def iota(shape, dim):
    return lax.broadcasted_iota(I32, shape, dim)


def band(psf, rows, inner, offset, flip):
    lanes = KS * inner
    lane = iota((1, lanes), 1)
    tap_b = jnp.zeros((1, lanes), I32)
    for m in range(1, KS):
        tap_b = tap_b + (lane >= m * inner).astype(I32)
    inside = lane - tap_b * inner
    pick_b = (KS - 1) - tap_b if flip else tap_b
    hot = (iota((CB, lanes), 0) == pick_b).astype(F32).astype(BF16)
    taps = jnp.dot(psf, hot, preferred_element_type=F32)
    delta = inside - iota((rows, lanes), 0) + offset
    result = jnp.zeros((rows, lanes), F32)
    for m in range(KS):
        a = (KS - 1) - m if flip else m
        result = jnp.where(delta == m, taps[a : a + 1, :], result)
    return result.astype(BF16)


def shifted(field, stack):
    rows = field.shape[0]
    padded = jnp.concatenate([field, jnp.zeros((rows, CB), F32)], axis=1)
    width = COLS + CB
    for b in range(KS):
        shift = (RADIUS - b) % width
        moved = pltpu.roll(padded, shift, 1) if shift else padded
        stack[b * rows : (b + 1) * rows, :] = moved[:, :COLS].astype(BF16)


def split2(x):
    high = x.astype(BF16)
    return high, (x - high.astype(F32)).astype(BF16)


def split3(x):
    high = x.astype(BF16)
    rest = x - high.astype(F32)
    mid = rest.astype(BF16)
    return high, mid, (rest - mid.astype(F32)).astype(BF16)


def column_of(row):
    n = row.shape[1]
    return jnp.transpose(jnp.broadcast_to(row, (CB, n)))


def prepare_kernel(psf, block, neuron, weights, owner, t1f, t1b, t2f, t2b, gram, q_row, q_col, n_col, b_col):
    spread = psf[...]
    t1f[...] = band(spread, 80, 80, 0, False)
    t1b[...] = band(spread, 64, 80, 4, True)
    t2f[...] = band(spread, 48, 64, -4, False)
    t2b[...] = band(spread, 32, 48, 0, True)
    foot = weights[...]
    product = lax.dot_general(foot, foot, (((1,), (1,)), ((), ())), preferred_element_type=F32)
    blocks = column_of(block[...].astype(F32))
    neurons = column_of(neuron[...].astype(F32))
    same = jnp.concatenate([blocks, blocks], axis=1) == block[...].astype(F32)
    gram[...] = jnp.where(same, product, 0.0)
    n_int = neurons.astype(I32)
    n_col[...] = n_int
    b_col[...] = blocks.astype(I32)
    table = owner[...]
    tables = jnp.concatenate([(table >> 7).astype(F32), (table & 127).astype(F32)], axis=1).astype(BF16)
    hot = (iota((SLOTS, 64), 1) == (n_int[:, :64] >> 7)).astype(F32).astype(BF16)
    found = jnp.dot(hot, tables, preferred_element_type=F32)
    lane_hot = iota((SLOTS, CB), 1) == (n_int & 127)
    value = jnp.where(lane_hot, found[:, :CB] * 128.0 + found[:, CB:], 0.0)
    place = jnp.sum(value, axis=1, keepdims=True)
    place = jnp.broadcast_to(place, (SLOTS, CB))
    place = jnp.where(n_int >= 0, place, -1.0)
    q_col[...] = place.astype(I32)
    q_row[...] = jnp.transpose(place)[0:8, :].astype(I32)


def forward1_kernel(where, psf_band, volume, left, right, measured, pieces, meas1, meas2, stack):
    half = where[0]
    field = jnp.concatenate([left[:, :COLS], volume[...], right[:, :COLS]], axis=0)
    shifted(field, stack)
    value = jnp.dot(psf_band[...], stack[...], preferred_element_type=F32)
    for cb in range(NCB):
        part = value[:, cb * CB : (cb + 1) * CB].astype(BF16)
        pieces[2 * cb] = part[:H1]
        pieces[2 * cb + 1, 0:32, :] = part[H1:]
        pieces[2 * cb + 1, 32:48, :] = jnp.zeros((16, CB), BF16)
    sensor = jnp.concatenate([left[:, COLS:], measured[...], right[:, COLS:]], axis=0)
    second = jnp.concatenate([sensor[54:80], jnp.zeros((22, CB), F32)], axis=0)
    meas1[...] = jnp.where(half == 0, sensor[6:54], second)
    meas2[...] = jnp.where(half == 0, sensor[18:42], sensor[42:66])


def ratio_kernel(rows, valid, pad):
    def kernel(where, parts, measured, out):
        total = parts[0].astype(F32)
        for j in range(1, DEPTHS):
            total = total + parts[j].astype(F32)
        sensor = measured[...]
        inside = (iota((rows, CB), 0) + where[0] * rows < valid) & (sensor != 0.0)
        ratio = jnp.where(inside, sensor / jnp.where(inside, total, 1.0), 0.0)
        if pad:
            ratio = jnp.concatenate([ratio, jnp.zeros((pad, CB), F32)], axis=0)
        ratio = ratio.astype(BF16)
        for j in range(DEPTHS):
            out[j] = ratio

    return kernel


def spread_norm(psf):
    return jnp.sum(jnp.sum(psf[...].astype(F32), axis=0, keepdims=True), axis=1, keepdims=True)


def middle_kernel(psf, band_b, band_f, volume, left, right, ratio, pieces, estimate, stack_b, stack_f):
    columns = []
    for cb in range(NCB):
        columns.append(jnp.concatenate([ratio[2 * cb].astype(F32), ratio[2 * cb + 1].astype(F32)[:32]], axis=0))
    shifted(jnp.concatenate(columns, axis=1), stack_b)
    backward = jnp.dot(band_b[...], stack_b[...], preferred_element_type=F32)
    field = jnp.concatenate([left[8:24, :COLS], volume[...], right[0:16, :COLS]], axis=0)
    updated = field * backward / spread_norm(psf)
    estimate[...] = updated[16:48]
    shifted(updated, stack_f)
    value = jnp.dot(band_f[...], stack_f[...], preferred_element_type=F32)
    for cb in range(NCB):
        pieces[2 * cb] = value[:H2, cb * CB : (cb + 1) * CB]
        pieces[2 * cb + 1] = value[H2:, cb * CB : (cb + 1) * CB]


def last_kernel(where, psf, band_b, before, ratio, weights, b_col, s_plane, s_row, s_col, estimate, seeds, proj, stack, lines):
    columns = []
    for cb in range(NCB):
        columns.append(
            jnp.concatenate([ratio[2 * cb].astype(F32)[:H2], ratio[2 * cb + 1].astype(F32)[:H2]], axis=0)
        )
    shifted(jnp.concatenate(columns, axis=1), stack)
    backward = jnp.dot(band_b[...], stack[...], preferred_element_type=F32)
    updated = before[...] * backward / spread_norm(psf)
    estimate[...] = updated
    tall = jnp.concatenate([updated[:, c * CB : (c + 1) * CB] for c in range(NCB)], axis=0)
    flat = jnp.transpose(tall)
    left_side = jnp.concatenate(split2(flat), axis=0)
    chunk = NEURONS // DEPTHS
    for j in range(DEPTHS):
        row, col = s_row[j], s_col[j]
        local = (s_plane[j] == where[1]) & ((row >> 5) == where[2])
        key = jnp.where(local, (col >> 7) * ROWS + (row & (ROWS - 1)), -1)
        hot = (iota((SLOTS, chunk), 0) == key).astype(F32).astype(BF16)
        found = jnp.dot(left_side, hot, preferred_element_type=F32)
        found = found[:CB] + found[CB:]
        seeds[j] = jnp.sum(
            jnp.where(iota((CB, chunk), 0) == (col & (CB - 1)), found, 0.0), axis=0, keepdims=True
        )
    lines[...] = tall
    blocks = [lines[pl.ds(br, 64, stride=4), :] for br in range(4)]
    blocked = jnp.concatenate(blocks, axis=1)
    number = b_col[:, :64]
    number = (number & 7) * 8 + (number >> 3)
    hot = (iota((SLOTS, 64), 1) == number).astype(F32).astype(BF16)
    high, low = split2(blocked)
    picked = jnp.dot(hot, high, preferred_element_type=F32) + jnp.dot(hot, low, preferred_element_type=F32)
    product = weights[...].astype(F32) * picked
    total = product[:, :CB]
    for br in range(1, 4):
        total = total + product[:, br * CB : (br + 1) * CB]
    proj[...] = jnp.broadcast_to(jnp.sum(total, axis=1, keepdims=True), (SLOTS, CB))


def slots_kernel(where, initial, owner, gram, q_row, q_col, n_col, proj, out, own):
    table = jnp.concatenate([initial[j] for j in range(DEPTHS)], axis=0)
    chunk = NEURONS // DEPTHS
    number = n_col[...]
    hot = (iota((SLOTS, DEPTHS), 1) == (number[:, :DEPTHS] >> 9)).astype(F32).astype(BF16)
    parts = split3(table)
    found = jnp.dot(hot, parts[0], preferred_element_type=F32)
    found = found + jnp.dot(hot, parts[1], preferred_element_type=F32)
    found = found + jnp.dot(hot, parts[2], preferred_element_type=F32)
    wide = jnp.concatenate([number] * 4, axis=1) & (chunk - 1)
    value = jnp.where(iota((SLOTS, chunk), 1) == wide, found, 0.0)
    value = value[:, :128] + value[:, 128:256] + value[:, 256:384] + value[:, 384:]
    start = jnp.broadcast_to(jnp.sum(value, axis=1, keepdims=True), (SLOTS, CB))
    start_row = jnp.transpose(start)[0:1, :]
    terms = gram[...] * start_row
    over = jnp.sum(terms[:, :CB] + terms[:, CB:], axis=1, keepdims=True)
    place = q_col[...]
    lane = iota((SLOTS, CB), 1)
    target = ((place >> 4) & 3) * 32 + (place & 15)
    sent = jnp.where(lane == target, proj[...], 0.0) + jnp.where(lane == target + 16, over, 0.0)
    row_hot = (iota((CB, SLOTS), 0) == (q_row[0:1, :] >> 6)).astype(F32).astype(BF16)
    parts = split3(sent)
    dense = jnp.dot(row_hot, parts[0], preferred_element_type=F32)
    dense = dense + jnp.dot(row_hot, parts[1], preferred_element_type=F32)
    dense = dense + jnp.dot(row_hot, parts[2], preferred_element_type=F32)
    for j in range(DEPTHS):
        out[j] = dense[j * 8 : (j + 1) * 8]
    base = where[3]
    holder = owner[...]
    lanes = iota((1, CB), 1)
    result = jnp.zeros((1, CB), F32)
    for i in range(16):
        mine = jnp.sum(jnp.where(holder == base + i, table, 0.0), axis=0, keepdims=True)
        result = jnp.where(lanes == i, jnp.sum(mine, axis=1, keepdims=True), result)
    own[...] = result


def fold_kernel(parts, out):
    total = parts[0]
    for j in range(1, DEPTHS):
        total = total + parts[j]
    for m in range(4):
        moved = pltpu.roll(total, (CB - 32 * m) % CB, 1) if m else total
        for r in range(8):
            out[4 * r + m] = moved[r : r + 1]


def final_kernel(parts, own, out):
    total = parts[0]
    for j in range(1, TILES):
        total = total + parts[j]
    over = pltpu.roll(total, CB - 16, 1)
    initial = own[...]
    real = iota((1, CB), 1) < 16
    bottom = jnp.where(real, over + 100.0 * initial, 1.0)
    out[...] = jnp.where(real, initial * total, 0.0) / bottom


def swap(pieces, axis):
    return lax.all_to_all(pieces, axis, 0, 0)


def body(
    volume,
    measured,
    point_spread,
    entry_block,
    entry_neuron,
    footprints,
    seed_plane,
    seed_row,
    seed_col,
    owner_slot,
):
    d = lax.axis_index("depth")
    t = lax.axis_index("tile")
    where = jnp.stack([d % 2, d, t, (d * TILES + t) * 16]).astype(I32)
    vol = volume[0]
    sensor = lax.dynamic_slice(measured, (0, (d // 2) * CB), (ROWS, CB))
    down = jnp.concatenate([vol[ROWS - HALO :], sensor[ROWS - HALO :]], axis=1)
    up = jnp.concatenate([vol[:HALO], sensor[:HALO]], axis=1)
    left = lax.ppermute(down, "tile", [(i, i + 1) for i in range(TILES - 1)])
    right = lax.ppermute(up, "tile", [(i + 1, i) for i in range(TILES - 1)])
    psf = jnp.pad(point_spread[0], ((0, 16 - KS), (0, CB - KS)))
    weights = footprints[0].reshape(SLOTS, 512)
    t1f, t1b, t2f, t2b, gram, q_row, q_col, n_col, b_col = call(
        prepare_kernel,
        [
            ((80, KS * 80), BF16),
            ((64, KS * 80), BF16),
            ((48, KS * 64), BF16),
            ((32, KS * 48), BF16),
            ((SLOTS, SLOTS), F32),
            ((8, SLOTS), I32),
            ((SLOTS, CB), I32),
            ((SLOTS, CB), I32),
            ((SLOTS, CB), I32),
        ],
        5,
    )(psf, entry_block, entry_neuron, weights, owner_slot.reshape(64, CB))
    pieces, meas1, meas2 = call(
        forward1_kernel,
        [((DEPTHS, H1, CB), BF16), ((H1, CB), F32), ((H2, CB), F32)],
        6,
        scalars=(0,),
        scratch=[pltpu.VMEM((KS * 80, COLS), BF16)],
    )(where, t1f, vol, left, right, sensor)
    [ratio] = call(ratio_kernel(H1, 68, 0), [((DEPTHS, H1, CB), BF16)], 3, scalars=(0,))(
        where, swap(pieces, "depth"), meas1
    )
    pieces, before = call(
        middle_kernel,
        [((DEPTHS, H2, CB), F32), ((ROWS, COLS), F32)],
        7,
        scratch=[pltpu.VMEM((KS * 80, COLS), BF16), pltpu.VMEM((KS * 64, COLS), BF16)],
    )(psf, t1b, t2f, vol, left, right, swap(ratio, "depth"))
    [ratio] = call(ratio_kernel(H2, 44, 8), [((DEPTHS, 32, CB), BF16)], 3, scalars=(0,))(
        where, swap(pieces, "depth"), meas2
    )
    chunk = NEURONS // DEPTHS
    shape = (DEPTHS, 1, chunk)
    estimate, seeds, proj = call(
        last_kernel,
        [((ROWS, COLS), F32), (shape, F32), ((SLOTS, CB), F32)],
        10,
        scalars=(0,),
        scratch=[pltpu.VMEM((KS * 48, COLS), BF16), pltpu.VMEM((NCB * ROWS, CB), F32)],
    )(
        where,
        psf,
        t2b,
        before,
        swap(ratio, "depth"),
        weights,
        b_col,
        seed_plane.reshape(shape),
        seed_row.reshape(shape),
        seed_col.reshape(shape),
    )
    mine = jnp.sum(swap(seeds, "depth"), axis=0)
    mine = jnp.sum(swap(jnp.broadcast_to(mine, (TILES, 1, chunk)), "tile"), axis=0)
    initial = swap(jnp.broadcast_to(mine, shape), "depth")
    sent, own = call(slots_kernel, [((DEPTHS, 8, CB), F32), ((1, CB), F32)], 8, scalars=(0,))(
        where, initial, owner_slot.reshape(DEPTHS, chunk), gram, q_row, q_col, n_col, proj
    )
    [sent] = call(fold_kernel, [((TILES, 1, CB), F32)], 1)(swap(sent, "depth"))
    [demixed] = call(final_kernel, [((1, CB), F32)], 2)(swap(sent, "tile"), own)
    return estimate[None], demixed[0, :16]


def solution(mesh):
    in_specs = (
        P("depth", "tile", None),
        P("tile", None),
        P("depth", None, None),
        P("tile", "depth"),
        P("tile", "depth"),
        P("tile", "depth", None, None),
        P(),
        P(),
        P(),
        P(),
    )
    out_specs = (P("depth", "tile", None), P(("depth", "tile")))
    return jax.shard_map(body, mesh=mesh, in_specs=in_specs, out_specs=out_specs, check_vma=False)
```

time: 1040 us -> 153 us (0.15)
  waiting for transfers between devices: 739 us -> 8.09 us
  local copies, waits for them, and re-layouts: 79.5 us -> 5.11 us
  other arithmetic: 56.9 us -> 0.21 us
  matrix products: 16.2 us -> 0 us
  between operations: 15.1 us -> 0.81 us
  Pallas kernels: 0 us -> 11.4 us
    unnamed x4 -> x0, waiting for transfers between devices: 436 us -> none
    psum x2 -> x0, waiting for transfers between devices: 293 us -> none  [body(): lax.psum(partial_value.astype(jnp.bfloat16), 'depth').astype(jnp.float32)]
    all_to_all x0 -> x8, blocking collectives: none -> 116 us  [swap(): return lax.all_to_all(pieces, axis, 0, 0)]
    psum x1 -> x0, blocking collectives: 109 us -> none  [body(): proj_all, seed_all = lax.psum((proj_dense, seed_dense), ('depth', 'tile'))]
    gather x5 -> x0, local copies, waits for them, and re-layouts: 70.4 us -> none  [the longest x1 65 us: body(): estimate[seed_plane % planes_dev, seed_row % rows_dev, seed_col]]
    scatter-add x3 -> x0, other arithmetic: 48.6 us -> none  [the longest x1 43.2 us: body(): jnp.zeros((neurons,), jnp.float32).at[owner_slot].add(seed_value)]
    dot_general x55 -> x0, matrix products: 16.2 us -> none  [the longest x26 7.61 us: project_behind(): jnp.einsum('rnj,pji->prni', stacked[begin:begin + rows_dev], behind[:, ta...]
    ppermute x8 -> x2, starting transfers between devices: 18.8 us -> 5.24 us  [the longest x1 3.95 us: body(): left = lax.ppermute(down, 'tile', [(i, i + 1) for i in range(TILES - 1)])]
  transfers between devices with their start and end apart: 11 -> 3, of which waited for: 6 -> 2; matrix products, arithmetic and copies ran while one was open for 1% -> 1% of each run, Pallas kernels for 0% -> 1%
where the time goes in v1:
time: 153 us; the launch traced here: 152 us
  blocking collectives  116 us (76%)
  Pallas kernels  11.4 us (7%)
  starting transfers between devices  10.6 us (7%)
  waiting for transfers between devices  8.09 us (5%)
  local copies, waits for them, and re-layouts  5.11 us (3%)
    all_to_all x8, blocking collectives, swap(): return lax.all_to_all(pieces, axis, 0, 0)  116 us
    all_to_all x1, waiting for transfers between devices, swap(): return lax.all_to_all(pieces, axis, 0, 0)  7.37 us
    all_to_all x1, starting transfers between devices, swap(): return lax.all_to_all(pieces, axis, 0, 0)  5.33 us
    pallas_call x1, Pallas kernels, body(): call(last_kernel, [((ROWS, COLS), F32), (shape, F32), ((SLOTS, CB), F32)]...  4.19 us
    ppermute x1, starting transfers between devices, body(): left = lax.ppermute(down, 'tile', [(i, i + 1) for i in range(TILES - 1)])  3.95 us
  transfers between devices with their start and end apart: 3, of which 2 were waited for; matrix products, arithmetic and copies ran while one was open for 1% of the time, Pallas kernels for 1%

profile of v1, /device:TPU:1, one launch (start us, length us, event | category | flops | bytes accessed | tf_op | source)
XLA Modules:
  0.0 151.8 jit_solution(4533630327761561505)
XLA Ops:
  0.6 1.0 slice_bitcast_fusion
  1.7 0.8 constant_dynamic-slice_fusion
  2.5 4.0 %collective-permute-start = (f32[24,1152]{1,0:T(8,128)S(1)}, f32[24,1152]{1,0:T(8,128)S(1)}, u32[]{:S(2)}, u32[]{:S(2)}) collective-permute-start(f32[24,1152]{1,0:T(8,128)S(1)} %pad_maximum_fusion), channel_id=1, source_target_pairs={{0,1},{1,2},{2,3},{3,4},{4,5},{5,6},{6,7},{7,8},{8,9},{9,10},{10,1... | collective-permute-start | bytes 331784 | tf_op jit(solution)/shard_map/ppermute | solution.py:289
  6.4 1.3 collective-permute-start.1
  7.7 0.7 constant_dynamic-slice_fusion.1.measured
  8.5 0.7 copy-done.8
  9.2 0.0 copy-done.1
  9.2 0.7 copy-done.5
  9.9 1.4 shard_map.113
  11.3 0.1 pad_add_fusion.where
  11.4 0.7 collective-permute-done.1.right
  12.1 1.5 shard_map.114
  13.6 16.8 %all_to_all.45.parts = bf16[16,48,128]{2,1,0:T(8,128)(2,1)S(1)} all-to-all(bf16[16,48,128]{2,1,0:T(8,128)(2,1)S(1)} %get-tuple-element.25), channel_id=1, replica_groups=mesh['depth'=16,'tile'=32] {'depth'}, dimensions={0} | all-to-all | bytes 393216 | tf_op jit(solution)/shard_map/all_to_all | solution.py:267
  30.4 0.6 shard_map.115
  31.0 11.5 %all_to_all.46.ratio = bf16[16,48,128]{2,1,0:T(8,128)(2,1)S(1)} all-to-all(bf16[16,48,128]{2,1,0:T(8,128)(2,1)S(1)} %shard_map.115), channel_id=1, replica_groups=mesh['depth'=16,'tile'=32] {'depth'}, dimensions={0} | all-to-all | bytes 393216 | tf_op jit(solution)/shard_map/all_to_all | solution.py:267
  42.4 1.7 %shard_map.116 = (f32[16,24,128]{2,1,0:T(8,128)S(1)}, f32[32,1024]{1,0:T(8,128)S(1)}) custom-call(bf16[16,128]{1,0:T(8,128)(2,1)S(1)} %pad.4.psf, bf16[64,1040]{1,0:T(8,128)(2,1)S(1)} %get-tuple-element.22.band_b, bf16[48,832]{1,0:T(8,128)(2,1)S(1)} %get-tuple-element.23.band_f, f32[32,1024]{1,0:T(8,128)S(1)} %bitcast.25, ...), custom_call_target="tpu_custom_call" | custom-call | tf_op jit(solution)/shard_map/pallas_call | solution.py:318
  44.1 11.5 %all_to_all.47.parts = f32[16,24,128]{2,1,0:T(8,128)S(1)} all-to-all(f32[16,24,128]{2,1,0:T(8,128)S(1)} %get-tuple-element.28), channel_id=1, replica_groups=mesh['depth'=16,'tile'=32] {'depth'}, dimensions={0} | all-to-all | bytes 393216 | tf_op jit(solution)/shard_map/all_to_all | solution.py:267
  55.5 0.6 shard_map.117
  56.2 11.1 %all_to_all.48.ratio = bf16[16,32,128]{2,1,0:T(8,128)(2,1)S(1)} all-to-all(bf16[16,32,128]{2,1,0:T(8,128)(2,1)S(1)} %shard_map.117), channel_id=1, replica_groups=mesh['depth'=16,'tile'=32] {'depth'}, dimensions={0} | all-to-all | bytes 262144 | tf_op jit(solution)/shard_map/all_to_all | solution.py:267
  67.2 4.2 %shard_map.118 = (f32[32,1024]{1,0:T(8,128)}, f32[16,1,512]{2,1,0:T(1,128)S(1)}, f32[256,128]{1,0:T(8,128)S(1)}) custom-call(s32[4]{0:T(128)S(1)} %pad_add_fusion.where, bf16[16,128]{1,0:T(8,128)(2,1)S(1)} %pad.4.psf, bf16[32,624]{1,0:T(8,128)(2,1)S(1)} %get-tuple-element.21.band_b, f32[32,1024]{1,0:T(8,128)S(1)} %get-tuple-element.27.before, ...), custom_call_target="tpu_custom_call" | custom-call | tf_op jit(solution)/shard_map/pallas_call | solution.py:329
  71.4 10.4 %all_to_all.49 = f32[16,1,512]{2,1,0:T(1,128)S(1)} all-to-all(f32[16,1,512]{2,1,0:T(1,128)S(1)} %get-tuple-element.32), channel_id=1, replica_groups=mesh['depth'=16,'tile'=32] {'depth'}, dimensions={0} | all-to-all | bytes 65536 | tf_op jit(solution)/shard_map/all_to_all | solution.py:267
  81.9 29.2 %all_to_all.50 = f32[32,1,512]{2,1,0:T(1,128)S(1)} all-to-all(f32[32,1,512]{2,1,0:T(1,128)S(1)} %broadcast_in_dim.10), channel_id=1, replica_groups=mesh['depth'=16,'tile'=32] {'tile'}, dimensions={0} | all-to-all | bytes 131072 | tf_op jit(solution)/shard_map/all_to_all | solution.py:267
  111.1 0.1 reduce_sum.19
  111.2 0.6 broadcast_in_dim.11
  111.8 5.3 %all-to-all-start.6 = ((f32[16,1,512]{2,1,0:T(1,128)}), f32[16,1,512]{2,1,0:T(1,128)S(1)}, u32[]{:S(2)}, u32[]{:S(2)}) async-start(f32[16,1,512]{2,1,0:T(1,128)} %broadcast_in_dim.11), calls=%async_computation.6 | async-start | bytes 65536 | tf_op jit(solution)/shard_map/all_to_all | solution.py:267
  117.2 7.4 %all-to-all-done.6.initial = f32[16,1,512]{2,1,0:T(1,128)S(1)} async-done(((f32[16,1,512]{2,1,0:T(1,128)}), f32[16,1,512]{2,1,0:T(1,128)S(1)}, u32[]{:S(2)}, u32[]{:S(2)}) %all-to-all-start.6) | async-done | bytes 32800 | tf_op jit(solution)/shard_map/all_to_all | solution.py:267
  124.5 1.3 shard_map.119
  125.9 10.2 %all_to_all.51.parts = f32[16,8,128]{2,1,0:T(8,128)S(1)} all-to-all(f32[16,8,128]{2,1,0:T(8,128)S(1)} %get-tuple-element.38), channel_id=1, replica_groups=mesh['depth'=16,'tile'=32] {'depth'}, dimensions={0} | all-to-all | bytes 131072 | tf_op jit(solution)/shard_map/all_to_all | solution.py:267
  136.1 0.1 shard_map.120
  136.2 15.0 %all_to_all.52.parts = f32[32,1,128]{2,1,0:T(1,128)S(1)} all-to-all(f32[32,1,128]{2,1,0:T(1,128)S(1)} %shard_map.120), channel_id=1, replica_groups=mesh['depth'=16,'tile'=32] {'tile'}, dimensions={0} | all-to-all | bytes 32768 | tf_op jit(solution)/shard_map/all_to_all | solution.py:267
  151.2 0.1 shard_map.121
  151.3 0.5 slice_bitcast_fusion.2
  (23 shorter events, 0.2 us)
Async XLA Ops:
  1.6 6.8 %copy-start.7 = (bf16[1,256,4,128]{3,2,1,0:T(4,128)(2,1)S(1)}, bf16[1,256,4,128]{3,2,1,0:T(4,128)(2,1)}, u32[]{:S(2)}) copy-start(bf16[1,256,4,128]{3,2,1,0:T(4,128)(2,1)} %param.15) | copy-start | bytes 786436
  2.5 8.9 %collective-permute-start = (f32[24,1152]{1,0:T(8,128)S(1)}, f32[24,1152]{1,0:T(8,128)S(1)}, u32[]{:S(2)}, u32[]{:S(2)}) collective-permute-start(f32[24,1152]{1,0:T(8,128)S(1)} %pad_maximum_fusion), channel_id=1, source_target_pairs={{0,1},{1,2},{2,3},{3,4},{4,5},{5,6},{6,7},{7,8},{8,9},{9,10},{10,1... | collective-permute-start | bytes 331784 | tf_op jit(solution)/shard_map/ppermute | solution.py:289
  6.4 5.6 %collective-permute-start.1 = (f32[24,1152]{1,0:T(8,128)S(1)}, f32[24,1152]{1,0:T(8,128)S(1)}, u32[]{:S(2)}, u32[]{:S(2)}) collective-permute-start(f32[24,1152]{1,0:T(8,128)S(1)} %pad_maximum_fusion.1), channel_id=1, source_target_pairs={{1,0},{2,1},{3,2},{4,3},{5,4},{6,5},{7,6},{8,7},{9,8},{10,9},{11,1... | collective-permute-start | bytes 331784 | tf_op jit(solution)/shard_map/ppermute | solution.py:290
  8.5 0.8 copy-start.1
  8.5 0.7 copy-start.8
  8.5 0.7 copy-start.6
  9.2 0.7 copy-start.5
  9.9 2.2 %copy-start = (f32[1,32,1024]{2,1,0:T(8,128)S(1)}, f32[1,32,1024]{2,1,0:T(8,128)}, u32[]{:S(2)}) copy-start(f32[1,32,1024]{2,1,0:T(8,128)} %param.10) | copy-start | bytes 393220
  56.1 11.1 %copy-start.2 = (s32[8192]{0:T(1024)S(1)}, s32[8192]{0:T(1024)}, u32[]{:S(2)}) copy-start(s32[8192]{0:T(1024)} %param.16) | copy-start | bytes 98308
  56.1 11.1 %copy-start.3 = (s32[8192]{0:T(1024)S(1)}, s32[8192]{0:T(1024)}, u32[]{:S(2)}) copy-start(s32[8192]{0:T(1024)} %param.17) | copy-start | bytes 98308
  56.2 11.1 %copy-start.4 = (s32[8192]{0:T(1024)S(1)}, s32[8192]{0:T(1024)}, u32[]{:S(2)}) copy-start(s32[8192]{0:T(1024)} %param.18) | copy-start | bytes 98308
  111.8 12.7 %all-to-all-start.6 = ((f32[16,1,512]{2,1,0:T(1,128)}), f32[16,1,512]{2,1,0:T(1,128)S(1)}, u32[]{:S(2)}, u32[]{:S(2)}) async-start(f32[16,1,512]{2,1,0:T(1,128)} %broadcast_in_dim.11), calls=%async_computation.6 | async-start | bytes 65536 | tf_op jit(solution)/shard_map/all_to_all | solution.py:267

commit v2 on v1

v2 whole, which is shorter than its diff:
```python
import jax
import jax.numpy as jnp
from jax import lax
from jax.experimental import pallas as pl
from jax.experimental.pallas import tpu as pltpu
from jax.sharding import PartitionSpec as P

F32 = jnp.float32
BF16 = jnp.bfloat16
I32 = jnp.int32
KS = 13
RADIUS = 6
ROWS = 32
COLS = 1024
CB = 128
NCB = COLS // CB
DEPTHS = 16
TILES = 32
SLOTS = 256
NEURONS = 8192
HALO = 24
WIN = 64
LIVE = WIN + 2 * HALO
ROW = DEPTHS
BLOCK = 16
DEEP = 32 * ROW
VMEM = pl.BlockSpec(memory_space=pltpu.VMEM)
SMEM = pl.BlockSpec(memory_space=pltpu.SMEM)


def call(kernel, outs, n_in, scalars=(), scratch=(), mib=24):
    return pl.pallas_call(
        kernel,
        out_shape=[jax.ShapeDtypeStruct(s, t) for s, t in outs],
        in_specs=[SMEM if i in scalars else VMEM for i in range(n_in)],
        out_specs=[VMEM] * len(outs),
        scratch_shapes=list(scratch),
        compiler_params=pltpu.CompilerParams(vmem_limit_bytes=mib * 2**20),
    )


def iota(shape, dim):
    return lax.broadcasted_iota(I32, shape, dim)


def split2(x):
    high = x.astype(BF16)
    return high, (x - high.astype(F32)).astype(BF16)


def split3(x):
    high = x.astype(BF16)
    rest = x - high.astype(F32)
    mid = rest.astype(BF16)
    return high, mid, (rest - mid.astype(F32)).astype(BF16)


def column_of(row):
    n = row.shape[1]
    return jnp.transpose(jnp.broadcast_to(row, (CB, n)))


def prepare_kernel(block, neuron, weights, owner, gram, q_row, q_col, n_col, b_col):
    foot = weights[...]
    product = lax.dot_general(foot, foot, (((1,), (1,)), ((), ())), preferred_element_type=F32)
    blocks = column_of(block[...].astype(F32))
    neurons = column_of(neuron[...].astype(F32))
    same = jnp.concatenate([blocks, blocks], axis=1) == block[...].astype(F32)
    gram[...] = jnp.where(same, product, 0.0)
    n_int = neurons.astype(I32)
    n_col[...] = n_int
    b_col[...] = blocks.astype(I32)
    table = owner[...]
    tables = jnp.concatenate([(table >> 7).astype(F32), (table & 127).astype(F32)], axis=1).astype(BF16)
    hot = (iota((SLOTS, 64), 1) == (n_int[:, :64] >> 7)).astype(F32).astype(BF16)
    found = jnp.dot(hot, tables, preferred_element_type=F32)
    lane_hot = iota((SLOTS, CB), 1) == (n_int & 127)
    value = jnp.where(lane_hot, found[:, :CB] * 128.0 + found[:, CB:], 0.0)
    place = jnp.sum(value, axis=1, keepdims=True)
    place = jnp.broadcast_to(place, (SLOTS, CB))
    place = jnp.where(n_int >= 0, place, -1.0)
    q_col[...] = place.astype(I32)
    q_row[...] = jnp.transpose(place)[0:8, :].astype(I32)


def window_kernel(where, volume, spread, measured, windows, sensor, wide):
    lane = iota((ROWS, CB), 1)
    zeros = jnp.zeros((ROWS, CB), F32)
    padded = jnp.concatenate([zeros, volume[...], zeros], axis=1)
    for j in range(DEPTHS):
        start = CB - HALO + WIN * j
        low = start // CB * CB
        moved = pltpu.roll(padded[:, low : low + 2 * CB], 2 * CB - start % CB, 1)[:, :CB]
        windows[j] = jnp.where(lane < LIVE, moved, spread[...])
    wide[:, :CB] = zeros
    wide[:, CB : CB + COLS] = measured[...]
    wide[:, CB + COLS :] = zeros
    start = CB - HALO + WIN * where[0]
    low = pl.multiple_of((start >> 7) * CB, CB)
    moved = pltpu.roll(wide[:, pl.ds(low, 2 * CB)], 2 * CB - (start & (CB - 1)), 1)[:, :CB]
    sensor[...] = jnp.where(lane < LIVE, moved, 0.0)


def arrange_kernel(parts, sensor, own, down, up):
    lane = iota((ROW, CB), 1)
    for r in range(ROWS):
        line = jnp.where(lane < LIVE, parts[pl.ds(r, ROW, stride=ROWS), :], 0.0)
        own[r * ROW : (r + 1) * ROW, :] = line
        if r < HALO:
            up[r * ROW : (r + 1) * ROW, :] = line
        if r >= ROWS - HALO:
            at = (r - ROWS + HALO) * ROW
            down[at : at + ROW, :] = line
    up[HALO * ROW :, :] = sensor[:HALO]
    down[HALO * ROW :, :] = sensor[ROWS - HALO :]


def tables_kernel(parts, ahead, behind, scale):
    taps = jnp.concatenate([parts[pl.ds(a, ROW, stride=ROWS), :] for a in range(16)], axis=0)
    taps = jnp.where(iota((256, CB), 1) >= LIVE, taps, 0.0)
    first = jnp.transpose(taps)[LIVE:, :]
    first = jnp.concatenate([first, jnp.zeros((16, 256), F32)], axis=1)
    for i in range(BLOCK):
        moved = pltpu.roll(first, i * ROW, 1) if i else first
        ahead[i * 16 : (i + 1) * 16, :] = moved.astype(BF16)
    lane = iota((CB, DEEP), 1)
    hot = (iota((CB, DEEP), 0) == LIVE + KS - 1 - (lane >> 5)).astype(F32).astype(BF16)
    spread = jnp.dot(taps.astype(BF16), hot, preferred_element_type=F32)
    inside = iota((ROW, DEEP), 1)
    within = jnp.where(inside < KS * 32, inside & 31, 32)
    second = jnp.zeros((ROW, DEEP), F32)
    for a in range(KS):
        second = jnp.where(within == KS - 1 - a, spread[a * ROW : (a + 1) * ROW], second)
    for i in range(BLOCK):
        moved = pltpu.roll(second, i, 1) if i else second
        behind[i * ROW : (i + 1) * ROW, :] = moved.astype(BF16)
    total = taps[:ROW]
    for a in range(1, KS):
        total = total + taps[a * ROW : (a + 1) * ROW]
    norm = jnp.sum(total, axis=1, keepdims=True)
    scale[...] = jnp.broadcast_to(1.0 / norm, (ROW, CB))


def lane_shift(x, b):
    shift = (RADIUS - b) % CB
    return pltpu.roll(x, shift, 1) if shift else x


def iterate_kernel(
    where, own, left, right, sensor, ahead, behind, scale, s_plane, s_row, s_col,
    sent, exact, rounded, first, second, light, sums, ratio, stack, packed,
):
    rows = (HALO * ROW, (HALO + ROWS) * ROW, (2 * HALO + ROWS) * ROW)
    exact[: rows[0], :] = left[: rows[0]]
    exact[rows[0] : rows[1], :] = own[...]
    exact[rows[1] : rows[2], :] = right[: rows[0]]
    exact[rows[2] :, :] = jnp.zeros((16 * ROW, CB), F32)
    rounded[...] = exact[...].astype(BF16)
    light[:HALO, :] = left[rows[0] :]
    light[HALO : HALO + ROWS, :] = sensor[...]
    light[HALO + ROWS : 2 * HALO + ROWS, :] = right[rows[0] :]
    light[2 * HALO + ROWS :, :] = jnp.zeros((16, CB), F32)
    for m in range(4):
        stack[m * DEEP + KS * 32 : (m + 1) * DEEP, :] = jnp.zeros((DEEP - KS * 32, CB), BF16)
    tall = jnp.concatenate([scale[...]] * BLOCK, axis=0)

    def divide(source, blocks, offset, valid):
        for m in range(blocks):
            sums[...] = jnp.dot(
                ahead[...], source[m * 256 : m * 256 + DEEP, :], preferred_element_type=F32
            )
            total = lane_shift(sums[pl.ds(0, BLOCK, stride=16), :], 0)
            for b in range(1, KS):
                total = total + lane_shift(sums[pl.ds(b, BLOCK, stride=16), :], b)
            seen = light[m * BLOCK + offset : (m + 1) * BLOCK + offset, :]
            inside = (iota((BLOCK, CB), 0) < valid - m * BLOCK) & (seen != 0.0) & (total != 0.0)
            value = jnp.where(inside, seen / jnp.where(inside, total, 1.0), 0.0)
            ratio[m * BLOCK : (m + 1) * BLOCK, :] = value

    def spread_back(blocks):
        height = 16 * blocks + 16
        for b in range(KS):
            moved = lane_shift(ratio[:height, :], b).astype(BF16)
            for m in range(blocks):
                stack[m * DEEP + b * 32 : m * DEEP + (b + 1) * 32, :] = moved[m * 16 : m * 16 + 32]

    def back(m):
        value = jnp.dot(behind[...], stack[m * DEEP : (m + 1) * DEEP, :], preferred_element_type=F32)
        return value * tall

    divide(rounded, 5, 6, 68)
    spread_back(4)
    for m in range(4):
        value = exact[(m * 16 + 12) * ROW : (m * 16 + 28) * ROW, :] * back(m)
        first[m * 256 : (m + 1) * 256, :] = value
        second[m * 256 : (m + 1) * 256, :] = value.astype(BF16)
    divide(second, 3, 18, 44)
    spread_back(2)
    done = [first[(m * 16 + 12) * ROW : (m * 16 + 28) * ROW, :] * back(m) for m in range(2)]
    lane = iota((256, CB), 1)
    flat = jnp.where(lane < WIN, pltpu.roll(done[0], CB - HALO, 1), pltpu.roll(done[1], WIN - HALO, 1))
    packed[...] = flat
    for p in range(DEPTHS):
        sent[p, 0:16, :] = packed[pl.ds(p, 16, stride=ROW), :]
        sent[p, 20:24, :] = jnp.zeros((4, CB), F32)
    left_side = jnp.concatenate(split2(jnp.transpose(flat)), axis=0)
    chunk = NEURONS // DEPTHS
    for j in range(DEPTHS):
        plane, row, col = s_plane[j], s_row[j], s_col[j]
        local = ((row >> 5) == where[1]) & ((col >> 6) == where[0])
        key = jnp.where(local, (row & 15) * ROW + plane, -1)
        hot = (iota((256, chunk), 0) == key).astype(F32).astype(BF16)
        found = jnp.dot(left_side, hot, preferred_element_type=F32)
        found = found[:CB] + found[CB:]
        spot = ((row >> 4) & 1) * WIN + (col & (WIN - 1))
        picked = jnp.sum(jnp.where(iota((CB, chunk), 0) == spot, found, 0.0), axis=0, keepdims=True)
        for i in range(4):
            sent[j, 16 + i : 17 + i, :] = picked[:, i * CB : (i + 1) * CB]


def sum_kernel(count, at, copies):
    def kernel(parts, out):
        total = parts[0, at : at + 4, :]
        for j in range(1, count):
            total = total + parts[j, at : at + 4, :]
        for j in range(copies):
            out[j] = total

    return kernel


def home_kernel(parts, weights, b_col, estimate, proj, lines):
    lane = iota((16, CB), 1)
    for c in range(NCB):
        a, b = parts[2 * c, :16, :], parts[2 * c + 1, :16, :]
        top = jnp.where(lane < WIN, a, pltpu.roll(b, WIN, 1))
        bottom = jnp.where(lane < WIN, pltpu.roll(a, WIN, 1), b)
        estimate[:16, c * CB : (c + 1) * CB] = top
        estimate[16:, c * CB : (c + 1) * CB] = bottom
        lines[c * ROWS : c * ROWS + 16, :] = top
        lines[c * ROWS + 16 : (c + 1) * ROWS, :] = bottom
    blocks = [lines[pl.ds(br, 64, stride=4), :] for br in range(4)]
    blocked = jnp.concatenate(blocks, axis=1)
    number = b_col[:, :64]
    number = (number & 7) * 8 + (number >> 3)
    hot = (iota((SLOTS, 64), 1) == number).astype(F32).astype(BF16)
    high, low = split2(blocked)
    picked = jnp.dot(hot, high, preferred_element_type=F32) + jnp.dot(hot, low, preferred_element_type=F32)
    product = weights[...].astype(F32) * picked
    total = product[:, :CB]
    for br in range(1, 4):
        total = total + product[:, br * CB : (br + 1) * CB]
    proj[...] = jnp.broadcast_to(jnp.sum(total, axis=1, keepdims=True), (SLOTS, CB))


def slots_kernel(where, initial, owner, gram, q_row, q_col, n_col, proj, out, own):
    table = jnp.concatenate([initial[j] for j in range(DEPTHS)], axis=0)
    number = n_col[...]
    hot = (iota((SLOTS, 64), 1) == (number[:, :64] >> 7)).astype(F32).astype(BF16)
    parts = split3(table)
    found = jnp.dot(hot, parts[0], preferred_element_type=F32)
    found = found + jnp.dot(hot, parts[1], preferred_element_type=F32)
    found = found + jnp.dot(hot, parts[2], preferred_element_type=F32)
    value = jnp.where(iota((SLOTS, CB), 1) == (number & (CB - 1)), found, 0.0)
    start = jnp.broadcast_to(jnp.sum(value, axis=1, keepdims=True), (SLOTS, CB))
    start_row = jnp.transpose(start)[0:1, :]
    terms = gram[...] * start_row
    over = jnp.sum(terms[:, :CB] + terms[:, CB:], axis=1, keepdims=True)
    place = q_col[...]
    lane = iota((SLOTS, CB), 1)
    target = ((place >> 4) & 3) * 32 + (place & 15)
    sent = jnp.where(lane == target, proj[...], 0.0) + jnp.where(lane == target + 16, over, 0.0)
    row_hot = (iota((CB, SLOTS), 0) == (q_row[0:1, :] >> 6)).astype(F32).astype(BF16)
    parts = split3(sent)
    dense = jnp.dot(row_hot, parts[0], preferred_element_type=F32)
    dense = dense + jnp.dot(row_hot, parts[1], preferred_element_type=F32)
    dense = dense + jnp.dot(row_hot, parts[2], preferred_element_type=F32)
    for j in range(DEPTHS):
        out[j] = dense[j * 8 : (j + 1) * 8]
    base = where[2]
    holder = owner[...]
    lanes = iota((1, CB), 1)
    result = jnp.zeros((1, CB), F32)
    for i in range(16):
        mine = jnp.sum(jnp.where(holder == base + i, table, 0.0), axis=0, keepdims=True)
        result = jnp.where(lanes == i, jnp.sum(mine, axis=1, keepdims=True), result)
    own[...] = result


def fold_kernel(parts, out):
    total = parts[0]
    for j in range(1, DEPTHS):
        total = total + parts[j]
    for m in range(4):
        moved = pltpu.roll(total, (CB - 32 * m) % CB, 1) if m else total
        for r in range(8):
            out[4 * r + m] = moved[r : r + 1]


def final_kernel(parts, own, out):
    total = parts[0]
    for j in range(1, TILES):
        total = total + parts[j]
    over = pltpu.roll(total, CB - 16, 1)
    initial = own[...]
    real = iota((1, CB), 1) < 16
    bottom = jnp.where(real, over + 100.0 * initial, 1.0)
    out[...] = jnp.where(real, initial * total, 0.0) / bottom


def swap(pieces, axis):
    return lax.all_to_all(pieces, axis, 0, 0)


def body(
    volume,
    measured,
    point_spread,
    entry_block,
    entry_neuron,
    footprints,
    seed_plane,
    seed_row,
    seed_col,
    owner_slot,
):
    d = lax.axis_index("depth")
    t = lax.axis_index("tile")
    where = jnp.stack([d, t, (d * TILES + t) * 16]).astype(I32)
    table = owner_slot.reshape(64, CB)
    spread = jnp.pad(point_spread[0].astype(F32), ((0, ROWS - KS), (LIVE, CB - LIVE - KS)))
    windows, sensor = call(
        window_kernel,
        [((DEPTHS, ROWS, CB), F32), ((ROWS, CB), F32)],
        4,
        scalars=(0,),
        scratch=[pltpu.VMEM((ROWS, COLS + 2 * CB), F32)],
    )(where, volume[0], spread, measured)
    parts = swap(windows, "depth").reshape(DEPTHS * ROWS, CB)
    message = ((HALO * ROW + HALO, CB), F32)
    own, down, up = call(arrange_kernel, [((ROWS * ROW, CB), F32), message, message], 2)(parts, sensor)
    left = lax.ppermute(down, "tile", [(i, i + 1) for i in range(TILES - 1)])
    right = lax.ppermute(up, "tile", [(i + 1, i) for i in range(TILES - 1)])
    ahead, behind, scale = call(
        tables_kernel, [((256, DEEP), BF16), ((256, DEEP), BF16), ((ROW, CB), F32)], 1
    )(parts)
    weights = footprints[0].reshape(SLOTS, 512)
    gram, q_row, q_col, n_col, b_col = call(
        prepare_kernel,
        [
            ((SLOTS, SLOTS), F32),
            ((8, SLOTS), I32),
            ((SLOTS, CB), I32),
            ((SLOTS, CB), I32),
            ((SLOTS, CB), I32),
        ],
        4,
    )(entry_block, entry_neuron, weights, table)
    chunk = NEURONS // DEPTHS
    shape = (DEPTHS, 1, chunk)
    [sent] = call(
        iterate_kernel,
        [((DEPTHS, 24, CB), F32)],
        11,
        scalars=(0,),
        scratch=[
            pltpu.VMEM((96 * ROW, CB), F32),
            pltpu.VMEM((96 * ROW, CB), BF16),
            pltpu.VMEM((64 * ROW, CB), F32),
            pltpu.VMEM((64 * ROW, CB), BF16),
            pltpu.VMEM((96, CB), F32),
            pltpu.VMEM((256, CB), F32),
            pltpu.VMEM((80, CB), F32),
            pltpu.VMEM((4 * DEEP, CB), BF16),
            pltpu.VMEM((256, CB), F32),
        ],
    )(
        where,
        own,
        left,
        right,
        sensor,
        ahead,
        behind,
        scale,
        seed_plane.reshape(shape),
        seed_row.reshape(shape),
        seed_col.reshape(shape),
    )
    parts = swap(sent, "depth")
    [mine] = call(sum_kernel(DEPTHS, 16, TILES), [((TILES, 4, CB), F32)], 1)(parts)
    [mine] = call(sum_kernel(TILES, 0, DEPTHS), [((DEPTHS, 4, CB), F32)], 1)(swap(mine, "tile"))
    initial = swap(mine, "depth")
    estimate, proj = call(
        home_kernel,
        [((ROWS, COLS), F32), ((SLOTS, CB), F32)],
        3,
        scratch=[pltpu.VMEM((NCB * ROWS, CB), F32)],
    )(parts, weights, b_col)
    sent, own = call(slots_kernel, [((DEPTHS, 8, CB), F32), ((1, CB), F32)], 8, scalars=(0,))(
        where, initial, table, gram, q_row, q_col, n_col, proj
    )
    [sent] = call(fold_kernel, [((TILES, 1, CB), F32)], 1)(swap(sent, "depth"))
    [demixed] = call(final_kernel, [((1, CB), F32)], 2)(swap(sent, "tile"), own)
    return estimate[None], demixed[0, :16]


def solution(mesh):
    in_specs = (
        P("depth", "tile", None),
        P("tile", None),
        P("depth", None, None),
        P("tile", "depth"),
        P("tile", "depth"),
        P("tile", "depth", None, None),
        P(),
        P(),
        P(),
        P(),
    )
    out_specs = (P("depth", "tile", None), P(("depth", "tile")))
    return jax.shard_map(body, mesh=mesh, in_specs=in_specs, out_specs=out_specs, check_vma=False)
```

time: 153 us -> 122 us (0.80)
  blocking collectives: 116 us -> 87.3 us
  waiting for transfers between devices: 8.09 us -> 11.8 us
  starting transfers between devices: 10.6 us -> 8.11 us
  Pallas kernels: 11.4 us -> 9.65 us
    all_to_all x8 -> x5, blocking collectives: 116 us -> 87.3 us  [swap(): return lax.all_to_all(pieces, axis, 0, 0)]
    ppermute x1, waiting for transfers between devices: 0.72 us -> 4.75 us  [body(): right = lax.ppermute(up, 'tile', [(i + 1, i) for i in range(TILES - 1)])]
    ppermute x1, starting transfers between devices: 3.95 us -> 1.3 us  [body(): left = lax.ppermute(down, 'tile', [(i, i + 1) for i in range(TILES - 1)])]
    all_to_all x1, waiting for transfers between devices: 7.37 us -> 5.14 us  [swap(): return lax.all_to_all(pieces, axis, 0, 0)]
    ppermute x1, waiting for transfers between devices: 0.01 us -> 1.95 us  [body(): left = lax.ppermute(down, 'tile', [(i, i + 1) for i in range(TILES - 1)])]
    unnamed x19 -> x21, local copies, waits for them, and re-layouts: 1.41 us -> 3.25 us
    slice x2 -> x0, local copies, waits for them, and re-layouts: 1.78 us -> none  [body(): up = jnp.concatenate([vol[:HALO], sensor[:HALO]], axis=1)]
    pallas_call x6 -> x8, Pallas kernels: 9.88 us -> 8.21 us  [the longest x1 4.84 us: body(): call(iterate_kernel, [((DEPTHS, 24, CB), F32)], 11, scalars=(0,), scratch...]
  transfers between devices with their start and end apart: 3 -> 3, of which waited for: 2 -> 3; matrix products, arithmetic and copies ran while one was open for 1% -> 0% of each run, Pallas kernels for 1% -> 2%
where the time goes in v2:
time: 122 us
  blocking collectives  87.3 us (72%)
  waiting for transfers between devices  11.8 us (10%)
  Pallas kernels  9.65 us (8%)
  starting transfers between devices  8.11 us (7%)
  local copies, waits for them, and re-layouts  3.76 us (3%)
    all_to_all x5, blocking collectives, swap(): return lax.all_to_all(pieces, axis, 0, 0)  87.3 us
    all_to_all x1, starting transfers between devices, swap(): return lax.all_to_all(pieces, axis, 0, 0)  5.52 us
    all_to_all x1, waiting for transfers between devices, swap(): return lax.all_to_all(pieces, axis, 0, 0)  5.14 us
    pallas_call x1, Pallas kernels, body(): call(iterate_kernel, [((DEPTHS, 24, CB), F32)], 11, scalars=(0,), scratch...  4.84 us
    ppermute x1, waiting for transfers between devices, body(): right = lax.ppermute(up, 'tile', [(i + 1, i) for i in range(TILES - 1)])  4.75 us
    unnamed x21, local copies, waits for them, and re-layouts  3.25 us
  transfers between devices with their start and end apart: 3, of which 3 were waited for; matrix products, arithmetic and copies ran while one was open for 0% of the time, Pallas kernels for 2%

profile of v2, /device:TPU:1, one launch (start us, length us, event | category | flops | bytes accessed | tf_op | source)
XLA Modules:
  0.0 121.6 jit_solution(9993963149517220323)
XLA Ops:
  0.6 0.7 copy-done.9
  1.3 0.1 pad_convert_fusion.spread
  1.4 0.1 pad_add_fusion.where
  1.5 0.9 copy-done.1
  2.4 0.9 copy-done.2
  3.3 0.7 shard_map.113
  4.0 18.0 %all_to_all.30 = f32[16,32,128]{2,1,0:T(8,128)S(1)} all-to-all(f32[16,32,128]{2,1,0:T(8,128)S(1)} %get-tuple-element.19), channel_id=1, replica_groups=mesh['depth'=16,'tile'=32] {'depth'}, dimensions={0} | all-to-all | bytes 524288 | tf_op jit(solution)/shard_map/all_to_all | solution.py:312
  22.0 0.2 shard_map.114
  22.2 1.3 %collective-permute-start = (f32[408,128]{1,0:T(8,128)S(1)}, f32[408,128]{1,0:T(8,128)S(1)}, u32[]{:S(2)}, u32[]{:S(2)}) collective-permute-start(f32[408,128]{1,0:T(8,128)S(1)} %get-tuple-element.22), channel_id=1, source_target_pairs={{0,1},{1,2},{2,3},{3,4},{4,5},{5,6},{6,7},{7,8},{8,9},{9,10},{10,1... | collective-permute-start | bytes 626696 | tf_op jit(solution)/shard_map/ppermute | solution.py:342
  23.5 1.3 %collective-permute-start.1 = (f32[408,128]{1,0:T(8,128)S(1)}, f32[408,128]{1,0:T(8,128)S(1)}, u32[]{:S(2)}, u32[]{:S(2)}) collective-permute-start(f32[408,128]{1,0:T(8,128)S(1)} %get-tuple-element.23), channel_id=1, source_target_pairs={{1,0},{2,1},{3,2},{4,3},{5,4},{6,5},{7,6},{8,7},{9,8},{10,9},{11,1... | collective-permute-start | bytes 626696 | tf_op jit(solution)/shard_map/ppermute | solution.py:343
  24.8 0.0 copy-start.3
  24.8 0.0 copy-start.4
  24.8 0.0 copy-start.5
  24.8 0.4 shard_map.115
  25.2 2.0 %collective-permute-done.left = f32[408,128]{1,0:T(8,128)S(1)} collective-permute-done((f32[408,128]{1,0:T(8,128)S(1)}, f32[408,128]{1,0:T(8,128)S(1)}, u32[]{:S(2)}, u32[]{:S(2)}) %collective-permute-start) | collective-permute-done | bytes 208928 | tf_op jit(solution)/shard_map/ppermute | solution.py:342
  27.2 4.7 %collective-permute-done.1.right = f32[408,128]{1,0:T(8,128)S(1)} collective-permute-done((f32[408,128]{1,0:T(8,128)S(1)}, f32[408,128]{1,0:T(8,128)S(1)}, u32[]{:S(2)}, u32[]{:S(2)}) %collective-permute-start.1) | collective-permute-done | bytes 208928 | tf_op jit(solution)/shard_map/ppermute | solution.py:343
  31.9 4.8 %shard_map.116 = f32[16,24,128]{2,1,0:T(8,128)S(1)} custom-call(s32[3]{0:T(128)S(1)} %pad_add_fusion.where, f32[512,128]{1,0:T(8,128)S(1)} %get-tuple-element.21.own, f32[408,128]{1,0:T(8,128)S(1)} %collective-permute-done.left, f32[408,128]{1,0:T(8,128)S(1)} %collective-permute-done.1.right, f32[32,128]{1,0:T(8,128)S(1)} %get-tuple-element.20.sensor, ...), custom_call_target="tpu_custom_call" | custom-call | tf_op jit(solution)/shard_map/pallas_call | solution.py:361
  36.8 13.0 %all_to_all.31.parts = f32[16,24,128]{2,1,0:T(8,128)S(1)} all-to-all(f32[16,24,128]{2,1,0:T(8,128)S(1)} %shard_map.116), channel_id=1, replica_groups=mesh['depth'=16,'tile'=32] {'depth'}, dimensions={0} | all-to-all | bytes 393216 | tf_op jit(solution)/shard_map/all_to_all | solution.py:312
  49.8 31.0 %all_to_all.32.parts = f32[32,4,128]{2,1,0:T(4,128)S(1)} all-to-all(f32[32,4,128]{2,1,0:T(4,128)S(1)} %shard_map.119), channel_id=1, replica_groups=mesh['depth'=16,'tile'=32] {'tile'}, dimensions={0} | all-to-all | bytes 131072 | tf_op jit(solution)/shard_map/all_to_all | solution.py:312
  80.8 0.6 shard_map.120
  81.5 5.5 %all-to-all-start.3 = ((f32[16,4,128]{2,1,0:T(4,128)}), f32[16,4,128]{2,1,0:T(4,128)S(1)}, u32[]{:S(2)}, u32[]{:S(2)}) async-start(f32[16,4,128]{2,1,0:T(4,128)} %shard_map.120), calls=%async_computation.3 | async-start | bytes 65536 | tf_op jit(solution)/shard_map/all_to_all | solution.py:312
  87.0 0.0 copy-start
  87.1 0.7 copy-done
  87.8 0.4 shard_map.117
  88.2 1.0 shard_map.118
  89.2 5.1 %all-to-all-done.3.initial = f32[16,4,128]{2,1,0:T(4,128)S(1)} async-done(((f32[16,4,128]{2,1,0:T(4,128)}), f32[16,4,128]{2,1,0:T(4,128)S(1)}, u32[]{:S(2)}, u32[]{:S(2)}) %all-to-all-start.3) | async-done | bytes 32800 | tf_op jit(solution)/shard_map/all_to_all | solution.py:312
  94.4 1.2 %shard_map.121 = (f32[16,8,128]{2,1,0:T(8,128)S(1)}, f32[1,128]{1,0:T(1,128)S(1)}) custom-call(s32[3]{0:T(128)S(1)} %pad_add_fusion.where, f32[16,4,128]{2,1,0:T(4,128)S(1)} %all-to-all-done.3.initial, s32[64,128]{1,0:T(8,128)S(1)} %bitcast.23, f32[256,256]{1,0:T(8,128)S(1)} %get-tuple-element.29.gram, s32[8,256]{1,0:T(8,128)S(1)} %get-tuple-element.30.q_row, ...), custom_call_target="tpu_custom_call" | custom-call | tf_op jit(solution)/shard_map/pallas_call | solution.py:400
  95.6 10.2 %all_to_all.33.parts = f32[16,8,128]{2,1,0:T(8,128)S(1)} all-to-all(f32[16,8,128]{2,1,0:T(8,128)S(1)} %get-tuple-element.34), channel_id=1, replica_groups=mesh['depth'=16,'tile'=32] {'depth'}, dimensions={0} | all-to-all | bytes 131072 | tf_op jit(solution)/shard_map/all_to_all | solution.py:312
  105.8 0.1 shard_map.122
  105.9 15.0 %all_to_all.34.parts = f32[32,1,128]{2,1,0:T(1,128)S(1)} all-to-all(f32[32,1,128]{2,1,0:T(1,128)S(1)} %shard_map.122), channel_id=1, replica_groups=mesh['depth'=16,'tile'=32] {'tile'}, dimensions={0} | all-to-all | bytes 32768 | tf_op jit(solution)/shard_map/all_to_all | solution.py:312
  121.0 0.1 shard_map.123
  121.1 0.5 slice_bitcast_fusion
  (14 shorter events, 0.1 us)
Async XLA Ops:
  0.6 0.7 copy-start.9
  1.5 0.9 copy-start.1
  2.4 0.9 copy-start.2
  22.2 5.0 %collective-permute-start = (f32[408,128]{1,0:T(8,128)S(1)}, f32[408,128]{1,0:T(8,128)S(1)}, u32[]{:S(2)}, u32[]{:S(2)}) collective-permute-start(f32[408,128]{1,0:T(8,128)S(1)} %get-tuple-element.22), channel_id=1, source_target_pairs={{0,1},{1,2},{2,3},{3,4},{4,5},{5,6},{6,7},{7,8},{8,9},{9,10},{10,1... | collective-permute-start | bytes 626696 | tf_op jit(solution)/shard_map/ppermute | solution.py:342
  23.5 8.4 %collective-permute-start.1 = (f32[408,128]{1,0:T(8,128)S(1)}, f32[408,128]{1,0:T(8,128)S(1)}, u32[]{:S(2)}, u32[]{:S(2)}) collective-permute-start(f32[408,128]{1,0:T(8,128)S(1)} %get-tuple-element.23), channel_id=1, source_target_pairs={{1,0},{2,1},{3,2},{4,3},{5,4},{6,5},{7,6},{8,7},{9,8},{10,9},{11,1... | collective-permute-start | bytes 626696 | tf_op jit(solution)/shard_map/ppermute | solution.py:343
  24.8 7.1 %copy-start.3 = (s32[8192]{0:T(1024)S(1)}, s32[8192]{0:T(1024)}, u32[]{:S(2)}) copy-start(s32[8192]{0:T(1024)} %param.16) | copy-start | bytes 98308
  24.8 7.1 %copy-start.4 = (s32[8192]{0:T(1024)S(1)}, s32[8192]{0:T(1024)}, u32[]{:S(2)}) copy-start(s32[8192]{0:T(1024)} %param.17) | copy-start | bytes 98308
  24.8 7.1 %copy-start.5 = (s32[8192]{0:T(1024)S(1)}, s32[8192]{0:T(1024)}, u32[]{:S(2)}) copy-start(s32[8192]{0:T(1024)} %param.18) | copy-start | bytes 98308
  49.8 37.2 %copy-start.8 = (bf16[1,256,4,128]{3,2,1,0:T(4,128)(2,1)S(1)}, bf16[1,256,4,128]{3,2,1,0:T(4,128)(2,1)}, u32[]{:S(2)}) copy-start(bf16[1,256,4,128]{3,2,1,0:T(4,128)(2,1)} %param.15) | copy-start | bytes 786436
  81.5 12.9 %all-to-all-start.3 = ((f32[16,4,128]{2,1,0:T(4,128)}), f32[16,4,128]{2,1,0:T(4,128)S(1)}, u32[]{:S(2)}, u32[]{:S(2)}) async-start(f32[16,4,128]{2,1,0:T(4,128)} %shard_map.120), calls=%async_computation.3 | async-start | bytes 65536 | tf_op jit(solution)/shard_map/all_to_all | solution.py:312
  87.0 0.8 copy-start
  87.0 0.8 copy-start.7
  87.1 0.7 copy-start.6

commit v3 on v2

--- a/solution.py
+++ b/solution.py
@@ -83,36 +83,44 @@
     q_row[...] = jnp.transpose(place)[0:8, :].astype(I32)
 
 
-def window_kernel(where, volume, spread, measured, windows, sensor, wide):
+def window_kernel(volume, spread, windows, local, arrived):
+    copy = pltpu.make_async_copy(volume.at[0], local, arrived)
+    copy.start()
     lane = iota((ROWS, CB), 1)
+    taps = jnp.concatenate([spread[0].astype(F32), jnp.zeros((KS, CB - KS), F32)], axis=1)
+    taps = jnp.concatenate([pltpu.roll(taps, LIVE, 1), jnp.zeros((ROWS - KS, CB), F32)], axis=0)
     zeros = jnp.zeros((ROWS, CB), F32)
-    padded = jnp.concatenate([zeros, volume[...], zeros], axis=1)
+    copy.wait()
+    padded = jnp.concatenate([zeros, local[...], zeros], axis=1)
     for j in range(DEPTHS):
         start = CB - HALO + WIN * j
         low = start // CB * CB
         moved = pltpu.roll(padded[:, low : low + 2 * CB], 2 * CB - start % CB, 1)[:, :CB]
-        windows[j] = jnp.where(lane < LIVE, moved, spread[...])
+        windows[j] = jnp.where(lane < LIVE, moved, taps)
+
+
+def arrange_kernel(where, parts, measured, own, sensor, down, up, wide):
+    lane = iota((ROW, CB), 1)
+    for r in range(ROWS):
+        line = jnp.where(lane < LIVE, parts[pl.ds(r, ROW, stride=ROWS), :], 0.0)
+        own[r * ROW : (r + 1) * ROW, :] = line
+        if r < HALO:
+            up[r * ROW : (r + 1) * ROW, :] = line.astype(BF16)
+        if r >= ROWS - HALO:
+            at = (r - ROWS + HALO) * ROW
+            down[at : at + ROW, :] = line.astype(BF16)
+    zeros = jnp.zeros((ROWS, CB), F32)
     wide[:, :CB] = zeros
     wide[:, CB : CB + COLS] = measured[...]
     wide[:, CB + COLS :] = zeros
     start = CB - HALO + WIN * where[0]
     low = pl.multiple_of((start >> 7) * CB, CB)
     moved = pltpu.roll(wide[:, pl.ds(low, 2 * CB)], 2 * CB - (start & (CB - 1)), 1)[:, :CB]
-    sensor[...] = jnp.where(lane < LIVE, moved, 0.0)
-
-
-def arrange_kernel(parts, sensor, own, down, up):
-    lane = iota((ROW, CB), 1)
-    for r in range(ROWS):
-        line = jnp.where(lane < LIVE, parts[pl.ds(r, ROW, stride=ROWS), :], 0.0)
-        own[r * ROW : (r + 1) * ROW, :] = line
-        if r < HALO:
-            up[r * ROW : (r + 1) * ROW, :] = line
-        if r >= ROWS - HALO:
-            at = (r - ROWS + HALO) * ROW
-            down[at : at + ROW, :] = line
-    up[HALO * ROW :, :] = sensor[:HALO]
-    down[HALO * ROW :, :] = sensor[ROWS - HALO :]
+    view = jnp.where(iota((ROWS, CB), 1) < LIVE, moved, 0.0)
+    sensor[...] = view
+    for out, part in ((up, view[:HALO]), (down, view[ROWS - HALO :])):
+        high = part.astype(BF16).astype(F32)
+        out[HALO * ROW :, :] = jnp.concatenate([high, part - high], axis=0).astype(BF16)
 
 
 def tables_kernel(parts, ahead, behind, scale):
@@ -151,14 +159,15 @@
     sent, exact, rounded, first, second, light, sums, ratio, stack, packed,
 ):
     rows = (HALO * ROW, (HALO + ROWS) * ROW, (2 * HALO + ROWS) * ROW)
-    exact[: rows[0], :] = left[: rows[0]]
+    exact[: rows[0], :] = left[: rows[0]].astype(F32)
     exact[rows[0] : rows[1], :] = own[...]
-    exact[rows[1] : rows[2], :] = right[: rows[0]]
+    exact[rows[1] : rows[2], :] = right[: rows[0]].astype(F32)
     exact[rows[2] :, :] = jnp.zeros((16 * ROW, CB), F32)
     rounded[...] = exact[...].astype(BF16)
-    light[:HALO, :] = left[rows[0] :]
+    before, after = left[rows[0] :].astype(F32), right[rows[0] :].astype(F32)
+    light[:HALO, :] = before[:HALO] + before[HALO:]
     light[HALO : HALO + ROWS, :] = sensor[...]
-    light[HALO + ROWS : 2 * HALO + ROWS, :] = right[rows[0] :]
+    light[HALO + ROWS : 2 * HALO + ROWS, :] = after[:HALO] + after[HALO:]
     light[2 * HALO + ROWS :, :] = jnp.zeros((16, CB), F32)
     for m in range(4):
         stack[m * DEEP + KS * 32 : (m + 1) * DEEP, :] = jnp.zeros((DEEP - KS * 32, CB), BF16)
@@ -328,17 +337,23 @@
     t = lax.axis_index("tile")
     where = jnp.stack([d, t, (d * TILES + t) * 16]).astype(I32)
     table = owner_slot.reshape(64, CB)
-    spread = jnp.pad(point_spread[0].astype(F32), ((0, ROWS - KS), (LIVE, CB - LIVE - KS)))
-    windows, sensor = call(
+    [windows] = pl.pallas_call(
         window_kernel,
-        [((DEPTHS, ROWS, CB), F32), ((ROWS, CB), F32)],
-        4,
+        out_shape=[jax.ShapeDtypeStruct((DEPTHS, ROWS, CB), F32)],
+        in_specs=[pl.BlockSpec(memory_space=pl.ANY), VMEM],
+        out_specs=[VMEM],
+        scratch_shapes=[pltpu.VMEM((ROWS, COLS), F32), pltpu.SemaphoreType.DMA],
+        compiler_params=pltpu.CompilerParams(vmem_limit_bytes=24 * 2**20),
+    )(volume, point_spread)
+    parts = swap(windows, "depth").reshape(DEPTHS * ROWS, CB)
+    message = ((HALO * ROW + 2 * HALO, CB), BF16)
+    own, sensor, down, up = call(
+        arrange_kernel,
+        [((ROWS * ROW, CB), F32), ((ROWS, CB), F32), message, message],
+        3,
         scalars=(0,),
         scratch=[pltpu.VMEM((ROWS, COLS + 2 * CB), F32)],
-    )(where, volume[0], spread, measured)
-    parts = swap(windows, "depth").reshape(DEPTHS * ROWS, CB)
-    message = ((HALO * ROW + HALO, CB), F32)
-    own, down, up = call(arrange_kernel, [((ROWS * ROW, CB), F32), message, message], 2)(parts, sensor)
+    )(where, parts, measured)
     left = lax.ppermute(down, "tile", [(i, i + 1) for i in range(TILES - 1)])
     right = lax.ppermute(up, "tile", [(i + 1, i) for i in range(TILES - 1)])
     ahead, behind, scale = call(

time: 122 us -> 119 us (0.975)
  blocking collectives: 87.3 us -> 67.9 us
  starting transfers between devices: 8.11 us -> 18.5 us
  waiting for transfers between devices: 11.8 us -> 17.7 us
    all_to_all x5 -> x4, blocking collectives: 87.3 us -> 67.9 us  [swap(): return lax.all_to_all(pieces, axis, 0, 0)]
    all_to_all x1 -> x2, starting transfers between devices: 5.52 us -> 15.9 us  [swap(): return lax.all_to_all(pieces, axis, 0, 0)]
    all_to_all x1 -> x2, waiting for transfers between devices: 5.14 us -> 13.8 us  [swap(): return lax.all_to_all(pieces, axis, 0, 0)]
    ppermute x1, waiting for transfers between devices: 1.95 us -> 0.01 us  [body(): left = lax.ppermute(down, 'tile', [(i, i + 1) for i in range(TILES - 1)])]
  transfers between devices with their start and end apart: 3 -> 4, of which waited for: 3 -> 3; matrix products, arithmetic and copies ran while one was open for 0% -> 0% of each run, Pallas kernels for 2% -> 2%
where the time goes in v3:
time: 119 us; the launch traced here: 118 us
  blocking collectives  67.9 us (57%)
  starting transfers between devices  18.5 us (16%)
  waiting for transfers between devices  17.7 us (15%)
  Pallas kernels  10.5 us (9%)
  local copies, waits for them, and re-layouts  2.87 us (2%)
    all_to_all x4, blocking collectives, swap(): return lax.all_to_all(pieces, axis, 0, 0)  67.9 us
    all_to_all x2, starting transfers between devices, swap(): return lax.all_to_all(pieces, axis, 0, 0)  15.9 us
    all_to_all x2, waiting for transfers between devices, swap(): return lax.all_to_all(pieces, axis, 0, 0)  13.8 us
    pallas_call x1, Pallas kernels, body(): call(iterate_kernel, [((DEPTHS, 24, CB), F32)], 11, scalars=(0,), scratch...  4.81 us
    ppermute x1, waiting for transfers between devices, body(): right = lax.ppermute(up, 'tile', [(i + 1, i) for i in range(TILES - 1)])  3.92 us
  transfers between devices with their start and end apart: 4, of which 3 were waited for; matrix products, arithmetic and copies ran while one was open for 0% of the time, Pallas kernels for 2%

profile of v3, /device:TPU:1, one launch (start us, length us, event | category | flops | bytes accessed | tf_op | source)
XLA Modules:
  0.0 118.4 jit_solution(10948576090920512357)
XLA Ops:
  0.6 0.9 copy-done
  1.5 0.7 copy-done.6
  2.2 1.1 shard_map.113
  3.3 0.0 copy-start.2
  3.3 10.3 %all-to-all-start = ((f32[16,32,128]{2,1,0:T(8,128)}), f32[16,32,128]{2,1,0:T(8,128)S(1)}, u32[]{:S(2)}, u32[]{:S(2)}) async-start(f32[16,32,128]{2,1,0:T(8,128)} %shard_map.113), calls=%async_computation | async-start | bytes 524288 | tf_op jit(solution)/shard_map/all_to_all | solution.py:321
  13.6 0.1 pad_add_fusion.where
  13.7 8.7 %all-to-all-done = f32[16,32,128]{2,1,0:T(8,128)S(1)} async-done(((f32[16,32,128]{2,1,0:T(8,128)}), f32[16,32,128]{2,1,0:T(8,128)S(1)}, u32[]{:S(2)}, u32[]{:S(2)}) %all-to-all-start) | async-done | bytes 262176 | tf_op jit(solution)/shard_map/all_to_all | solution.py:321
  22.4 0.7 shard_map.114
  23.1 1.3 %collective-permute-start = (bf16[432,128]{1,0:T(8,128)(2,1)S(1)}, bf16[432,128]{1,0:T(8,128)(2,1)S(1)}, u32[]{:S(2)}, u32[]{:S(2)}) collective-permute-start(bf16[432,128]{1,0:T(8,128)(2,1)S(1)} %get-tuple-element.19), channel_id=1, source_target_pairs={{0,1},{1,2},{2,3},{3,4},{4,5},{5,6},{6,7},{7,8},{8,9},{9,10},{10,1... | collective-permute-start | bytes 331784 | tf_op jit(solution)/shard_map/ppermute | solution.py:357
  24.4 1.3 %collective-permute-start.1 = (bf16[432,128]{1,0:T(8,128)(2,1)S(1)}, bf16[432,128]{1,0:T(8,128)(2,1)S(1)}, u32[]{:S(2)}, u32[]{:S(2)}) collective-permute-start(bf16[432,128]{1,0:T(8,128)(2,1)S(1)} %get-tuple-element.20), channel_id=1, source_target_pairs={{1,0},{2,1},{3,2},{4,3},{5,4},{6,5},{7,6},{8,7},{9,8},{10,9},{11,1... | collective-permute-start | bytes 331784 | tf_op jit(solution)/shard_map/ppermute | solution.py:358
  25.7 0.0 copy-start.3
  25.7 0.0 copy-start.4
  25.8 0.0 copy-start.5
  25.8 0.4 shard_map.115
  26.1 0.0 collective-permute-done.left
  26.2 3.9 %collective-permute-done.1.right = bf16[432,128]{1,0:T(8,128)(2,1)S(1)} collective-permute-done((bf16[432,128]{1,0:T(8,128)(2,1)S(1)}, bf16[432,128]{1,0:T(8,128)(2,1)S(1)}, u32[]{:S(2)}, u32[]{:S(2)}) %collective-permute-start.1) | collective-permute-done | bytes 110624 | tf_op jit(solution)/shard_map/ppermute | solution.py:358
  30.1 4.8 %shard_map.116 = f32[16,24,128]{2,1,0:T(8,128)S(1)} custom-call(s32[3]{0:T(128)S(1)} %pad_add_fusion.where, f32[512,128]{1,0:T(8,128)S(1)} %get-tuple-element.18.own, bf16[432,128]{1,0:T(8,128)(2,1)S(1)} %collective-permute-done.left, bf16[432,128]{1,0:T(8,128)(2,1)S(1)} %collective-permute-done.1.right, f32[32,128]{1,0:T(8,128)S(1)} %get-tuple-element.21.sensor, ...), custom_call_target="tpu_custom_call" | custom-call | tf_op jit(solution)/shard_map/pallas_call | solution.py:376
  34.9 13.0 %all_to_all.30.parts = f32[16,24,128]{2,1,0:T(8,128)S(1)} all-to-all(f32[16,24,128]{2,1,0:T(8,128)S(1)} %shard_map.116), channel_id=1, replica_groups=mesh['depth'=16,'tile'=32] {'depth'}, dimensions={0} | all-to-all | bytes 393216 | tf_op jit(solution)/shard_map/all_to_all | solution.py:321
  47.9 29.7 %all_to_all.31.parts = f32[32,4,128]{2,1,0:T(4,128)S(1)} all-to-all(f32[32,4,128]{2,1,0:T(4,128)S(1)} %shard_map.119), channel_id=1, replica_groups=mesh['depth'=16,'tile'=32] {'tile'}, dimensions={0} | all-to-all | bytes 131072 | tf_op jit(solution)/shard_map/all_to_all | solution.py:321
  77.6 0.6 shard_map.120
  78.3 5.6 %all-to-all-start.3 = ((f32[16,4,128]{2,1,0:T(4,128)}), f32[16,4,128]{2,1,0:T(4,128)S(1)}, u32[]{:S(2)}, u32[]{:S(2)}) async-start(f32[16,4,128]{2,1,0:T(4,128)} %shard_map.120), calls=%async_computation.3 | async-start | bytes 65536 | tf_op jit(solution)/shard_map/all_to_all | solution.py:321
  83.9 0.0 copy-start.8
  83.9 0.7 copy-done.1
  84.6 0.4 shard_map.117
  85.0 1.0 shard_map.118
  86.1 5.1 %all-to-all-done.3.initial = f32[16,4,128]{2,1,0:T(4,128)S(1)} async-done(((f32[16,4,128]{2,1,0:T(4,128)}), f32[16,4,128]{2,1,0:T(4,128)S(1)}, u32[]{:S(2)}, u32[]{:S(2)}) %all-to-all-start.3) | async-done | bytes 32800 | tf_op jit(solution)/shard_map/all_to_all | solution.py:321
  91.2 1.2 %shard_map.121 = (f32[16,8,128]{2,1,0:T(8,128)S(1)}, f32[1,128]{1,0:T(1,128)S(1)}) custom-call(s32[3]{0:T(128)S(1)} %pad_add_fusion.where, f32[16,4,128]{2,1,0:T(4,128)S(1)} %all-to-all-done.3.initial, s32[64,128]{1,0:T(8,128)S(1)} %bitcast.21, f32[256,256]{1,0:T(8,128)S(1)} %get-tuple-element.27.gram, s32[8,256]{1,0:T(8,128)S(1)} %get-tuple-element.28.q_row, ...), custom_call_target="tpu_custom_call" | custom-call | tf_op jit(solution)/shard_map/pallas_call | solution.py:415
  92.4 10.2 %all_to_all.32.parts = f32[16,8,128]{2,1,0:T(8,128)S(1)} all-to-all(f32[16,8,128]{2,1,0:T(8,128)S(1)} %get-tuple-element.32), channel_id=1, replica_groups=mesh['depth'=16,'tile'=32] {'depth'}, dimensions={0} | all-to-all | bytes 131072 | tf_op jit(solution)/shard_map/all_to_all | solution.py:321
  102.6 0.1 shard_map.122
  102.7 15.0 %all_to_all.33.parts = f32[32,1,128]{2,1,0:T(1,128)S(1)} all-to-all(f32[32,1,128]{2,1,0:T(1,128)S(1)} %shard_map.122), channel_id=1, replica_groups=mesh['depth'=16,'tile'=32] {'tile'}, dimensions={0} | all-to-all | bytes 32768 | tf_op jit(solution)/shard_map/all_to_all | solution.py:321
  117.8 0.1 shard_map.123
  117.9 0.5 slice_bitcast_fusion
  (14 shorter events, 0.1 us)
Async XLA Ops:
  0.6 0.9 copy-start
  1.5 0.7 copy-start.6
  3.3 19.1 %copy-start.2 = (f32[32,1024]{1,0:T(8,128)S(1)}, f32[32,1024]{1,0:T(8,128)}, u32[]{:S(2)}) copy-start(f32[32,1024]{1,0:T(8,128)} %measured.1) | copy-start | bytes 393220
  3.3 19.1 %all-to-all-start = ((f32[16,32,128]{2,1,0:T(8,128)}), f32[16,32,128]{2,1,0:T(8,128)S(1)}, u32[]{:S(2)}, u32[]{:S(2)}) async-start(f32[16,32,128]{2,1,0:T(8,128)} %shard_map.113), calls=%async_computation | async-start | bytes 524288 | tf_op jit(solution)/shard_map/all_to_all | solution.py:321
  23.1 3.0 %collective-permute-start = (bf16[432,128]{1,0:T(8,128)(2,1)S(1)}, bf16[432,128]{1,0:T(8,128)(2,1)S(1)}, u32[]{:S(2)}, u32[]{:S(2)}) collective-permute-start(bf16[432,128]{1,0:T(8,128)(2,1)S(1)} %get-tuple-element.19), channel_id=1, source_target_pairs={{0,1},{1,2},{2,3},{3,4},{4,5},{5,6},{6,7},{7,8},{8,9},{9,10},{10,1... | collective-permute-start | bytes 331784 | tf_op jit(solution)/shard_map/ppermute | solution.py:357
  24.4 5.7 %collective-permute-start.1 = (bf16[432,128]{1,0:T(8,128)(2,1)S(1)}, bf16[432,128]{1,0:T(8,128)(2,1)S(1)}, u32[]{:S(2)}, u32[]{:S(2)}) collective-permute-start(bf16[432,128]{1,0:T(8,128)(2,1)S(1)} %get-tuple-element.20), channel_id=1, source_target_pairs={{1,0},{2,1},{3,2},{4,3},{5,4},{6,5},{7,6},{8,7},{9,8},{10,9},{11,1... | collective-permute-start | bytes 331784 | tf_op jit(solution)/shard_map/ppermute | solution.py:358
  25.7 4.4 %copy-start.3 = (s32[8192]{0:T(1024)S(1)}, s32[8192]{0:T(1024)}, u32[]{:S(2)}) copy-start(s32[8192]{0:T(1024)} %param.16) | copy-start | bytes 98308
  25.7 4.3 %copy-start.4 = (s32[8192]{0:T(1024)S(1)}, s32[8192]{0:T(1024)}, u32[]{:S(2)}) copy-start(s32[8192]{0:T(1024)} %param.17) | copy-start | bytes 98308
  25.8 4.3 %copy-start.5 = (s32[8192]{0:T(1024)S(1)}, s32[8192]{0:T(1024)}, u32[]{:S(2)}) copy-start(s32[8192]{0:T(1024)} %param.18) | copy-start | bytes 98308
  47.9 35.9 %copy-start.9 = (bf16[1,256,4,128]{3,2,1,0:T(4,128)(2,1)S(1)}, bf16[1,256,4,128]{3,2,1,0:T(4,128)(2,1)}, u32[]{:S(2)}) copy-start(bf16[1,256,4,128]{3,2,1,0:T(4,128)(2,1)} %param.15) | copy-start | bytes 786436
  78.3 12.9 %all-to-all-start.3 = ((f32[16,4,128]{2,1,0:T(4,128)}), f32[16,4,128]{2,1,0:T(4,128)S(1)}, u32[]{:S(2)}, u32[]{:S(2)}) async-start(f32[16,4,128]{2,1,0:T(4,128)} %shard_map.120), calls=%async_computation.3 | async-start | bytes 65536 | tf_op jit(solution)/shard_map/all_to_all | solution.py:321
  83.8 0.8 copy-start.1
  83.9 0.8 copy-start.8
  83.9 0.7 copy-start.7

commit v4 on v3

--- a/solution.py
+++ b/solution.py
@@ -24,6 +24,8 @@
 ROW = DEPTHS
 BLOCK = 16
 DEEP = 32 * ROW
+CAP = 64
+NAMES = SLOTS + 16
 VMEM = pl.BlockSpec(memory_space=pltpu.VMEM)
 SMEM = pl.BlockSpec(memory_space=pltpu.SMEM)
 
@@ -60,27 +62,98 @@
     return jnp.transpose(jnp.broadcast_to(row, (CB, n)))
 
 
-def prepare_kernel(block, neuron, weights, owner, gram, q_row, q_col, n_col, b_col):
+def lane_sum(x):
+    return jnp.sum(x, axis=1, keepdims=True)
+
+
+def prepare_kernel(
+    where, block, neuron, weights, owner, s_plane, s_row, s_col,
+    gram, q_row, q_col, b_col, a_row, a_lane, rank, code, first, most,
+):
     foot = weights[...]
     product = lax.dot_general(foot, foot, (((1,), (1,)), ((), ())), preferred_element_type=F32)
     blocks = column_of(block[...].astype(F32))
-    neurons = column_of(neuron[...].astype(F32))
     same = jnp.concatenate([blocks, blocks], axis=1) == block[...].astype(F32)
     gram[...] = jnp.where(same, product, 0.0)
-    n_int = neurons.astype(I32)
-    n_col[...] = n_int
     b_col[...] = blocks.astype(I32)
     table = owner[...]
-    tables = jnp.concatenate([(table >> 7).astype(F32), (table & 127).astype(F32)], axis=1).astype(BF16)
-    hot = (iota((SLOTS, 64), 1) == (n_int[:, :64] >> 7)).astype(F32).astype(BF16)
+    number = iota((64, CB), 0) * CB + iota((64, CB), 1)
+    own = jnp.zeros((16, CB), F32)
+    for i in range(16):
+        hit = jnp.sum(jnp.where(table == where[2] + i, number.astype(F32), 0.0), axis=0, keepdims=True)
+        own = jnp.where(iota((16, CB), 0) == i, lane_sum(hit), own)
+    names = jnp.concatenate([column_of(neuron[...].astype(F32)), own], axis=0).astype(I32)
+    row, col = s_row[...], s_col[...]
+    tile, window = row >> 5, col >> 6
+    tables = [tile, window, table >> 7, table & 127]
+    tables = jnp.concatenate([x.astype(F32) for x in tables], axis=1).astype(BF16)
+    hot = (iota((NAMES, 64), 1) == (names[:, :64] >> 7)).astype(F32).astype(BF16)
     found = jnp.dot(hot, tables, preferred_element_type=F32)
-    lane_hot = iota((SLOTS, CB), 1) == (n_int & 127)
-    value = jnp.where(lane_hot, found[:, :CB] * 128.0 + found[:, CB:], 0.0)
-    place = jnp.sum(value, axis=1, keepdims=True)
-    place = jnp.broadcast_to(place, (SLOTS, CB))
-    place = jnp.where(n_int >= 0, place, -1.0)
+    lane_hot = iota((NAMES, CB), 1) == (names & 127)
+    picked = [lane_sum(jnp.where(lane_hot, found[:, i * CB : (i + 1) * CB], 0.0)) for i in range(4)]
+    n_tile, n_window = picked[0].astype(I32), picked[1].astype(I32)
+    place = jnp.broadcast_to(picked[2] * 128.0 + picked[3], (NAMES, CB))[:SLOTS]
+    place = jnp.where(names[:SLOTS] >= 0, place, -1.0)
     q_col[...] = place.astype(I32)
     q_row[...] = jnp.transpose(place)[0:8, :].astype(I32)
+    keys = (tile * DEPTHS + window) * NEURONS + number
+    low = jnp.broadcast_to((n_tile * DEPTHS + n_window) * NEURONS, (NAMES, CB))
+    high = low + names
+    count = jnp.zeros((NAMES, CB), F32)
+    for r in range(64):
+        key = keys[r : r + 1, :]
+        count = count + jnp.where((key >= low) & (key < high), 1.0, 0.0)
+    position = jnp.broadcast_to(lane_sum(count), (NAMES, CB)).astype(I32)
+    at = (position // CAP) * 256 + n_tile * 8 + (n_window >> 1)
+    a_row[...] = jnp.where(names >= 0, at, -1)
+    a_lane[...] = (n_window & 1) * CAP + position % CAP
+    local = (tile == where[1]) & (window == where[0])
+    mask = local.astype(F32)
+    before = (iota((CB, CB), 0) < iota((CB, CB), 1)).astype(F32).astype(BF16)
+    inside = jnp.dot(mask.astype(BF16), before, preferred_element_type=F32)
+    rows = jnp.broadcast_to(lane_sum(mask), (64, CB)).astype(BF16)
+    above = (iota((64, 64), 1) < iota((64, 64), 0)).astype(F32).astype(BF16)
+    inside = inside + jnp.dot(above, rows, preferred_element_type=F32)
+    order = jnp.where(local, inside, -1.0).astype(I32)
+    spot = ((row >> 4) & 1) * WIN + (col & (WIN - 1))
+    coded = ((row & 15) * ROW + s_plane[...]) * CB + spot + 1
+    rank[...] = order
+    code[...] = coded
+    first[...] = listed(order, coded, 0)
+    both = jnp.zeros((TILES, DEPTHS), F32)
+    for r in range(0, 64, 8):
+        tiles = [iota((TILES, CB), 0) == tile[i : i + 1, :] for i in range(r, r + 8)]
+        windows = [iota((DEPTHS, CB), 0) == window[i : i + 1, :] for i in range(r, r + 8)]
+        tiles = jnp.concatenate([x.astype(F32) for x in tiles], axis=1).astype(BF16)
+        windows = jnp.concatenate([x.astype(F32) for x in windows], axis=1).astype(BF16)
+        both = both + lax.dot_general(
+            tiles, windows, (((1,), (1,)), ((), ())), preferred_element_type=F32
+        )
+    top = jnp.max(jnp.max(both, axis=0, keepdims=True), axis=1, keepdims=True)
+    most[...] = jnp.broadcast_to(top, (8, CB)).astype(I32)
+
+
+def listed(order, coded, start):
+    result = jnp.zeros((CAP, CB), F32)
+    wanted = iota((CAP, CB), 0) + start
+    for r in range(64):
+        result = result + jnp.where(
+            wanted == order[r : r + 1, :], coded[r : r + 1, :].astype(F32), 0.0
+        )
+    return jnp.broadcast_to(lane_sum(result), (CAP, CB)).astype(I32)
+
+
+def seed_values(codes, flat):
+    index = codes - 1
+    key = jnp.concatenate([index, index], axis=1) >> 7
+    hot = (iota((CAP, 256), 1) == key).astype(F32).astype(BF16)
+    parts = split3(flat)
+    found = jnp.dot(hot, parts[0], preferred_element_type=F32)
+    found = found + jnp.dot(hot, parts[1], preferred_element_type=F32)
+    found = found + jnp.dot(hot, parts[2], preferred_element_type=F32)
+    value = lane_sum(jnp.where(iota((CAP, CB), 1) == (index & (CB - 1)), found, 0.0))
+    value = jnp.broadcast_to(value, (CAP, CB))
+    return jnp.transpose(jnp.concatenate([value, value], axis=0))[0:1, :]
 
 
 def window_kernel(volume, spread, windows, local, arrived):
@@ -155,8 +228,8 @@
 
 
 def iterate_kernel(
-    where, own, left, right, sensor, ahead, behind, scale, s_plane, s_row, s_col,
-    sent, exact, rounded, first, second, light, sums, ratio, stack, packed,
+    own, left, right, sensor, ahead, behind, scale, codes,
+    sent, flat, exact, rounded, first, second, light, sums, ratio, stack,
 ):
     rows = (HALO * ROW, (HALO + ROWS) * ROW, (2 * HALO + ROWS) * ROW)
     exact[: rows[0], :] = left[: rows[0]].astype(F32)
@@ -207,35 +280,45 @@
     spread_back(2)
     done = [first[(m * 16 + 12) * ROW : (m * 16 + 28) * ROW, :] * back(m) for m in range(2)]
     lane = iota((256, CB), 1)
-    flat = jnp.where(lane < WIN, pltpu.roll(done[0], CB - HALO, 1), pltpu.roll(done[1], WIN - HALO, 1))
-    packed[...] = flat
+    packed = jnp.where(lane < WIN, pltpu.roll(done[0], CB - HALO, 1), pltpu.roll(done[1], WIN - HALO, 1))
+    flat[...] = packed
+    values = jnp.broadcast_to(seed_values(codes[...], packed), (8, CB))
     for p in range(DEPTHS):
-        sent[p, 0:16, :] = packed[pl.ds(p, 16, stride=ROW), :]
-        sent[p, 20:24, :] = jnp.zeros((4, CB), F32)
-    left_side = jnp.concatenate(split2(jnp.transpose(flat)), axis=0)
-    chunk = NEURONS // DEPTHS
-    for j in range(DEPTHS):
-        plane, row, col = s_plane[j], s_row[j], s_col[j]
-        local = ((row >> 5) == where[1]) & ((col >> 6) == where[0])
-        key = jnp.where(local, (row & 15) * ROW + plane, -1)
-        hot = (iota((256, chunk), 0) == key).astype(F32).astype(BF16)
-        found = jnp.dot(left_side, hot, preferred_element_type=F32)
-        found = found[:CB] + found[CB:]
-        spot = ((row >> 4) & 1) * WIN + (col & (WIN - 1))
-        picked = jnp.sum(jnp.where(iota((CB, chunk), 0) == spot, found, 0.0), axis=0, keepdims=True)
-        for i in range(4):
-            sent[j, 16 + i : 17 + i, :] = picked[:, i * CB : (i + 1) * CB]
-
-
-def sum_kernel(count, at, copies):
+        sent[p, 0:16, :] = flat[pl.ds(p, 16, stride=ROW), :]
+        sent[p, 16:24, :] = values
+
+
+def more_kernel(start, rank, code, flat, sent):
+    codes = listed(rank[...], code[...], start[0])
+    values = jnp.broadcast_to(seed_values(codes, flat[...]), (8, CB))
+    for p in range(DEPTHS):
+        sent[p] = values
+
+
+def gather_kernel(at):
     def kernel(parts, out):
-        total = parts[0, at : at + 4, :]
-        for j in range(1, count):
-            total = total + parts[j, at : at + 4, :]
-        for j in range(copies):
+        lane = iota((1, CB), 1)
+        rows = [
+            jnp.where(lane < CAP, parts[2 * m, at : at + 1, :], parts[2 * m + 1, at : at + 1, :])
+            for m in range(8)
+        ]
+        total = jnp.concatenate(rows, axis=0)
+        for j in range(TILES):
             out[j] = total
 
     return kernel
+
+
+def look_kernel(start, parts, a_row, a_lane, known, out):
+    table = jnp.concatenate([parts[t] for t in range(TILES)], axis=0)
+    row = a_row[...] - start[0] * (256 // CAP)
+    hot = (iota((NAMES, 256), 1) == jnp.concatenate([row, row], axis=1)).astype(F32).astype(BF16)
+    parts = split3(table)
+    found = jnp.dot(hot, parts[0], preferred_element_type=F32)
+    found = found + jnp.dot(hot, parts[1], preferred_element_type=F32)
+    found = found + jnp.dot(hot, parts[2], preferred_element_type=F32)
+    value = lane_sum(jnp.where(iota((NAMES, CB), 1) == a_lane[...], found, 0.0))
+    out[...] = known[...] + jnp.broadcast_to(value, (NAMES, CB))
 
 
 def home_kernel(parts, weights, b_col, estimate, proj, lines):
@@ -262,17 +345,11 @@
     proj[...] = jnp.broadcast_to(jnp.sum(total, axis=1, keepdims=True), (SLOTS, CB))
 
 
-def slots_kernel(where, initial, owner, gram, q_row, q_col, n_col, proj, out, own):
-    table = jnp.concatenate([initial[j] for j in range(DEPTHS)], axis=0)
-    number = n_col[...]
-    hot = (iota((SLOTS, 64), 1) == (number[:, :64] >> 7)).astype(F32).astype(BF16)
-    parts = split3(table)
-    found = jnp.dot(hot, parts[0], preferred_element_type=F32)
-    found = found + jnp.dot(hot, parts[1], preferred_element_type=F32)
-    found = found + jnp.dot(hot, parts[2], preferred_element_type=F32)
-    value = jnp.where(iota((SLOTS, CB), 1) == (number & (CB - 1)), found, 0.0)
-    start = jnp.broadcast_to(jnp.sum(value, axis=1, keepdims=True), (SLOTS, CB))
-    start_row = jnp.transpose(start)[0:1, :]
+def slots_kernel(start, gram, q_row, q_col, proj, out, own):
+    padded = jnp.concatenate([start[...], jnp.zeros((3 * CB - NAMES, CB), F32)], axis=0)
+    row = jnp.transpose(padded)[0:1, :]
+    own[...] = row[:, SLOTS:]
+    start_row = row[:, :SLOTS]
     terms = gram[...] * start_row
     over = jnp.sum(terms[:, :CB] + terms[:, CB:], axis=1, keepdims=True)
     place = q_col[...]
@@ -286,14 +363,6 @@
     dense = dense + jnp.dot(row_hot, parts[2], preferred_element_type=F32)
     for j in range(DEPTHS):
         out[j] = dense[j * 8 : (j + 1) * 8]
-    base = where[2]
-    holder = owner[...]
-    lanes = iota((1, CB), 1)
-    result = jnp.zeros((1, CB), F32)
-    for i in range(16):
-        mine = jnp.sum(jnp.where(holder == base + i, table, 0.0), axis=0, keepdims=True)
-        result = jnp.where(lanes == i, jnp.sum(mine, axis=1, keepdims=True), result)
-    own[...] = result
 
 
 def fold_kernel(parts, out):
@@ -360,24 +429,39 @@
         tables_kernel, [((256, DEEP), BF16), ((256, DEEP), BF16), ((ROW, CB), F32)], 1
     )(parts)
     weights = footprints[0].reshape(SLOTS, 512)
-    gram, q_row, q_col, n_col, b_col = call(
+    column = ((SLOTS, CB), I32)
+    names = ((NAMES, CB), I32)
+    square = ((64, CB), I32)
+    gram, q_row, q_col, b_col, a_row, a_lane, rank, code, first, most = call(
         prepare_kernel,
         [
             ((SLOTS, SLOTS), F32),
             ((8, SLOTS), I32),
-            ((SLOTS, CB), I32),
-            ((SLOTS, CB), I32),
-            ((SLOTS, CB), I32),
+            column,
+            column,
+            names,
+            names,
+            square,
+            square,
+            ((CAP, CB), I32),
+            ((8, CB), I32),
         ],
-        4,
-    )(entry_block, entry_neuron, weights, table)
-    chunk = NEURONS // DEPTHS
-    shape = (DEPTHS, 1, chunk)
-    [sent] = call(
+        8,
+        scalars=(0,),
+    )(
+        where,
+        entry_block,
+        entry_neuron,
+        weights,
+        table,
+        seed_plane.reshape(64, CB),
+        seed_row.reshape(64, CB),
+        seed_col.reshape(64, CB),
+    )
+    sent, flat = call(
         iterate_kernel,
-        [((DEPTHS, 24, CB), F32)],
-        11,
-        scalars=(0,),
+        [((DEPTHS, 24, CB), F32), ((256, CB), F32)],
+        8,
         scratch=[
             pltpu.VMEM((96 * ROW, CB), F32),
             pltpu.VMEM((96 * ROW, CB), BF16),
@@ -387,33 +471,36 @@
             pltpu.VMEM((256, CB), F32),
             pltpu.VMEM((80, CB), F32),
             pltpu.VMEM((4 * DEEP, CB), BF16),
-            pltpu.VMEM((256, CB), F32),
         ],
-    )(
-        where,
-        own,
-        left,
-        right,
-        sensor,
-        ahead,
-        behind,
-        scale,
-        seed_plane.reshape(shape),
-        seed_row.reshape(shape),
-        seed_col.reshape(shape),
-    )
+    )(own, left, right, sensor, ahead, behind, scale, first)
     parts = swap(sent, "depth")
-    [mine] = call(sum_kernel(DEPTHS, 16, TILES), [((TILES, 4, CB), F32)], 1)(parts)
-    [mine] = call(sum_kernel(TILES, 0, DEPTHS), [((DEPTHS, 4, CB), F32)], 1)(swap(mine, "tile"))
-    initial = swap(mine, "depth")
+
+    def share(values, at):
+        [values] = call(gather_kernel(at), [((TILES, 8, CB), F32)], 1)(values)
+        return swap(values, "tile")
+
+    def look(begin, values, known):
+        return call(look_kernel, [((NAMES, CB), F32)], 5, scalars=(0,))(
+            begin, values, a_row, a_lane, known
+        )[0]
+
+    def another(step, known):
+        begin = jnp.reshape(step * CAP, (1,))
+        [values] = call(more_kernel, [((DEPTHS, 8, CB), F32)], 4, scalars=(0,))(
+            begin, rank, code, flat
+        )
+        return look(begin, share(swap(values, "depth"), 0), known)
+
+    known = look(jnp.zeros((1,), I32), share(parts, 16), jnp.zeros((NAMES, CB), F32))
+    known = lax.fori_loop(1, (most[0, 0] + CAP - 1) // CAP, another, known)
     estimate, proj = call(
         home_kernel,
         [((ROWS, COLS), F32), ((SLOTS, CB), F32)],
         3,
         scratch=[pltpu.VMEM((NCB * ROWS, CB), F32)],
     )(parts, weights, b_col)
-    sent, own = call(slots_kernel, [((DEPTHS, 8, CB), F32), ((1, CB), F32)], 8, scalars=(0,))(
-        where, initial, table, gram, q_row, q_col, n_col, proj
+    sent, own = call(slots_kernel, [((DEPTHS, 8, CB), F32), ((1, CB), F32)], 5)(
+        known, gram, q_row, q_col, proj
     )
     [sent] = call(fold_kernel, [((TILES, 1, CB), F32)], 1)(swap(sent, "depth"))
     [demixed] = call(final_kernel, [((1, CB), F32)], 2)(swap(sent, "tile"), own)

time: 119 us -> 108 us (0.908)
  blocking collectives: 67.9 us -> 40.9 us
  starting transfers between devices: 18.5 us -> 30.7 us
  waiting for transfers between devices: 17.7 us -> 20.5 us
    all_to_all x4 -> x3, blocking collectives: 67.9 us -> 40.9 us  [swap(): return lax.all_to_all(pieces, axis, 0, 0)]
    all_to_all x2, starting transfers between devices: 15.9 us -> 28.1 us  [swap(): return lax.all_to_all(pieces, axis, 0, 0)]
    all_to_all x2, waiting for transfers between devices: 13.8 us -> 20.5 us  [swap(): return lax.all_to_all(pieces, axis, 0, 0)]
    ppermute x1, waiting for transfers between devices: 3.92 us -> 0.01 us  [body(): right = lax.ppermute(up, 'tile', [(i + 1, i) for i in range(TILES - 1)])]
  transfers between devices with their start and end apart: 4 -> 4, of which waited for: 3 -> 2; matrix products, arithmetic and copies ran while one was open for 0% -> 1% of each run, Pallas kernels for 2% -> 5%
where the time goes in v4:
time: 108 us
  blocking collectives  40.9 us (38%)
  starting transfers between devices  30.7 us (28%)
  waiting for transfers between devices  20.5 us (19%)
  Pallas kernels  10.5 us (10%)
  local copies, waits for them, and re-layouts  3.4 us (3%)
  between operations  1.49 us (1%)
    all_to_all x3, blocking collectives, swap(): return lax.all_to_all(pieces, axis, 0, 0)  40.9 us
    all_to_all x2, starting transfers between devices, swap(): return lax.all_to_all(pieces, axis, 0, 0)  28.1 us
    all_to_all x2, waiting for transfers between devices, swap(): return lax.all_to_all(pieces, axis, 0, 0)  20.5 us
    pallas_call x1, Pallas kernels, body(): call(prepare_kernel, [((SLOTS, SLOTS), F32), ((8, SLOTS), I32), column, c...  3.46 us
    unnamed x21, local copies, waits for them, and re-layouts  2.36 us
    pallas_call x1, Pallas kernels, body(): call(iterate_kernel, [((DEPTHS, 24, CB), F32), ((256, CB), F32)], 8, scra...  2.24 us
  transfers between devices with their start and end apart: 4, of which 2 were waited for; matrix products, arithmetic and copies ran while one was open for 1% of the time, Pallas kernels for 5%

profile of v4, /device:TPU:1, one launch (start us, length us, event | category | flops | bytes accessed | tf_op | source)
XLA Modules:
  0.0 107.6 jit_solution(1691295579196792419)
XLA Ops:
  0.6 0.9 copy-done
  1.5 0.7 copy-done.6
  2.2 1.1 shard_map.113
  3.3 10.3 %all-to-all-start.2 = ((f32[16,32,128]{2,1,0:T(8,128)}), f32[16,32,128]{2,1,0:T(8,128)S(1)}, u32[]{:S(2)}, u32[]{:S(2)}) async-start(f32[16,32,128]{2,1,0:T(8,128)} %shard_map.113), calls=%async_computation.2 | async-start | bytes 524288 | tf_op jit(solution)/shard_map/all_to_all | solution.py:390
  13.7 0.1 pad_add_fusion.where
  13.7 8.7 %all-to-all-done.2 = f32[16,32,128]{2,1,0:T(8,128)S(1)} async-done(((f32[16,32,128]{2,1,0:T(8,128)}), f32[16,32,128]{2,1,0:T(8,128)S(1)}, u32[]{:S(2)}, u32[]{:S(2)}) %all-to-all-start.2) | async-done | bytes 262176 | tf_op jit(solution)/shard_map/all_to_all | solution.py:390
  22.4 0.7 shard_map.114
  23.1 1.3 %collective-permute-start = (bf16[432,128]{1,0:T(8,128)(2,1)S(1)}, bf16[432,128]{1,0:T(8,128)(2,1)S(1)}, u32[]{:S(2)}, u32[]{:S(2)}) collective-permute-start(bf16[432,128]{1,0:T(8,128)(2,1)S(1)} %get-tuple-element.69), channel_id=1, source_target_pairs={{0,1},{1,2},{2,3},{3,4},{4,5},{5,6},{6,7},{7,8},{8,9},{9,10},{10,1... | collective-permute-start | bytes 331784 | tf_op jit(solution)/shard_map/ppermute | solution.py:426
  24.4 1.3 %collective-permute-start.1 = (bf16[432,128]{1,0:T(8,128)(2,1)S(1)}, bf16[432,128]{1,0:T(8,128)(2,1)S(1)}, u32[]{:S(2)}, u32[]{:S(2)}) collective-permute-start(bf16[432,128]{1,0:T(8,128)(2,1)S(1)} %get-tuple-element.70), channel_id=1, source_target_pairs={{1,0},{2,1},{3,2},{4,3},{5,4},{6,5},{7,6},{8,7},{9,8},{10,9},{11,1... | collective-permute-start | bytes 331784 | tf_op jit(solution)/shard_map/ppermute | solution.py:427
  25.7 0.0 copy-start.2
  25.8 0.0 copy-start.5
  25.8 0.0 copy-start.8
  25.9 0.6 copy-done.2
  26.5 0.0 copy-done.3
  26.5 0.0 copy-done.4
  26.5 0.0 copy-done.5
  26.6 3.5 %shard_map.116 = (f32[256,256]{1,0:T(8,128)S(1)}, s32[8,256]{1,0:T(8,128)S(1)}, s32[256,128]{1,0:T(8,128)S(1)}, s32[256,128]{1,0:T(8,128)S(1)}, s32[272,128]{1,0...) custom-call(s32[3]{0:T(128)S(1)} %pad_add_fusion.where, ...), custom_call_target="tpu_custom_call" | custom-call | tf_op jit(solution)/shard_map/pallas_call | solution.py:435
  30.0 0.4 shard_map.115
  30.4 2.2 %shard_map.117 = (f32[16,24,128]{2,1,0:T(8,128)S(1)}, f32[256,128]{1,0:T(8,128)S(1)}) custom-call(f32[512,128]{1,0:T(8,128)S(1)} %get-tuple-element.68.own, bf16[432,128]{1,0:T(8,128)(2,1)S(1)} %collective-permute-done.left, bf16[432,128]{1,0:T(8,128)(2,1)S(1)} %collective-permute-done.1.right, f32[32,128]{1,0:T(8,128)S(1)} %get-tuple-element.71.sensor, ...), custom_call_target="tpu_custom_call" | custom-call | tf_op jit(solution)/shard_map/pallas_call | solution.py:461
  32.7 12.7 %all_to_all.37.parts = f32[16,24,128]{2,1,0:T(8,128)S(1)} all-to-all(f32[16,24,128]{2,1,0:T(8,128)S(1)} %get-tuple-element.76), channel_id=1, replica_groups=mesh['depth'=16,'tile'=32] {'depth'}, dimensions={0} | all-to-all | bytes 393216 | tf_op jit(solution)/shard_map/all_to_all | solution.py:390
  45.3 0.7 shard_map.119
  46.0 17.7 %all-to-all-start.4 = ((f32[32,8,128]{2,1,0:T(8,128)}), f32[32,8,128]{2,1,0:T(8,128)S(1)}, u32[]{:S(2)}, u32[]{:S(2)}) async-start(f32[32,8,128]{2,1,0:T(8,128)} %shard_map.119), calls=%async_computation.4 | async-start | bytes 262144 | tf_op jit(solution)/shard_map/all_to_all | solution.py:390
  63.7 0.5 slice.6
  64.9 1.0 shard_map.118
  66.0 11.8 %all-to-all-done.4.parts = f32[32,8,128]{2,1,0:T(8,128)S(1)} async-done(((f32[32,8,128]{2,1,0:T(8,128)}), f32[32,8,128]{2,1,0:T(8,128)S(1)}, u32[]{:S(2)}, u32[]{:S(2)}) %all-to-all-start.4) | async-done | bytes 131104 | tf_op jit(solution)/shard_map/all_to_all | solution.py:390
  77.8 0.4 shard_map.120
  78.2 0.4 shard_map.121
  78.6 13.2 %all_to_all.38.parts = f32[16,8,128]{2,1,0:T(8,128)S(1)} all-to-all(f32[16,8,128]{2,1,0:T(8,128)S(1)} %get-tuple-element.90), channel_id=1, replica_groups=mesh['depth'=16,'tile'=32] {'depth'}, dimensions={0} | all-to-all | bytes 131072 | tf_op jit(solution)/shard_map/all_to_all | solution.py:390
  91.8 0.1 shard_map.122
  91.9 15.1 %all_to_all.39.parts = f32[32,1,128]{2,1,0:T(1,128)S(1)} all-to-all(f32[32,1,128]{2,1,0:T(1,128)S(1)} %shard_map.122), channel_id=1, replica_groups=mesh['depth'=16,'tile'=32] {'tile'}, dimensions={0} | all-to-all | bytes 32768 | tf_op jit(solution)/shard_map/all_to_all | solution.py:390
  107.0 0.1 shard_map.123
  107.1 0.5 slice_bitcast_fusion
  (16 shorter events, 0.1 us)
Async XLA Ops:
  0.6 0.9 copy-start
  1.5 0.7 copy-start.6
  3.3 19.1 %copy-start.1 = (f32[32,1024]{1,0:T(8,128)S(1)}, f32[32,1024]{1,0:T(8,128)}, u32[]{:S(2)}) copy-start(f32[32,1024]{1,0:T(8,128)} %measured.1) | copy-start | bytes 393220
  3.3 19.1 %all-to-all-start.2 = ((f32[16,32,128]{2,1,0:T(8,128)}), f32[16,32,128]{2,1,0:T(8,128)S(1)}, u32[]{:S(2)}, u32[]{:S(2)}) async-start(f32[16,32,128]{2,1,0:T(8,128)} %shard_map.113), calls=%async_computation.2 | async-start | bytes 524288 | tf_op jit(solution)/shard_map/all_to_all | solution.py:390
  13.7 12.1 %copy-start.9 = (bf16[1,256,4,128]{3,2,1,0:T(4,128)(2,1)S(1)}, bf16[1,256,4,128]{3,2,1,0:T(4,128)(2,1)}, u32[]{:S(2)}) copy-start(bf16[1,256,4,128]{3,2,1,0:T(4,128)(2,1)} %param.17) | copy-start | bytes 786436
  23.1 7.3 %collective-permute-start = (bf16[432,128]{1,0:T(8,128)(2,1)S(1)}, bf16[432,128]{1,0:T(8,128)(2,1)S(1)}, u32[]{:S(2)}, u32[]{:S(2)}) collective-permute-start(bf16[432,128]{1,0:T(8,128)(2,1)S(1)} %get-tuple-element.69), channel_id=1, source_target_pairs={{0,1},{1,2},{2,3},{3,4},{4,5},{5,6},{6,7},{7,8},{8,9},{9,10},{10,1... | collective-permute-start | bytes 331784 | tf_op jit(solution)/shard_map/ppermute | solution.py:426
  24.4 6.0 %collective-permute-start.1 = (bf16[432,128]{1,0:T(8,128)(2,1)S(1)}, bf16[432,128]{1,0:T(8,128)(2,1)S(1)}, u32[]{:S(2)}, u32[]{:S(2)}) collective-permute-start(bf16[432,128]{1,0:T(8,128)(2,1)S(1)} %get-tuple-element.70), channel_id=1, source_target_pairs={{1,0},{2,1},{3,2},{4,3},{5,4},{6,5},{7,6},{8,7},{9,8},{10,9},{11,1... | collective-permute-start | bytes 331784 | tf_op jit(solution)/shard_map/ppermute | solution.py:427
  25.7 0.8 copy-start.2
  25.8 0.8 copy-start.3
  25.8 0.8 copy-start.4
  25.8 0.8 copy-start.5
  25.8 0.8 copy-start.8
  25.9 0.7 copy-start.7
  46.0 31.8 %all-to-all-start.4 = ((f32[32,8,128]{2,1,0:T(8,128)}), f32[32,8,128]{2,1,0:T(8,128)S(1)}, u32[]{:S(2)}, u32[]{:S(2)}) async-start(f32[32,8,128]{2,1,0:T(8,128)} %shard_map.119), calls=%async_computation.4 | async-start | bytes 262144 | tf_op jit(solution)/shard_map/all_to_all | solution.py:390

commit v5 on v4

--- a/solution.py
+++ b/solution.py
@@ -130,7 +130,7 @@
             tiles, windows, (((1,), (1,)), ((), ())), preferred_element_type=F32
         )
     top = jnp.max(jnp.max(both, axis=0, keepdims=True), axis=1, keepdims=True)
-    most[...] = jnp.broadcast_to(top, (8, CB)).astype(I32)
+    most[...] = (jnp.broadcast_to(top, (8, CB)).astype(I32) + (CAP - 1)) >> 6
 
 
 def listed(order, coded, start):
@@ -156,9 +156,12 @@
     return jnp.transpose(jnp.concatenate([value, value], axis=0))[0:1, :]
 
 
-def window_kernel(volume, spread, windows, local, arrived):
-    copy = pltpu.make_async_copy(volume.at[0], local, arrived)
+def window_kernel(volume, point_spread, windows, local, spread, arrived):
+    small = pltpu.make_async_copy(point_spread, spread, arrived.at[1])
+    small.start()
+    copy = pltpu.make_async_copy(volume.at[0], local, arrived.at[0])
     copy.start()
+    small.wait()
     lane = iota((ROWS, CB), 1)
     taps = jnp.concatenate([spread[0].astype(F32), jnp.zeros((KS, CB - KS), F32)], axis=1)
     taps = jnp.concatenate([pltpu.roll(taps, LIVE, 1), jnp.zeros((ROWS - KS, CB), F32)], axis=0)
@@ -383,7 +386,7 @@
     initial = own[...]
     real = iota((1, CB), 1) < 16
     bottom = jnp.where(real, over + 100.0 * initial, 1.0)
-    out[...] = jnp.where(real, initial * total, 0.0) / bottom
+    out[...] = (jnp.where(real, initial * total, 0.0) / bottom)[:, :16]
 
 
 def swap(pieces, axis):
@@ -409,25 +412,17 @@
     [windows] = pl.pallas_call(
         window_kernel,
         out_shape=[jax.ShapeDtypeStruct((DEPTHS, ROWS, CB), F32)],
-        in_specs=[pl.BlockSpec(memory_space=pl.ANY), VMEM],
+        in_specs=[pl.BlockSpec(memory_space=pltpu.HBM)] * 2,
         out_specs=[VMEM],
-        scratch_shapes=[pltpu.VMEM((ROWS, COLS), F32), pltpu.SemaphoreType.DMA],
+        scratch_shapes=[
+            pltpu.VMEM((ROWS, COLS), F32),
+            pltpu.VMEM((1, KS, KS), BF16),
+            pltpu.SemaphoreType.DMA((2,)),
+        ],
         compiler_params=pltpu.CompilerParams(vmem_limit_bytes=24 * 2**20),
     )(volume, point_spread)
     parts = swap(windows, "depth").reshape(DEPTHS * ROWS, CB)
     message = ((HALO * ROW + 2 * HALO, CB), BF16)
-    own, sensor, down, up = call(
-        arrange_kernel,
-        [((ROWS * ROW, CB), F32), ((ROWS, CB), F32), message, message],
-        3,
-        scalars=(0,),
-        scratch=[pltpu.VMEM((ROWS, COLS + 2 * CB), F32)],
-    )(where, parts, measured)
-    left = lax.ppermute(down, "tile", [(i, i + 1) for i in range(TILES - 1)])
-    right = lax.ppermute(up, "tile", [(i + 1, i) for i in range(TILES - 1)])
-    ahead, behind, scale = call(
-        tables_kernel, [((256, DEEP), BF16), ((256, DEEP), BF16), ((ROW, CB), F32)], 1
-    )(parts)
     weights = footprints[0].reshape(SLOTS, 512)
     column = ((SLOTS, CB), I32)
     names = ((NAMES, CB), I32)
@@ -458,6 +453,19 @@
         seed_row.reshape(64, CB),
         seed_col.reshape(64, CB),
     )
+    view, first, rounds = lax.optimization_barrier((measured, first, most[0, 0]))
+    own, sensor, down, up = call(
+        arrange_kernel,
+        [((ROWS * ROW, CB), F32), ((ROWS, CB), F32), message, message],
+        3,
+        scalars=(0,),
+        scratch=[pltpu.VMEM((ROWS, COLS + 2 * CB), F32)],
+    )(where, parts, view)
+    left = lax.ppermute(down, "tile", [(i, i + 1) for i in range(TILES - 1)])
+    right = lax.ppermute(up, "tile", [(i + 1, i) for i in range(TILES - 1)])
+    ahead, behind, scale = call(
+        tables_kernel, [((256, DEEP), BF16), ((256, DEEP), BF16), ((ROW, CB), F32)], 1
+    )(parts)
     sent, flat = call(
         iterate_kernel,
         [((DEPTHS, 24, CB), F32), ((256, CB), F32)],
@@ -491,8 +499,9 @@
         )
         return look(begin, share(swap(values, "depth"), 0), known)
 
-    known = look(jnp.zeros((1,), I32), share(parts, 16), jnp.zeros((NAMES, CB), F32))
-    known = lax.fori_loop(1, (most[0, 0] + CAP - 1) // CAP, another, known)
+    shared, parts = lax.optimization_barrier((share(parts, 16), parts))
+    known = look(jnp.zeros((1,), I32), shared, jnp.zeros((NAMES, CB), F32))
+    known = lax.fori_loop(1, rounds, another, known)
     estimate, proj = call(
         home_kernel,
         [((ROWS, COLS), F32), ((SLOTS, CB), F32)],
@@ -503,8 +512,8 @@
         known, gram, q_row, q_col, proj
     )
     [sent] = call(fold_kernel, [((TILES, 1, CB), F32)], 1)(swap(sent, "depth"))
-    [demixed] = call(final_kernel, [((1, CB), F32)], 2)(swap(sent, "tile"), own)
-    return estimate[None], demixed[0, :16]
+    [demixed] = call(final_kernel, [((1, 16), F32)], 2)(swap(sent, "tile"), own)
+    return estimate[None], demixed[0]
 
 
 def solution(mesh):

time: 108 us -> 110 us (1.019)
  waiting for transfers between devices: 20.5 us -> 21.8 us
    ppermute x1, waiting for transfers between devices: 0.01 us -> 3.92 us  [body(): right = lax.ppermute(up, 'tile', [(i + 1, i) for i in range(TILES - 1)])]
    all_to_all x2, waiting for transfers between devices: 20.5 us -> 17.9 us  [swap(): return lax.all_to_all(pieces, axis, 0, 0)]
  transfers between devices with their start and end apart: 4 -> 4, of which waited for: 2 -> 3; matrix products, arithmetic and copies ran while one was open for 1% -> 1% of each run, Pallas kernels for 5% -> 4%
where the time goes in v5:
time: 110 us; the launch traced here: 109 us
  blocking collectives  41.8 us (38%)
  starting transfers between devices  30.1 us (27%)
  waiting for transfers between devices  21.8 us (20%)
  Pallas kernels  11 us (10%)
  local copies, waits for them, and re-layouts  2.93 us (3%)
    all_to_all x3, blocking collectives, swap(): return lax.all_to_all(pieces, axis, 0, 0)  41.8 us
    all_to_all x2, starting transfers between devices, swap(): return lax.all_to_all(pieces, axis, 0, 0)  27.5 us
    all_to_all x2, waiting for transfers between devices, swap(): return lax.all_to_all(pieces, axis, 0, 0)  17.9 us
    ppermute x1, waiting for transfers between devices, body(): right = lax.ppermute(up, 'tile', [(i + 1, i) for i in range(TILES - 1)])  3.92 us
    pallas_call x1, Pallas kernels, body(): call(prepare_kernel, [((SLOTS, SLOTS), F32), ((8, SLOTS), I32), column, c...  3.46 us
    unnamed x21, local copies, waits for them, and re-layouts  2.35 us
    pallas_call x1, Pallas kernels, body(): call(iterate_kernel, [((DEPTHS, 24, CB), F32), ((256, CB), F32)], 8, scra...  2.25 us
  transfers between devices with their start and end apart: 4, of which 3 were waited for; matrix products, arithmetic and copies ran while one was open for 1% of the time, Pallas kernels for 4%

profile of v5, /device:TPU:1, one launch (start us, length us, event | category | flops | bytes accessed | tf_op | source)
XLA Modules:
  0.0 109.3 jit_solution(17980278377911201453)
XLA Ops:
  0.6 0.9 copy-done
  1.5 0.7 copy-done.6
  2.2 1.1 shard_map.113
  3.3 10.3 %all-to-all-start.2 = ((f32[16,32,128]{2,1,0:T(8,128)}), f32[16,32,128]{2,1,0:T(8,128)S(1)}, u32[]{:S(2)}, u32[]{:S(2)}) async-start(f32[16,32,128]{2,1,0:T(8,128)} %shard_map.113), calls=%async_computation.2 | async-start | bytes 524288 | tf_op jit(solution)/shard_map/all_to_all | solution.py:393
  13.8 0.1 pad_add_fusion.where
  13.9 0.6 copy-done.2
  14.4 0.0 copy-done.3
  14.5 0.0 copy-done.4
  14.5 0.0 copy-done.5
  14.5 0.1 copy-done.7
  14.6 3.5 %shard_map.114 = (f32[256,256]{1,0:T(8,128)S(1)}, s32[8,256]{1,0:T(8,128)S(1)}, s32[256,128]{1,0:T(8,128)S(1)}, s32[256,128]{1,0:T(8,128)S(1)}, s32[272,128]{1,0...) custom-call(s32[3]{0:T(128)S(1)} %pad_add_fusion.where, ...), custom_call_target="tpu_custom_call" | custom-call | tf_op jit(solution)/shard_map/pallas_call | solution.py:430
  18.0 0.6 slice.3
  18.6 3.8 %all-to-all-done.2 = f32[16,32,128]{2,1,0:T(8,128)S(1)} async-done(((f32[16,32,128]{2,1,0:T(8,128)}), f32[16,32,128]{2,1,0:T(8,128)S(1)}, u32[]{:S(2)}, u32[]{:S(2)}) %all-to-all-start.2) | async-done | bytes 262176 | tf_op jit(solution)/shard_map/all_to_all | solution.py:393
  22.4 0.7 shard_map.115
  23.2 1.3 %collective-permute-start = (bf16[432,128]{1,0:T(8,128)(2,1)S(1)}, bf16[432,128]{1,0:T(8,128)(2,1)S(1)}, u32[]{:S(2)}, u32[]{:S(2)}) collective-permute-start(bf16[432,128]{1,0:T(8,128)(2,1)S(1)} %get-tuple-element.77), channel_id=1, source_target_pairs={{0,1},{1,2},{2,3},{3,4},{4,5},{5,6},{6,7},{7,8},{8,9},{9,10},{10,1... | collective-permute-start | bytes 331784 | tf_op jit(solution)/shard_map/ppermute | solution.py:464
  24.5 1.3 %collective-permute-start.1 = (bf16[432,128]{1,0:T(8,128)(2,1)S(1)}, bf16[432,128]{1,0:T(8,128)(2,1)S(1)}, u32[]{:S(2)}, u32[]{:S(2)}) collective-permute-start(bf16[432,128]{1,0:T(8,128)(2,1)S(1)} %get-tuple-element.78), channel_id=1, source_target_pairs={{1,0},{2,1},{3,2},{4,3},{5,4},{6,5},{7,6},{8,7},{9,8},{10,9},{11,1... | collective-permute-start | bytes 331784 | tf_op jit(solution)/shard_map/ppermute | solution.py:465
  25.8 0.4 shard_map.116
  26.1 0.0 collective-permute-done.left
  26.2 3.9 %collective-permute-done.1.right = bf16[432,128]{1,0:T(8,128)(2,1)S(1)} collective-permute-done((bf16[432,128]{1,0:T(8,128)(2,1)S(1)}, bf16[432,128]{1,0:T(8,128)(2,1)S(1)}, u32[]{:S(2)}, u32[]{:S(2)}) %collective-permute-start.1) | collective-permute-done | bytes 110624 | tf_op jit(solution)/shard_map/ppermute | solution.py:465
  30.1 2.2 %shard_map.117 = (f32[16,24,128]{2,1,0:T(8,128)S(1)}, f32[256,128]{1,0:T(8,128)S(1)}) custom-call(f32[512,128]{1,0:T(8,128)S(1)} %get-tuple-element.76.own, bf16[432,128]{1,0:T(8,128)(2,1)S(1)} %collective-permute-done.left, bf16[432,128]{1,0:T(8,128)(2,1)S(1)} %collective-permute-done.1.right, f32[32,128]{1,0:T(8,128)S(1)} %get-tuple-element.79.sensor, ...), custom_call_target="tpu_custom_call" | custom-call | tf_op jit(solution)/shard_map/pallas_call | solution.py:469
  32.4 13.0 %all_to_all.37.parts = f32[16,24,128]{2,1,0:T(8,128)S(1)} all-to-all(f32[16,24,128]{2,1,0:T(8,128)S(1)} %get-tuple-element.84), channel_id=1, replica_groups=mesh['depth'=16,'tile'=32] {'depth'}, dimensions={0} | all-to-all | bytes 393216 | tf_op jit(solution)/shard_map/all_to_all | solution.py:393
  45.4 0.7 shard_map.118
  46.0 17.2 %all-to-all-start.4 = ((f32[32,8,128]{2,1,0:T(8,128)}), f32[32,8,128]{2,1,0:T(8,128)S(1)}, u32[]{:S(2)}, u32[]{:S(2)}) async-start(f32[32,8,128]{2,1,0:T(8,128)} %shard_map.118), calls=%async_computation.4 | async-start | bytes 262144 | tf_op jit(solution)/shard_map/all_to_all | solution.py:393
  63.2 14.1 %all-to-all-done.4.parts = f32[32,8,128]{2,1,0:T(8,128)S(1)} async-done(((f32[32,8,128]{2,1,0:T(8,128)}), f32[32,8,128]{2,1,0:T(8,128)S(1)}, u32[]{:S(2)}, u32[]{:S(2)}) %all-to-all-start.4) | async-done | bytes 131104 | tf_op jit(solution)/shard_map/all_to_all | solution.py:393
  77.3 1.0 shard_map.119
  78.4 0.4 shard_map.120
  78.7 0.6 while.10
  79.3 0.4 shard_map.121
  79.7 13.8 %all_to_all.38.parts = f32[16,8,128]{2,1,0:T(8,128)S(1)} all-to-all(f32[16,8,128]{2,1,0:T(8,128)S(1)} %get-tuple-element.100), channel_id=1, replica_groups=mesh['depth'=16,'tile'=32] {'depth'}, dimensions={0} | all-to-all | bytes 131072 | tf_op jit(solution)/shard_map/all_to_all | solution.py:393
  93.5 0.1 shard_map.122
  93.6 15.1 %all_to_all.39.parts = f32[32,1,128]{2,1,0:T(1,128)S(1)} all-to-all(f32[32,1,128]{2,1,0:T(1,128)S(1)} %shard_map.122), channel_id=1, replica_groups=mesh['depth'=16,'tile'=32] {'tile'}, dimensions={0} | all-to-all | bytes 32768 | tf_op jit(solution)/shard_map/all_to_all | solution.py:393
  108.6 0.6 shard_map.123
  (15 shorter events, 0.1 us)
Async XLA Ops:
  0.6 0.9 copy-start
  1.5 0.7 copy-start.6
  3.3 10.4 %copy-start.9 = (bf16[1,256,4,128]{3,2,1,0:T(4,128)(2,1)S(1)}, bf16[1,256,4,128]{3,2,1,0:T(4,128)(2,1)}, u32[]{:S(2)}) copy-start(bf16[1,256,4,128]{3,2,1,0:T(4,128)(2,1)} %param.17) | copy-start | bytes 786436
  3.3 19.1 %all-to-all-start.2 = ((f32[16,32,128]{2,1,0:T(8,128)}), f32[16,32,128]{2,1,0:T(8,128)S(1)}, u32[]{:S(2)}, u32[]{:S(2)}) async-start(f32[16,32,128]{2,1,0:T(8,128)} %shard_map.113), calls=%async_computation.2 | async-start | bytes 524288 | tf_op jit(solution)/shard_map/all_to_all | solution.py:393
  13.7 0.8 copy-start.2
  13.7 0.8 copy-start.3
  13.7 0.8 copy-start.4
  13.7 0.8 copy-start.5
  13.8 0.7 copy-start.8
  13.9 0.7 copy-start.7
  14.6 7.9 %copy-start.1 = (f32[32,1024]{1,0:T(8,128)S(1)}, f32[32,1024]{1,0:T(8,128)}, u32[]{:S(2)}) copy-start(f32[32,1024]{1,0:T(8,128)} %measured) | copy-start | bytes 393220
  23.2 3.0 %collective-permute-start = (bf16[432,128]{1,0:T(8,128)(2,1)S(1)}, bf16[432,128]{1,0:T(8,128)(2,1)S(1)}, u32[]{:S(2)}, u32[]{:S(2)}) collective-permute-start(bf16[432,128]{1,0:T(8,128)(2,1)S(1)} %get-tuple-element.77), channel_id=1, source_target_pairs={{0,1},{1,2},{2,3},{3,4},{4,5},{5,6},{6,7},{7,8},{8,9},{9,10},{10,1... | collective-permute-start | bytes 331784 | tf_op jit(solution)/shard_map/ppermute | solution.py:464
  24.5 5.7 %collective-permute-start.1 = (bf16[432,128]{1,0:T(8,128)(2,1)S(1)}, bf16[432,128]{1,0:T(8,128)(2,1)S(1)}, u32[]{:S(2)}, u32[]{:S(2)}) collective-permute-start(bf16[432,128]{1,0:T(8,128)(2,1)S(1)} %get-tuple-element.78), channel_id=1, source_target_pairs={{1,0},{2,1},{3,2},{4,3},{5,4},{6,5},{7,6},{8,7},{9,8},{10,9},{11,1... | collective-permute-start | bytes 331784 | tf_op jit(solution)/shard_map/ppermute | solution.py:465
  46.0 31.3 %all-to-all-start.4 = ((f32[32,8,128]{2,1,0:T(8,128)}), f32[32,8,128]{2,1,0:T(8,128)S(1)}, u32[]{:S(2)}, u32[]{:S(2)}) async-start(f32[32,8,128]{2,1,0:T(8,128)} %shard_map.118), calls=%async_computation.4 | async-start | bytes 262144 | tf_op jit(solution)/shard_map/all_to_all | solution.py:393

commit v6 on v4

--- a/solution.py
+++ b/solution.py
@@ -24,7 +24,8 @@
 ROW = DEPTHS
 BLOCK = 16
 DEEP = 32 * ROW
-CAP = 64
+CAP = 384
+LANES = CAP // CB
 NAMES = SLOTS + 16
 VMEM = pl.BlockSpec(memory_space=pltpu.VMEM)
 SMEM = pl.BlockSpec(memory_space=pltpu.SMEM)
@@ -85,86 +86,106 @@
     names = jnp.concatenate([column_of(neuron[...].astype(F32)), own], axis=0).astype(I32)
     row, col = s_row[...], s_col[...]
     tile, window = row >> 5, col >> 6
-    tables = [tile, window, table >> 7, table & 127]
+    tables = [tile, table >> 7, table & 127]
     tables = jnp.concatenate([x.astype(F32) for x in tables], axis=1).astype(BF16)
     hot = (iota((NAMES, 64), 1) == (names[:, :64] >> 7)).astype(F32).astype(BF16)
     found = jnp.dot(hot, tables, preferred_element_type=F32)
     lane_hot = iota((NAMES, CB), 1) == (names & 127)
-    picked = [lane_sum(jnp.where(lane_hot, found[:, i * CB : (i + 1) * CB], 0.0)) for i in range(4)]
-    n_tile, n_window = picked[0].astype(I32), picked[1].astype(I32)
-    place = jnp.broadcast_to(picked[2] * 128.0 + picked[3], (NAMES, CB))[:SLOTS]
+    picked = [lane_sum(jnp.where(lane_hot, found[:, i * CB : (i + 1) * CB], 0.0)) for i in range(3)]
+    n_tile = picked[0].astype(I32)
+    place = jnp.broadcast_to(picked[1] * 128.0 + picked[2], (NAMES, CB))[:SLOTS]
     place = jnp.where(names[:SLOTS] >= 0, place, -1.0)
     q_col[...] = place.astype(I32)
     q_row[...] = jnp.transpose(place)[0:8, :].astype(I32)
-    keys = (tile * DEPTHS + window) * NEURONS + number
-    low = jnp.broadcast_to((n_tile * DEPTHS + n_window) * NEURONS, (NAMES, CB))
+    keys = tile * NEURONS + number
+    low = jnp.broadcast_to(n_tile * NEURONS, (NAMES, CB))
     high = low + names
     count = jnp.zeros((NAMES, CB), F32)
     for r in range(64):
         key = keys[r : r + 1, :]
         count = count + jnp.where((key >= low) & (key < high), 1.0, 0.0)
     position = jnp.broadcast_to(lane_sum(count), (NAMES, CB)).astype(I32)
-    at = (position // CAP) * 256 + n_tile * 8 + (n_window >> 1)
-    a_row[...] = jnp.where(names >= 0, at, -1)
-    a_lane[...] = (n_window & 1) * CAP + position % CAP
-    local = (tile == where[1]) & (window == where[0])
+    turn = jnp.zeros((NAMES, CB), I32)
+    for i in range(1, (NEURONS + CAP - 1) // CAP):
+        turn = turn + (position >= i * CAP).astype(I32)
+    a_row[...] = jnp.where(names >= 0, turn * TILES + n_tile, -1)
+    a_lane[...] = position - turn * CAP
+    local = tile == where[1]
     mask = local.astype(F32)
     before = (iota((CB, CB), 0) < iota((CB, CB), 1)).astype(F32).astype(BF16)
     inside = jnp.dot(mask.astype(BF16), before, preferred_element_type=F32)
     rows = jnp.broadcast_to(lane_sum(mask), (64, CB)).astype(BF16)
     above = (iota((64, 64), 1) < iota((64, 64), 0)).astype(F32).astype(BF16)
     inside = inside + jnp.dot(above, rows, preferred_element_type=F32)
-    order = jnp.where(local, inside, -1.0).astype(I32)
+    order = jnp.where(local & (window == where[0]), inside, -1.0).astype(I32)
     spot = ((row >> 4) & 1) * WIN + (col & (WIN - 1))
-    coded = ((row & 15) * ROW + s_plane[...]) * CB + spot + 1
+    coded = ((row & 15) * ROW + s_plane[...]) * CB + spot
     rank[...] = order
     code[...] = coded
     first[...] = listed(order, coded, 0)
-    both = jnp.zeros((TILES, DEPTHS), F32)
+    both = jnp.zeros((TILES, 1), F32)
     for r in range(0, 64, 8):
-        tiles = [iota((TILES, CB), 0) == tile[i : i + 1, :] for i in range(r, r + 8)]
-        windows = [iota((DEPTHS, CB), 0) == window[i : i + 1, :] for i in range(r, r + 8)]
-        tiles = jnp.concatenate([x.astype(F32) for x in tiles], axis=1).astype(BF16)
-        windows = jnp.concatenate([x.astype(F32) for x in windows], axis=1).astype(BF16)
-        both = both + lax.dot_general(
-            tiles, windows, (((1,), (1,)), ((), ())), preferred_element_type=F32
+        tiles = jnp.zeros((TILES, CB), F32)
+        for i in range(r, r + 8):
+            tiles = tiles + (iota((TILES, CB), 0) == tile[i : i + 1, :]).astype(F32)
+        both = both + lane_sum(tiles)
+    top = jnp.max(both, axis=0, keepdims=True)
+    most[...] = jnp.broadcast_to(top, (8, CB)).astype(I32)
+
+
+def listed(order, coded, start):
+    place = order - start
+    place = jnp.where(place < CAP, place, -1)
+    total = jnp.zeros((32, CB), F32)
+    for r in range(0, 64, 8):
+        lines = [place[i : i + 1, :] for i in range(r, r + 8)]
+        codes = [coded[i : i + 1, :] for i in range(r, r + 8)]
+        left = []
+        for at, code in zip(lines, codes):
+            here = iota((8, CB), 0) == (at >> 7)
+            left.append(
+                jnp.concatenate(
+                    [
+                        jnp.where(here, (code >> 7).astype(F32), 0.0),
+                        jnp.where(here, (code & 127).astype(F32), 0.0),
+                        jnp.where(here, 1.0, 0.0),
+                        jnp.zeros((8, CB), F32),
+                    ],
+                    axis=0,
+                )
+            )
+        left = jnp.concatenate(left, axis=1).astype(BF16)
+        right = [(iota((CB, CB), 0) == jnp.where(at >= 0, at & 127, -1)).astype(F32) for at in lines]
+        right = jnp.concatenate(right, axis=1).astype(BF16)
+        total = total + lax.dot_general(
+            left, right, (((1,), (1,)), ((), ())), preferred_element_type=F32
         )
-    top = jnp.max(jnp.max(both, axis=0, keepdims=True), axis=1, keepdims=True)
-    most[...] = jnp.broadcast_to(top, (8, CB)).astype(I32)
-
-
-def listed(order, coded, start):
-    result = jnp.zeros((CAP, CB), F32)
-    wanted = iota((CAP, CB), 0) + start
-    for r in range(64):
-        result = result + jnp.where(
-            wanted == order[r : r + 1, :], coded[r : r + 1, :].astype(F32), 0.0
-        )
-    return jnp.broadcast_to(lane_sum(result), (CAP, CB)).astype(I32)
+    value = total[0:8] * 128.0 + total[8:16]
+    return jnp.where(total[16:24] > 0.0, value, -1.0).astype(I32)
 
 
 def seed_values(codes, flat):
-    index = codes - 1
-    key = jnp.concatenate([index, index], axis=1) >> 7
-    hot = (iota((CAP, 256), 1) == key).astype(F32).astype(BF16)
     parts = split3(flat)
-    found = jnp.dot(hot, parts[0], preferred_element_type=F32)
-    found = found + jnp.dot(hot, parts[1], preferred_element_type=F32)
-    found = found + jnp.dot(hot, parts[2], preferred_element_type=F32)
-    value = lane_sum(jnp.where(iota((CAP, CB), 1) == (index & (CB - 1)), found, 0.0))
-    value = jnp.broadcast_to(value, (CAP, CB))
-    return jnp.transpose(jnp.concatenate([value, value], axis=0))[0:1, :]
-
-
-def window_kernel(volume, spread, windows, local, arrived):
-    copy = pltpu.make_async_copy(volume.at[0], local, arrived)
-    copy.start()
+    result = []
+    for i in range(LANES):
+        index = column_of(codes[i : i + 1, :].astype(F32)).astype(I32)
+        key = jnp.concatenate([index, index], axis=1) >> 7
+        hot = (iota((CB, 256), 1) == key).astype(F32).astype(BF16)
+        found = jnp.dot(hot, parts[0], preferred_element_type=F32)
+        found = found + jnp.dot(hot, parts[1], preferred_element_type=F32)
+        found = found + jnp.dot(hot, parts[2], preferred_element_type=F32)
+        picked = jnp.where(iota((CB, CB), 1) == (index & (CB - 1)), found, 0.0)
+        result.append(jnp.sum(jnp.transpose(picked), axis=0, keepdims=True))
+    result.append(jnp.zeros((8 - LANES, CB), F32))
+    return jnp.concatenate(result, axis=0)
+
+
+def window_kernel(volume, spread, windows):
     lane = iota((ROWS, CB), 1)
     taps = jnp.concatenate([spread[0].astype(F32), jnp.zeros((KS, CB - KS), F32)], axis=1)
     taps = jnp.concatenate([pltpu.roll(taps, LIVE, 1), jnp.zeros((ROWS - KS, CB), F32)], axis=0)
     zeros = jnp.zeros((ROWS, CB), F32)
-    copy.wait()
-    padded = jnp.concatenate([zeros, local[...], zeros], axis=1)
+    padded = jnp.concatenate([zeros, volume[0], zeros], axis=1)
     for j in range(DEPTHS):
         start = CB - HALO + WIN * j
         low = start // CB * CB
@@ -282,43 +303,44 @@
     lane = iota((256, CB), 1)
     packed = jnp.where(lane < WIN, pltpu.roll(done[0], CB - HALO, 1), pltpu.roll(done[1], WIN - HALO, 1))
     flat[...] = packed
-    values = jnp.broadcast_to(seed_values(codes[...], packed), (8, CB))
+    values = seed_values(codes[...], packed)
     for p in range(DEPTHS):
         sent[p, 0:16, :] = flat[pl.ds(p, 16, stride=ROW), :]
         sent[p, 16:24, :] = values
 
 
-def more_kernel(start, rank, code, flat, sent):
-    codes = listed(rank[...], code[...], start[0])
-    values = jnp.broadcast_to(seed_values(codes, flat[...]), (8, CB))
+def more_kernel(turn, rank, code, flat, sent):
+    codes = listed(rank[...], code[...], turn[0] * CAP)
+    values = seed_values(codes, flat[...])
     for p in range(DEPTHS):
         sent[p] = values
 
 
 def gather_kernel(at):
     def kernel(parts, out):
-        lane = iota((1, CB), 1)
-        rows = [
-            jnp.where(lane < CAP, parts[2 * m, at : at + 1, :], parts[2 * m + 1, at : at + 1, :])
-            for m in range(8)
-        ]
-        total = jnp.concatenate(rows, axis=0)
+        total = parts[0, at : at + 8, :]
+        for j in range(1, DEPTHS):
+            total = total + parts[j, at : at + 8, :]
+        line = jnp.concatenate([total[i : i + 1, :] for i in range(LANES)], axis=1)
         for j in range(TILES):
-            out[j] = total
+            out[j] = line
 
     return kernel
 
 
-def look_kernel(start, parts, a_row, a_lane, known, out):
+def look_kernel(turn, parts, a_row, a_lane, known, out):
     table = jnp.concatenate([parts[t] for t in range(TILES)], axis=0)
-    row = a_row[...] - start[0] * (256 // CAP)
-    hot = (iota((NAMES, 256), 1) == jnp.concatenate([row, row], axis=1)).astype(F32).astype(BF16)
+    row = a_row[...] - turn[0] * TILES
+    hot = (iota((NAMES, TILES), 1) == row[:, :TILES]).astype(F32).astype(BF16)
     parts = split3(table)
     found = jnp.dot(hot, parts[0], preferred_element_type=F32)
     found = found + jnp.dot(hot, parts[1], preferred_element_type=F32)
     found = found + jnp.dot(hot, parts[2], preferred_element_type=F32)
-    value = lane_sum(jnp.where(iota((NAMES, CB), 1) == a_lane[...], found, 0.0))
-    out[...] = known[...] + jnp.broadcast_to(value, (NAMES, CB))
+    total = jnp.zeros((NAMES, CB), F32)
+    for i in range(LANES):
+        here = iota((NAMES, CB), 1) + i * CB == a_lane[...]
+        total = total + jnp.where(here, found[:, i * CB : (i + 1) * CB], 0.0)
+    out[...] = known[...] + jnp.broadcast_to(lane_sum(total), (NAMES, CB))
 
 
 def home_kernel(parts, weights, b_col, estimate, proj, lines):
@@ -406,14 +428,7 @@
     t = lax.axis_index("tile")
     where = jnp.stack([d, t, (d * TILES + t) * 16]).astype(I32)
     table = owner_slot.reshape(64, CB)
-    [windows] = pl.pallas_call(
-        window_kernel,
-        out_shape=[jax.ShapeDtypeStruct((DEPTHS, ROWS, CB), F32)],
-        in_specs=[pl.BlockSpec(memory_space=pl.ANY), VMEM],
-        out_specs=[VMEM],
-        scratch_shapes=[pltpu.VMEM((ROWS, COLS), F32), pltpu.SemaphoreType.DMA],
-        compiler_params=pltpu.CompilerParams(vmem_limit_bytes=24 * 2**20),
-    )(volume, point_spread)
+    [windows] = call(window_kernel, [((DEPTHS, ROWS, CB), F32)], 2)(volume, point_spread)
     parts = swap(windows, "depth").reshape(DEPTHS * ROWS, CB)
     message = ((HALO * ROW + 2 * HALO, CB), BF16)
     own, sensor, down, up = call(
@@ -443,7 +458,7 @@
             names,
             square,
             square,
-            ((CAP, CB), I32),
+            ((8, CB), I32),
             ((8, CB), I32),
         ],
         8,
@@ -476,20 +491,20 @@
     parts = swap(sent, "depth")
 
     def share(values, at):
-        [values] = call(gather_kernel(at), [((TILES, 8, CB), F32)], 1)(values)
+        [values] = call(gather_kernel(at), [((TILES, 1, CAP), F32)], 1)(values)
         return swap(values, "tile")
 
-    def look(begin, values, known):
+    def look(turn, values, known):
         return call(look_kernel, [((NAMES, CB), F32)], 5, scalars=(0,))(
-            begin, values, a_row, a_lane, known
+            turn, values, a_row, a_lane, known
         )[0]
 
     def another(step, known):
-        begin = jnp.reshape(step * CAP, (1,))
+        turn = jnp.reshape(step, (1,))
         [values] = call(more_kernel, [((DEPTHS, 8, CB), F32)], 4, scalars=(0,))(
-            begin, rank, code, flat
+            turn, rank, code, flat
         )
-        return look(begin, share(swap(values, "depth"), 0), known)
+        return look(turn, share(swap(values, "depth"), 0), known)
 
     known = look(jnp.zeros((1,), I32), share(parts, 16), jnp.zeros((NAMES, CB), F32))
     known = lax.fori_loop(1, (most[0, 0] + CAP - 1) // CAP, another, known)

time: 108 us -> 106 us (0.981)
  blocking collectives: 40.9 us -> 39.1 us
  waiting for transfers between devices: 20.5 us -> 18.8 us
    all_to_all x3, blocking collectives: 40.9 us -> 39.1 us  [swap(): return lax.all_to_all(pieces, axis, 0, 0)]
    all_to_all x2, waiting for transfers between devices: 20.5 us -> 18.8 us  [swap(): return lax.all_to_all(pieces, axis, 0, 0)]
where the time goes in v6:
time: 106 us; the launch traced here: 105 us
  blocking collectives  39.1 us (37%)
  starting transfers between devices  31.2 us (29%)
  waiting for transfers between devices  18.8 us (18%)
  Pallas kernels  11.1 us (10%)
  local copies, waits for them, and re-layouts  3.4 us (3%)
  between operations  1.48 us (1%)
    all_to_all x3, blocking collectives, swap(): return lax.all_to_all(pieces, axis, 0, 0)  39.1 us
    all_to_all x2, starting transfers between devices, swap(): return lax.all_to_all(pieces, axis, 0, 0)  28.6 us
    all_to_all x2, waiting for transfers between devices, swap(): return lax.all_to_all(pieces, axis, 0, 0)  18.8 us
    pallas_call x1, Pallas kernels, body(): call(prepare_kernel, [((SLOTS, SLOTS), F32), ((8, SLOTS), I32), column, c...  4.01 us
    pallas_call x1, Pallas kernels, body(): call(iterate_kernel, [((DEPTHS, 24, CB), F32), ((256, CB), F32)], 8, scra...  2.4 us
    unnamed x21, local copies, waits for them, and re-layouts  2.35 us
  transfers between devices with their start and end apart: 4, of which 2 were waited for; matrix products, arithmetic and copies ran while one was open for 1% of the time, Pallas kernels for 5%

profile of v6, /device:TPU:1, one launch (start us, length us, event | category | flops | bytes accessed | tf_op | source)
XLA Modules:
  0.0 105.2 jit_solution(8481543883520150508)
XLA Ops:
  0.6 0.9 copy-done
  1.5 0.7 copy-done.6
  2.2 0.9 shard_map.113
  3.1 10.3 %all-to-all-start.2 = ((f32[16,32,128]{2,1,0:T(8,128)}), f32[16,32,128]{2,1,0:T(8,128)S(1)}, u32[]{:S(2)}, u32[]{:S(2)}) async-start(f32[16,32,128]{2,1,0:T(8,128)} %shard_map.113), calls=%async_computation.2 | async-start | bytes 524288 | tf_op jit(solution)/shard_map/all_to_all | solution.py:412
  13.4 0.1 pad_add_fusion.where
  13.5 8.7 %all-to-all-done.2 = f32[16,32,128]{2,1,0:T(8,128)S(1)} async-done(((f32[16,32,128]{2,1,0:T(8,128)}), f32[16,32,128]{2,1,0:T(8,128)S(1)}, u32[]{:S(2)}, u32[]{:S(2)}) %all-to-all-start.2) | async-done | bytes 262176 | tf_op jit(solution)/shard_map/all_to_all | solution.py:412
  22.2 0.7 shard_map.114
  22.9 1.3 %collective-permute-start = (bf16[432,128]{1,0:T(8,128)(2,1)S(1)}, bf16[432,128]{1,0:T(8,128)(2,1)S(1)}, u32[]{:S(2)}, u32[]{:S(2)}) collective-permute-start(bf16[432,128]{1,0:T(8,128)(2,1)S(1)} %get-tuple-element.69), channel_id=1, source_target_pairs={{0,1},{1,2},{2,3},{3,4},{4,5},{5,6},{6,7},{7,8},{8,9},{9,10},{10,1... | collective-permute-start | bytes 331784 | tf_op jit(solution)/shard_map/ppermute | solution.py:441
  24.2 1.3 %collective-permute-start.1 = (bf16[432,128]{1,0:T(8,128)(2,1)S(1)}, bf16[432,128]{1,0:T(8,128)(2,1)S(1)}, u32[]{:S(2)}, u32[]{:S(2)}) collective-permute-start(bf16[432,128]{1,0:T(8,128)(2,1)S(1)} %get-tuple-element.70), channel_id=1, source_target_pairs={{1,0},{2,1},{3,2},{4,3},{5,4},{6,5},{7,6},{8,7},{9,8},{10,9},{11,1... | collective-permute-start | bytes 331784 | tf_op jit(solution)/shard_map/ppermute | solution.py:442
  25.5 0.0 copy-start.2
  25.5 0.0 copy-start.3
  25.5 0.0 copy-start.4
  25.6 0.6 copy-done.2
  26.3 0.0 copy-done.3
  26.3 0.0 copy-done.4
  26.3 0.0 copy-done.5
  26.3 4.0 %shard_map.116 = (f32[256,256]{1,0:T(8,128)S(1)}, s32[8,256]{1,0:T(8,128)S(1)}, s32[256,128]{1,0:T(8,128)S(1)}, s32[256,128]{1,0:T(8,128)S(1)}, s32[272,128]{1,0...) custom-call(s32[3]{0:T(128)S(1)} %pad_add_fusion.where, ...), custom_call_target="tpu_custom_call" | custom-call | tf_op jit(solution)/shard_map/pallas_call | solution.py:450
  30.3 0.4 shard_map.115
  30.8 2.4 %shard_map.117 = (f32[16,24,128]{2,1,0:T(8,128)S(1)}, f32[256,128]{1,0:T(8,128)S(1)}) custom-call(f32[512,128]{1,0:T(8,128)S(1)} %get-tuple-element.68.own, bf16[432,128]{1,0:T(8,128)(2,1)S(1)} %collective-permute-done.left, bf16[432,128]{1,0:T(8,128)(2,1)S(1)} %collective-permute-done.1.right, f32[32,128]{1,0:T(8,128)S(1)} %get-tuple-element.71.sensor, ...), custom_call_target="tpu_custom_call" | custom-call | tf_op jit(solution)/shard_map/pallas_call | solution.py:476
  33.2 12.1 %all_to_all.37.parts = f32[16,24,128]{2,1,0:T(8,128)S(1)} all-to-all(f32[16,24,128]{2,1,0:T(8,128)S(1)} %get-tuple-element.76), channel_id=1, replica_groups=mesh['depth'=16,'tile'=32] {'depth'}, dimensions={0} | all-to-all | bytes 393216 | tf_op jit(solution)/shard_map/all_to_all | solution.py:412
  45.3 0.7 shard_map.119
  45.9 18.3 %all-to-all-start.4 = ((f32[32,1,384]{2,1,0:T(1,128)}), f32[32,1,384]{2,1,0:T(1,128)S(1)}, u32[]{:S(2)}, u32[]{:S(2)}) async-start(f32[32,1,384]{2,1,0:T(1,128)} %shard_map.119), calls=%async_computation.4 | async-start | bytes 98304 | tf_op jit(solution)/shard_map/all_to_all | solution.py:412
  64.2 0.5 slice.6
  65.4 1.0 shard_map.118
  66.4 10.2 %all-to-all-done.4.parts = f32[32,1,384]{2,1,0:T(1,128)S(1)} async-done(((f32[32,1,384]{2,1,0:T(1,128)}), f32[32,1,384]{2,1,0:T(1,128)S(1)}, u32[]{:S(2)}, u32[]{:S(2)}) %all-to-all-start.4) | async-done | bytes 49184 | tf_op jit(solution)/shard_map/all_to_all | solution.py:412
  76.6 0.5 shard_map.120
  77.1 0.4 shard_map.121
  77.5 12.0 %all_to_all.38.parts = f32[16,8,128]{2,1,0:T(8,128)S(1)} all-to-all(f32[16,8,128]{2,1,0:T(8,128)S(1)} %get-tuple-element.90), channel_id=1, replica_groups=mesh['depth'=16,'tile'=32] {'depth'}, dimensions={0} | all-to-all | bytes 131072 | tf_op jit(solution)/shard_map/all_to_all | solution.py:412
  89.5 0.1 shard_map.122
  89.6 15.0 %all_to_all.39.parts = f32[32,1,128]{2,1,0:T(1,128)S(1)} all-to-all(f32[32,1,128]{2,1,0:T(1,128)S(1)} %shard_map.122), channel_id=1, replica_groups=mesh['depth'=16,'tile'=32] {'tile'}, dimensions={0} | all-to-all | bytes 32768 | tf_op jit(solution)/shard_map/all_to_all | solution.py:412
  104.6 0.1 shard_map.123
  104.7 0.5 slice_bitcast_fusion
  (16 shorter events, 0.1 us)
Async XLA Ops:
  0.6 0.9 copy-start
  1.5 0.7 copy-start.6
  3.1 19.1 %copy-start.1 = (f32[32,1024]{1,0:T(8,128)S(1)}, f32[32,1024]{1,0:T(8,128)}, u32[]{:S(2)}) copy-start(f32[32,1024]{1,0:T(8,128)} %measured.1) | copy-start | bytes 393220
  3.1 19.1 %all-to-all-start.2 = ((f32[16,32,128]{2,1,0:T(8,128)}), f32[16,32,128]{2,1,0:T(8,128)S(1)}, u32[]{:S(2)}, u32[]{:S(2)}) async-start(f32[16,32,128]{2,1,0:T(8,128)} %shard_map.113), calls=%async_computation.2 | async-start | bytes 524288 | tf_op jit(solution)/shard_map/all_to_all | solution.py:412
  13.4 12.1 %copy-start.9 = (bf16[1,256,4,128]{3,2,1,0:T(4,128)(2,1)S(1)}, bf16[1,256,4,128]{3,2,1,0:T(4,128)(2,1)}, u32[]{:S(2)}) copy-start(bf16[1,256,4,128]{3,2,1,0:T(4,128)(2,1)} %param.17) | copy-start | bytes 786436
  22.9 7.9 %collective-permute-start = (bf16[432,128]{1,0:T(8,128)(2,1)S(1)}, bf16[432,128]{1,0:T(8,128)(2,1)S(1)}, u32[]{:S(2)}, u32[]{:S(2)}) collective-permute-start(bf16[432,128]{1,0:T(8,128)(2,1)S(1)} %get-tuple-element.69), channel_id=1, source_target_pairs={{0,1},{1,2},{2,3},{3,4},{4,5},{5,6},{6,7},{7,8},{8,9},{9,10},{10,1... | collective-permute-start | bytes 331784 | tf_op jit(solution)/shard_map/ppermute | solution.py:441
  24.2 6.6 %collective-permute-start.1 = (bf16[432,128]{1,0:T(8,128)(2,1)S(1)}, bf16[432,128]{1,0:T(8,128)(2,1)S(1)}, u32[]{:S(2)}, u32[]{:S(2)}) collective-permute-start(bf16[432,128]{1,0:T(8,128)(2,1)S(1)} %get-tuple-element.70), channel_id=1, source_target_pairs={{1,0},{2,1},{3,2},{4,3},{5,4},{6,5},{7,6},{8,7},{9,8},{10,9},{11,1... | collective-permute-start | bytes 331784 | tf_op jit(solution)/shard_map/ppermute | solution.py:442
  25.5 0.8 copy-start.2
  25.5 0.8 copy-start.3
  25.5 0.8 copy-start.4
  25.5 0.8 copy-start.5
  25.6 0.8 copy-start.8
  25.6 0.7 copy-start.7
  45.9 30.7 %all-to-all-start.4 = ((f32[32,1,384]{2,1,0:T(1,128)}), f32[32,1,384]{2,1,0:T(1,128)S(1)}, u32[]{:S(2)}, u32[]{:S(2)}) async-start(f32[32,1,384]{2,1,0:T(1,128)} %shard_map.119), calls=%async_computation.4 | async-start | bytes 98304 | tf_op jit(solution)/shard_map/all_to_all | solution.py:412

commit v7 on v6

--- a/solution.py
+++ b/solution.py
@@ -97,14 +97,23 @@
     place = jnp.where(names[:SLOTS] >= 0, place, -1.0)
     q_col[...] = place.astype(I32)
     q_row[...] = jnp.transpose(place)[0:8, :].astype(I32)
+    both = jnp.zeros((TILES, 1), F32)
+    for r in range(0, 64, 8):
+        tiles = jnp.zeros((TILES, CB), F32)
+        for i in range(r, r + 8):
+            tiles = tiles + (iota((TILES, CB), 0) == tile[i : i + 1, :]).astype(F32)
+        both = both + lane_sum(tiles)
+    top = jnp.max(both, axis=0, keepdims=True)
+    most[...] = jnp.broadcast_to(top, (8, CB)).astype(I32)
+    wide = jnp.concatenate([both, jnp.zeros((CB - TILES, 1), F32)], axis=0)
+    held = jnp.transpose(jnp.broadcast_to(wide, (CB, CB)))[0:1, :]
+    earlier = lane_sum(jnp.where(iota((NAMES, CB), 1) < n_tile, held, 0.0))
     keys = tile * NEURONS + number
-    low = jnp.broadcast_to(n_tile * NEURONS, (NAMES, CB))
-    high = low + names
+    high = jnp.broadcast_to(n_tile * NEURONS, (NAMES, CB)) + names
     count = jnp.zeros((NAMES, CB), F32)
     for r in range(64):
-        key = keys[r : r + 1, :]
-        count = count + jnp.where((key >= low) & (key < high), 1.0, 0.0)
-    position = jnp.broadcast_to(lane_sum(count), (NAMES, CB)).astype(I32)
+        count = count + jnp.where(keys[r : r + 1, :] < high, 1.0, 0.0)
+    position = jnp.broadcast_to(lane_sum(count) - earlier, (NAMES, CB)).astype(I32)
     turn = jnp.zeros((NAMES, CB), I32)
     for i in range(1, (NEURONS + CAP - 1) // CAP):
         turn = turn + (position >= i * CAP).astype(I32)
@@ -123,14 +132,6 @@
     rank[...] = order
     code[...] = coded
     first[...] = listed(order, coded, 0)
-    both = jnp.zeros((TILES, 1), F32)
-    for r in range(0, 64, 8):
-        tiles = jnp.zeros((TILES, CB), F32)
-        for i in range(r, r + 8):
-            tiles = tiles + (iota((TILES, CB), 0) == tile[i : i + 1, :]).astype(F32)
-        both = both + lane_sum(tiles)
-    top = jnp.max(both, axis=0, keepdims=True)
-    most[...] = jnp.broadcast_to(top, (8, CB)).astype(I32)
 
 
 def listed(order, coded, start):
@@ -263,43 +264,51 @@
     light[HALO : HALO + ROWS, :] = sensor[...]
     light[HALO + ROWS : 2 * HALO + ROWS, :] = after[:HALO] + after[HALO:]
     light[2 * HALO + ROWS :, :] = jnp.zeros((16, CB), F32)
-    for m in range(4):
-        stack[m * DEEP + KS * 32 : (m + 1) * DEEP, :] = jnp.zeros((DEEP - KS * 32, CB), BF16)
+    for m in range(2):
+        stack[m * DEEP + KS * 32 : (m + 1) * DEEP, :] = jnp.zeros((DEEP - KS * 32, 2 * CB), BF16)
     tall = jnp.concatenate([scale[...]] * BLOCK, axis=0)
 
     def divide(source, blocks, offset, valid):
-        for m in range(blocks):
-            sums[...] = jnp.dot(
-                ahead[...], source[m * 256 : m * 256 + DEEP, :], preferred_element_type=F32
-            )
-            total = lane_shift(sums[pl.ds(0, BLOCK, stride=16), :], 0)
-            for b in range(1, KS):
-                total = total + lane_shift(sums[pl.ds(b, BLOCK, stride=16), :], b)
-            seen = light[m * BLOCK + offset : (m + 1) * BLOCK + offset, :]
-            inside = (iota((BLOCK, CB), 0) < valid - m * BLOCK) & (seen != 0.0) & (total != 0.0)
-            value = jnp.where(inside, seen / jnp.where(inside, total, 1.0), 0.0)
-            ratio[m * BLOCK : (m + 1) * BLOCK, :] = value
+        for m in range(0, blocks, 2):
+            pair = range(m, min(m + 2, blocks))
+            right = jnp.concatenate([source[i * 256 : i * 256 + DEEP, :] for i in pair], axis=1)
+            value = jnp.dot(ahead[...], right, preferred_element_type=F32)
+            for i in pair:
+                at = (i - m) * CB
+                sums[i - m] = value[:, at : at + CB]
+            for i in pair:
+                total = lane_shift(sums[i - m, pl.ds(0, BLOCK, stride=16), :], 0)
+                for b in range(1, KS):
+                    total = total + lane_shift(sums[i - m, pl.ds(b, BLOCK, stride=16), :], b)
+                seen = light[i * BLOCK + offset : (i + 1) * BLOCK + offset, :]
+                inside = (iota((BLOCK, CB), 0) < valid - i * BLOCK) & (seen != 0.0) & (total != 0.0)
+                ratio[i * BLOCK : (i + 1) * BLOCK, :] = jnp.where(
+                    inside, seen / jnp.where(inside, total, 1.0), 0.0
+                )
 
     def spread_back(blocks):
         height = 16 * blocks + 16
         for b in range(KS):
             moved = lane_shift(ratio[:height, :], b).astype(BF16)
             for m in range(blocks):
-                stack[m * DEEP + b * 32 : m * DEEP + (b + 1) * 32, :] = moved[m * 16 : m * 16 + 32]
+                at = (m // 2) * DEEP + b * 32
+                stack[at : at + 32, (m % 2) * CB : (m % 2 + 1) * CB] = moved[m * 16 : m * 16 + 32]
 
     def back(m):
         value = jnp.dot(behind[...], stack[m * DEEP : (m + 1) * DEEP, :], preferred_element_type=F32)
-        return value * tall
+        return value[:, :CB] * tall, value[:, CB:] * tall
 
     divide(rounded, 5, 6, 68)
     spread_back(4)
+    factors = back(0) + back(1)
     for m in range(4):
-        value = exact[(m * 16 + 12) * ROW : (m * 16 + 28) * ROW, :] * back(m)
+        value = exact[(m * 16 + 12) * ROW : (m * 16 + 28) * ROW, :] * factors[m]
         first[m * 256 : (m + 1) * 256, :] = value
         second[m * 256 : (m + 1) * 256, :] = value.astype(BF16)
     divide(second, 3, 18, 44)
     spread_back(2)
-    done = [first[(m * 16 + 12) * ROW : (m * 16 + 28) * ROW, :] * back(m) for m in range(2)]
+    factors = back(0)
+    done = [first[(m * 16 + 12) * ROW : (m * 16 + 28) * ROW, :] * factors[m] for m in range(2)]
     lane = iota((256, CB), 1)
     packed = jnp.where(lane < WIN, pltpu.roll(done[0], CB - HALO, 1), pltpu.roll(done[1], WIN - HALO, 1))
     flat[...] = packed
@@ -328,9 +337,9 @@
     return kernel
 
 
-def look_kernel(turn, parts, a_row, a_lane, known, out):
+def looked(turn, parts, a_row, a_lane):
     table = jnp.concatenate([parts[t] for t in range(TILES)], axis=0)
-    row = a_row[...] - turn[0] * TILES
+    row = a_row[...] - turn * TILES
     hot = (iota((NAMES, TILES), 1) == row[:, :TILES]).astype(F32).astype(BF16)
     parts = split3(table)
     found = jnp.dot(hot, parts[0], preferred_element_type=F32)
@@ -340,7 +349,11 @@
     for i in range(LANES):
         here = iota((NAMES, CB), 1) + i * CB == a_lane[...]
         total = total + jnp.where(here, found[:, i * CB : (i + 1) * CB], 0.0)
-    out[...] = known[...] + jnp.broadcast_to(lane_sum(total), (NAMES, CB))
+    return jnp.broadcast_to(lane_sum(total), (NAMES, CB))
+
+
+def look_kernel(turn, parts, a_row, a_lane, known, out):
+    out[...] = known[...] + looked(turn[0], parts, a_row, a_lane)
 
 
 def home_kernel(parts, weights, b_col, estimate, proj, lines):
@@ -367,8 +380,9 @@
     proj[...] = jnp.broadcast_to(jnp.sum(total, axis=1, keepdims=True), (SLOTS, CB))
 
 
-def slots_kernel(start, gram, q_row, q_col, proj, out, own):
-    padded = jnp.concatenate([start[...], jnp.zeros((3 * CB - NAMES, CB), F32)], axis=0)
+def slots_kernel(parts, a_row, a_lane, known, gram, q_row, q_col, proj, out, own):
+    start = known[...] + looked(0, parts, a_row, a_lane)
+    padded = jnp.concatenate([start, jnp.zeros((3 * CB - NAMES, CB), F32)], axis=0)
     row = jnp.transpose(padded)[0:1, :]
     own[...] = row[:, SLOTS:]
     start_row = row[:, :SLOTS]
@@ -427,9 +441,14 @@
     d = lax.axis_index("depth")
     t = lax.axis_index("tile")
     where = jnp.stack([d, t, (d * TILES + t) * 16]).astype(I32)
+    [windows] = call(window_kernel, [((DEPTHS, ROWS, CB), F32)], 2)(volume, point_spread)
+    windows, where = lax.optimization_barrier((windows, where))
+    tied = (swap(windows, "depth"), where, measured, entry_block, entry_neuron, footprints, owner_slot)
+    tied = lax.optimization_barrier(tied + (seed_plane, seed_row, seed_col))
+    parts, where, measured, entry_block, entry_neuron, footprints, owner_slot = tied[:7]
+    seed_plane, seed_row, seed_col = tied[7:]
+    parts = parts.reshape(DEPTHS * ROWS, CB)
     table = owner_slot.reshape(64, CB)
-    [windows] = call(window_kernel, [((DEPTHS, ROWS, CB), F32)], 2)(volume, point_spread)
-    parts = swap(windows, "depth").reshape(DEPTHS * ROWS, CB)
     message = ((HALO * ROW + 2 * HALO, CB), BF16)
     own, sensor, down, up = call(
         arrange_kernel,
@@ -483,12 +502,12 @@
             pltpu.VMEM((64 * ROW, CB), F32),
             pltpu.VMEM((64 * ROW, CB), BF16),
             pltpu.VMEM((96, CB), F32),
-            pltpu.VMEM((256, CB), F32),
+            pltpu.VMEM((2, 256, CB), F32),
             pltpu.VMEM((80, CB), F32),
-            pltpu.VMEM((4 * DEEP, CB), BF16),
+            pltpu.VMEM((2 * DEEP, 2 * CB), BF16),
         ],
     )(own, left, right, sensor, ahead, behind, scale, first)
-    parts = swap(sent, "depth")
+    parts, most = lax.optimization_barrier((swap(sent, "depth"), most))
 
     def share(values, at):
         [values] = call(gather_kernel(at), [((TILES, 1, CAP), F32)], 1)(values)
@@ -506,16 +525,17 @@
         )
         return look(turn, share(swap(values, "depth"), 0), known)
 
-    known = look(jnp.zeros((1,), I32), share(parts, 16), jnp.zeros((NAMES, CB), F32))
-    known = lax.fori_loop(1, (most[0, 0] + CAP - 1) // CAP, another, known)
+    rounds = (most[0, 0] + CAP - 1) // CAP
+    shared, none = lax.optimization_barrier((share(parts, 16), jnp.zeros((NAMES, CB), F32)))
+    known = lax.fori_loop(1, rounds, another, none)
     estimate, proj = call(
         home_kernel,
         [((ROWS, COLS), F32), ((SLOTS, CB), F32)],
         3,
         scratch=[pltpu.VMEM((NCB * ROWS, CB), F32)],
     )(parts, weights, b_col)
-    sent, own = call(slots_kernel, [((DEPTHS, 8, CB), F32), ((1, CB), F32)], 5)(
-        known, gram, q_row, q_col, proj
+    sent, own = call(slots_kernel, [((DEPTHS, 8, CB), F32), ((1, CB), F32)], 8)(
+        shared, a_row, a_lane, known, gram, q_row, q_col, proj
     )
     [sent] = call(fold_kernel, [((TILES, 1, CB), F32)], 1)(swap(sent, "depth"))
     [demixed] = call(final_kernel, [((1, CB), F32)], 2)(swap(sent, "tile"), own)

time: 106 us -> 104 us (0.981)
  blocking collectives: 39.1 us -> 58.3 us
  starting transfers between devices: 31.2 us -> 20 us
  waiting for transfers between devices: 18.8 us -> 10.9 us
  Pallas kernels: 11.1 us -> 9.26 us
    all_to_all x3 -> x4, blocking collectives: 39.1 us -> 58.3 us  [swap(): return lax.all_to_all(pieces, axis, 0, 0)]
    all_to_all x2 -> x1, starting transfers between devices: 28.6 us -> 17.4 us  [swap(): return lax.all_to_all(pieces, axis, 0, 0)]
    all_to_all x2 -> x1, waiting for transfers between devices: 18.8 us -> 10.2 us  [swap(): return lax.all_to_all(pieces, axis, 0, 0)]
  transfers between devices with their start and end apart: 4 -> 3, of which waited for: 2 -> 2; matrix products, arithmetic and copies ran while one was open for 1% -> 1% of each run, Pallas kernels for 5% -> 4%
where the time goes in v7:
time: 104 us; the launch traced here: 103 us
  blocking collectives  58.3 us (56%)
  starting transfers between devices  20 us (19%)
  waiting for transfers between devices  10.9 us (10%)
  Pallas kernels  9.26 us (9%)
  local copies, waits for them, and re-layouts  3.39 us (3%)
  between operations  1.47 us (1%)
    all_to_all x4, blocking collectives, swap(): return lax.all_to_all(pieces, axis, 0, 0)  58.3 us
    all_to_all x1, starting transfers between devices, swap(): return lax.all_to_all(pieces, axis, 0, 0)  17.4 us
    all_to_all x1, waiting for transfers between devices, swap(): return lax.all_to_all(pieces, axis, 0, 0)  10.2 us
    pallas_call x1, Pallas kernels, body(): call(prepare_kernel, [((SLOTS, SLOTS), F32), ((8, SLOTS), I32), column, c...  3.08 us
    unnamed x21, local copies, waits for them, and re-layouts  2.35 us
    pallas_call x1, Pallas kernels, body(): call(iterate_kernel, [((DEPTHS, 24, CB), F32), ((256, CB), F32)], 8, scra...  2.27 us
  transfers between devices with their start and end apart: 3, of which 2 were waited for; matrix products, arithmetic and copies ran while one was open for 1% of the time, Pallas kernels for 4%

profile of v7, /device:TPU:1, one launch (start us, length us, event | category | flops | bytes accessed | tf_op | source)
XLA Modules:
  0.0 103.4 jit_solution(14106780220681759018)
XLA Ops:
  0.7 0.7 copy-done.6
  1.3 0.9 copy-done
  2.2 0.1 shard_map.113
  2.4 0.1 pad_add_fusion.where
  2.5 18.2 %all_to_all.37 = f32[16,32,128]{2,1,0:T(8,128)S(1)} all-to-all(f32[16,32,128]{2,1,0:T(8,128)S(1)} %shard_map.113), channel_id=1, replica_groups=mesh['depth'=16,'tile'=32] {'depth'}, dimensions={0} | all-to-all | bytes 524288 | tf_op jit(solution)/shard_map/all_to_all | solution.py:426
  20.6 0.7 shard_map.114
  21.4 1.3 %collective-permute-start = (bf16[432,128]{1,0:T(8,128)(2,1)S(1)}, bf16[432,128]{1,0:T(8,128)(2,1)S(1)}, u32[]{:S(2)}, u32[]{:S(2)}) collective-permute-start(bf16[432,128]{1,0:T(8,128)(2,1)S(1)} %get-tuple-element.90), channel_id=1, source_target_pairs={{0,1},{1,2},{2,3},{3,4},{4,5},{5,6},{6,7},{7,8},{8,9},{9,10},{10,1... | collective-permute-start | bytes 331784 | tf_op jit(solution)/shard_map/ppermute | solution.py:460
  22.7 1.3 %collective-permute-start.1 = (bf16[432,128]{1,0:T(8,128)(2,1)S(1)}, bf16[432,128]{1,0:T(8,128)(2,1)S(1)}, u32[]{:S(2)}, u32[]{:S(2)}) collective-permute-start(bf16[432,128]{1,0:T(8,128)(2,1)S(1)} %get-tuple-element.91), channel_id=1, source_target_pairs={{1,0},{2,1},{3,2},{4,3},{5,4},{6,5},{7,6},{8,7},{9,8},{10,9},{11,1... | collective-permute-start | bytes 331784 | tf_op jit(solution)/shard_map/ppermute | solution.py:461
  24.0 0.4 shard_map.115
  24.4 0.0 copy-start.3
  24.4 0.0 copy-start.4
  24.4 0.0 copy-start.8
  24.5 0.6 copy-done.2
  25.1 0.0 copy-done.3
  25.1 0.0 copy-done.4
  25.1 0.0 copy-done.5
  25.2 3.1 %shard_map.116 = (f32[256,256]{1,0:T(8,128)S(1)}, s32[8,256]{1,0:T(8,128)S(1)}, s32[256,128]{1,0:T(8,128)S(1)}, s32[256,128]{1,0:T(8,128)S(1)}, s32[272,128]{1,0...) custom-call(s32[3]{0:T(128)S(1)} %pad_add_fusion.where, ...), custom_call_target="tpu_custom_call" | custom-call | tf_op jit(solution)/shard_map/pallas_call | solution.py:469
  28.3 0.0 collective-permute-done.left
  28.3 0.7 collective-permute-done.1.right
  29.0 2.3 %shard_map.117 = (f32[16,24,128]{2,1,0:T(8,128)S(1)}, f32[256,128]{1,0:T(8,128)S(1)}) custom-call(f32[512,128]{1,0:T(8,128)S(1)} %get-tuple-element.89.own, bf16[432,128]{1,0:T(8,128)(2,1)S(1)} %collective-permute-done.left, bf16[432,128]{1,0:T(8,128)(2,1)S(1)} %collective-permute-done.1.right, f32[32,128]{1,0:T(8,128)S(1)} %get-tuple-element.92.sensor, ...), custom_call_target="tpu_custom_call" | custom-call | tf_op jit(solution)/shard_map/pallas_call | solution.py:495
  31.3 13.0 %all_to_all.38.parts = f32[16,24,128]{2,1,0:T(8,128)S(1)} all-to-all(f32[16,24,128]{2,1,0:T(8,128)S(1)} %get-tuple-element.104), channel_id=1, replica_groups=mesh['depth'=16,'tile'=32] {'depth'}, dimensions={0} | all-to-all | bytes 393216 | tf_op jit(solution)/shard_map/all_to_all | solution.py:426
  44.3 0.6 shard_map.119
  44.9 17.4 %all-to-all-start.4 = ((f32[32,1,384]{2,1,0:T(1,128)}), f32[32,1,384]{2,1,0:T(1,128)S(1)}, u32[]{:S(2)}, u32[]{:S(2)}) async-start(f32[32,1,384]{2,1,0:T(1,128)} %shard_map.119), calls=%async_computation.4 | async-start | bytes 98304 | tf_op jit(solution)/shard_map/all_to_all | solution.py:426
  62.3 0.5 slice.6
  63.5 1.0 shard_map.118
  64.5 10.2 %all-to-all-done.4.parts = f32[32,1,384]{2,1,0:T(1,128)S(1)} async-done(((f32[32,1,384]{2,1,0:T(1,128)}), f32[32,1,384]{2,1,0:T(1,128)S(1)}, u32[]{:S(2)}, u32[]{:S(2)}) %all-to-all-start.4) | async-done | bytes 49184 | tf_op jit(solution)/shard_map/all_to_all | solution.py:426
  74.7 0.8 shard_map.120
  75.5 12.1 %all_to_all.39.parts = f32[16,8,128]{2,1,0:T(8,128)S(1)} all-to-all(f32[16,8,128]{2,1,0:T(8,128)S(1)} %get-tuple-element.122), channel_id=1, replica_groups=mesh['depth'=16,'tile'=32] {'depth'}, dimensions={0} | all-to-all | bytes 131072 | tf_op jit(solution)/shard_map/all_to_all | solution.py:426
  87.6 0.1 shard_map.121
  87.7 15.0 %all_to_all.40.parts = f32[32,1,128]{2,1,0:T(1,128)S(1)} all-to-all(f32[32,1,128]{2,1,0:T(1,128)S(1)} %shard_map.121), channel_id=1, replica_groups=mesh['depth'=16,'tile'=32] {'tile'}, dimensions={0} | all-to-all | bytes 32768 | tf_op jit(solution)/shard_map/all_to_all | solution.py:426
  102.7 0.1 shard_map.122
  102.8 0.5 slice_bitcast_fusion
  (14 shorter events, 0.1 us)
Async XLA Ops:
  0.6 0.7 copy-start.6
  1.3 0.9 copy-start
  2.5 18.2 %copy-start.1 = (f32[32,1024]{1,0:T(8,128)S(1)}, f32[32,1024]{1,0:T(8,128)}, u32[]{:S(2)}) copy-start(f32[32,1024]{1,0:T(8,128)} %measured) | copy-start | bytes 393220
  20.6 3.7 %copy-start.9 = (bf16[1,256,4,128]{3,2,1,0:T(4,128)(2,1)S(1)}, bf16[1,256,4,128]{3,2,1,0:T(4,128)(2,1)}, u32[]{:S(2)}) copy-start(bf16[1,256,4,128]{3,2,1,0:T(4,128)(2,1)} %param.17) | copy-start | bytes 786436
  21.4 6.9 %collective-permute-start = (bf16[432,128]{1,0:T(8,128)(2,1)S(1)}, bf16[432,128]{1,0:T(8,128)(2,1)S(1)}, u32[]{:S(2)}, u32[]{:S(2)}) collective-permute-start(bf16[432,128]{1,0:T(8,128)(2,1)S(1)} %get-tuple-element.90), channel_id=1, source_target_pairs={{0,1},{1,2},{2,3},{3,4},{4,5},{5,6},{6,7},{7,8},{8,9},{9,10},{10,1... | collective-permute-start | bytes 331784 | tf_op jit(solution)/shard_map/ppermute | solution.py:460
  22.7 6.3 %collective-permute-start.1 = (bf16[432,128]{1,0:T(8,128)(2,1)S(1)}, bf16[432,128]{1,0:T(8,128)(2,1)S(1)}, u32[]{:S(2)}, u32[]{:S(2)}) collective-permute-start(bf16[432,128]{1,0:T(8,128)(2,1)S(1)} %get-tuple-element.91), channel_id=1, source_target_pairs={{1,0},{2,1},{3,2},{4,3},{5,4},{6,5},{7,6},{8,7},{9,8},{10,9},{11,1... | collective-permute-start | bytes 331784 | tf_op jit(solution)/shard_map/ppermute | solution.py:461
  24.4 0.8 copy-start.2
  24.4 0.8 copy-start.3
  24.4 0.8 copy-start.4
  24.4 0.8 copy-start.5
  24.4 0.8 copy-start.8
  24.5 0.7 copy-start.7
  44.9 29.8 %all-to-all-start.4 = ((f32[32,1,384]{2,1,0:T(1,128)}), f32[32,1,384]{2,1,0:T(1,128)S(1)}, u32[]{:S(2)}, u32[]{:S(2)}) async-start(f32[32,1,384]{2,1,0:T(1,128)} %shard_map.119), calls=%async_computation.4 | async-start | bytes 98304 | tf_op jit(solution)/shard_map/all_to_all | solution.py:426

commit v8 on v7

--- a/solution.py
+++ b/solution.py
@@ -26,6 +26,7 @@
 DEEP = 32 * ROW
 CAP = 384
 LANES = CAP // CB
+NEAR = 12
 NAMES = SLOTS + 16
 VMEM = pl.BlockSpec(memory_space=pltpu.VMEM)
 SMEM = pl.BlockSpec(memory_space=pltpu.SMEM)
@@ -194,16 +195,46 @@
         windows[j] = jnp.where(lane < LIVE, moved, taps)
 
 
-def arrange_kernel(where, parts, measured, own, sensor, down, up, wide):
+def lane_shift(x, b):
+    shift = (RADIUS - b) % CB
+    return pltpu.roll(x, shift, 1) if shift else x
+
+
+def forward(ahead, source, sums, blocks):
+    result = []
+    for m in range(0, blocks, 2):
+        pair = range(m, min(m + 2, blocks))
+        right = jnp.concatenate([source[i * 256 : i * 256 + DEEP, :] for i in pair], axis=1)
+        value = jnp.dot(ahead[...], right, preferred_element_type=F32)
+        for i in pair:
+            at = (i - m) * CB
+            sums[i - m] = value[:, at : at + CB]
+        for i in pair:
+            total = lane_shift(sums[i - m, pl.ds(0, BLOCK, stride=16), :], 0)
+            for b in range(1, KS):
+                total = total + lane_shift(sums[i - m, pl.ds(b, BLOCK, stride=16), :], b)
+            result.append(total)
+    return result
+
+
+def open_kernel(
+    where, parts, measured,
+    own, sensor, down, up, ahead, behind, scale, image,
+    wide, rounded, sums,
+):
     lane = iota((ROW, CB), 1)
+    rounded[: NEAR * ROW, :] = jnp.zeros((NEAR * ROW, CB), BF16)
+    rounded[(NEAR + ROWS) * ROW :, :] = jnp.zeros(((NEAR + 8) * ROW, CB), BF16)
     for r in range(ROWS):
         line = jnp.where(lane < LIVE, parts[pl.ds(r, ROW, stride=ROWS), :], 0.0)
         own[r * ROW : (r + 1) * ROW, :] = line
-        if r < HALO:
-            up[r * ROW : (r + 1) * ROW, :] = line.astype(BF16)
-        if r >= ROWS - HALO:
-            at = (r - ROWS + HALO) * ROW
-            down[at : at + ROW, :] = line.astype(BF16)
+        line = line.astype(BF16)
+        rounded[(NEAR + r) * ROW : (NEAR + r + 1) * ROW, :] = line
+        if r < NEAR:
+            up[r * ROW : (r + 1) * ROW, :] = line
+        if r >= ROWS - NEAR:
+            at = (r - ROWS + NEAR) * ROW
+            down[at : at + ROW, :] = line
     zeros = jnp.zeros((ROWS, CB), F32)
     wide[:, :CB] = zeros
     wide[:, CB : CB + COLS] = measured[...]
@@ -213,12 +244,6 @@
     moved = pltpu.roll(wide[:, pl.ds(low, 2 * CB)], 2 * CB - (start & (CB - 1)), 1)[:, :CB]
     view = jnp.where(iota((ROWS, CB), 1) < LIVE, moved, 0.0)
     sensor[...] = view
-    for out, part in ((up, view[:HALO]), (down, view[ROWS - HALO :])):
-        high = part.astype(BF16).astype(F32)
-        out[HALO * ROW :, :] = jnp.concatenate([high, part - high], axis=0).astype(BF16)
-
-
-def tables_kernel(parts, ahead, behind, scale):
     taps = jnp.concatenate([parts[pl.ds(a, ROW, stride=ROWS), :] for a in range(16)], axis=0)
     taps = jnp.where(iota((256, CB), 1) >= LIVE, taps, 0.0)
     first = jnp.transpose(taps)[LIVE:, :]
@@ -242,49 +267,47 @@
         total = total + taps[a * ROW : (a + 1) * ROW]
     norm = jnp.sum(total, axis=1, keepdims=True)
     scale[...] = jnp.broadcast_to(1.0 / norm, (ROW, CB))
-
-
-def lane_shift(x, b):
-    shift = (RADIUS - b) % CB
-    return pltpu.roll(x, shift, 1) if shift else x
+    image[...] = jnp.concatenate(forward(ahead, rounded, sums, 3), axis=0)
+    for out, part, lines in (
+        (up, view[:HALO], image[:HALO, :]),
+        (down, view[ROWS - HALO :], image[20 : 20 + HALO, :]),
+    ):
+        rows = []
+        for x in (part, lines):
+            high = x.astype(BF16).astype(F32)
+            rows += [high, x - high]
+        out[NEAR * ROW :, :] = jnp.concatenate(rows, axis=0).astype(BF16)
 
 
 def iterate_kernel(
-    own, left, right, sensor, ahead, behind, scale, codes,
-    sent, flat, exact, rounded, first, second, light, sums, ratio, stack,
+    own, left, right, sensor, image, ahead, behind, scale, codes,
+    sent, flat, exact, second, light, whole, sums, ratio, stack,
 ):
-    rows = (HALO * ROW, (HALO + ROWS) * ROW, (2 * HALO + ROWS) * ROW)
-    exact[: rows[0], :] = left[: rows[0]].astype(F32)
-    exact[rows[0] : rows[1], :] = own[...]
-    exact[rows[1] : rows[2], :] = right[: rows[0]].astype(F32)
-    exact[rows[2] :, :] = jnp.zeros((16 * ROW, CB), F32)
-    rounded[...] = exact[...].astype(BF16)
-    before, after = left[rows[0] :].astype(F32), right[rows[0] :].astype(F32)
-    light[:HALO, :] = before[:HALO] + before[HALO:]
+    near = NEAR * ROW
+    exact[:near, :] = left[:near].astype(F32)
+    exact[near : near + ROWS * ROW, :] = own[...]
+    exact[near + ROWS * ROW : 2 * near + ROWS * ROW, :] = right[:near].astype(F32)
+    exact[2 * near + ROWS * ROW :, :] = jnp.zeros((8 * ROW, CB), F32)
+    before, after = left[near:].astype(F32), right[near:].astype(F32)
+    light[:HALO, :] = before[:HALO] + before[HALO : 2 * HALO]
     light[HALO : HALO + ROWS, :] = sensor[...]
-    light[HALO + ROWS : 2 * HALO + ROWS, :] = after[:HALO] + after[HALO:]
+    light[HALO + ROWS : 2 * HALO + ROWS, :] = after[:HALO] + after[HALO : 2 * HALO]
     light[2 * HALO + ROWS :, :] = jnp.zeros((16, CB), F32)
+    blank = jnp.zeros((20, CB), F32)
+    total = jnp.concatenate([blank[:12], image[...], blank], axis=0)
+    above = jnp.concatenate([before[2 * HALO : 3 * HALO] + before[3 * HALO :], jnp.zeros((56, CB), F32)], axis=0)
+    below = after[2 * HALO : 3 * HALO] + after[3 * HALO :]
+    below = jnp.concatenate([jnp.zeros((44, CB), F32), below, blank[:12]], axis=0)
+    whole[...] = total + above + below
     for m in range(2):
         stack[m * DEEP + KS * 32 : (m + 1) * DEEP, :] = jnp.zeros((DEEP - KS * 32, 2 * CB), BF16)
     tall = jnp.concatenate([scale[...]] * BLOCK, axis=0)
 
-    def divide(source, blocks, offset, valid):
-        for m in range(0, blocks, 2):
-            pair = range(m, min(m + 2, blocks))
-            right = jnp.concatenate([source[i * 256 : i * 256 + DEEP, :] for i in pair], axis=1)
-            value = jnp.dot(ahead[...], right, preferred_element_type=F32)
-            for i in pair:
-                at = (i - m) * CB
-                sums[i - m] = value[:, at : at + CB]
-            for i in pair:
-                total = lane_shift(sums[i - m, pl.ds(0, BLOCK, stride=16), :], 0)
-                for b in range(1, KS):
-                    total = total + lane_shift(sums[i - m, pl.ds(b, BLOCK, stride=16), :], b)
-                seen = light[i * BLOCK + offset : (i + 1) * BLOCK + offset, :]
-                inside = (iota((BLOCK, CB), 0) < valid - i * BLOCK) & (seen != 0.0) & (total != 0.0)
-                ratio[i * BLOCK : (i + 1) * BLOCK, :] = jnp.where(
-                    inside, seen / jnp.where(inside, total, 1.0), 0.0
-                )
+    def divide(total, offset, valid):
+        rows = total.shape[0]
+        seen = light[offset : offset + rows, :]
+        inside = (iota((rows, CB), 0) < valid) & (seen != 0.0) & (total != 0.0)
+        ratio[:rows, :] = jnp.where(inside, seen / jnp.where(inside, total, 1.0), 0.0)
 
     def spread_back(blocks):
         height = 16 * blocks + 16
@@ -298,17 +321,17 @@
         value = jnp.dot(behind[...], stack[m * DEEP : (m + 1) * DEEP, :], preferred_element_type=F32)
         return value[:, :CB] * tall, value[:, CB:] * tall
 
-    divide(rounded, 5, 6, 68)
+    divide(whole[...], 6, 68)
     spread_back(4)
     factors = back(0) + back(1)
     for m in range(4):
-        value = exact[(m * 16 + 12) * ROW : (m * 16 + 28) * ROW, :] * factors[m]
-        first[m * 256 : (m + 1) * 256, :] = value
+        value = exact[m * 256 : (m + 1) * 256, :] * factors[m]
+        exact[m * 256 : (m + 1) * 256, :] = value
         second[m * 256 : (m + 1) * 256, :] = value.astype(BF16)
-    divide(second, 3, 18, 44)
+    divide(jnp.concatenate(forward(ahead, second, sums, 3), axis=0), 18, 44)
     spread_back(2)
     factors = back(0)
-    done = [first[(m * 16 + 12) * ROW : (m * 16 + 28) * ROW, :] * factors[m] for m in range(2)]
+    done = [exact[(m * 16 + 12) * ROW : (m * 16 + 28) * ROW, :] * factors[m] for m in range(2)]
     lane = iota((256, CB), 1)
     packed = jnp.where(lane < WIN, pltpu.roll(done[0], CB - HALO, 1), pltpu.roll(done[1], WIN - HALO, 1))
     flat[...] = packed
@@ -449,19 +472,21 @@
     seed_plane, seed_row, seed_col = tied[7:]
     parts = parts.reshape(DEPTHS * ROWS, CB)
     table = owner_slot.reshape(64, CB)
-    message = ((HALO * ROW + 2 * HALO, CB), BF16)
-    own, sensor, down, up = call(
-        arrange_kernel,
-        [((ROWS * ROW, CB), F32), ((ROWS, CB), F32), message, message],
+    message = ((NEAR * ROW + 4 * HALO, CB), BF16)
+    band = ((256, DEEP), BF16)
+    own, sensor, down, up, ahead, behind, scale, image = call(
+        open_kernel,
+        [((ROWS * ROW, CB), F32), ((ROWS, CB), F32), message, message, band, band, ((ROW, CB), F32), ((48, CB), F32)],
         3,
         scalars=(0,),
-        scratch=[pltpu.VMEM((ROWS, COLS + 2 * CB), F32)],
+        scratch=[
+            pltpu.VMEM((ROWS, COLS + 2 * CB), F32),
+            pltpu.VMEM((64 * ROW, CB), BF16),
+            pltpu.VMEM((2, 256, CB), F32),
+        ],
     )(where, parts, measured)
     left = lax.ppermute(down, "tile", [(i, i + 1) for i in range(TILES - 1)])
     right = lax.ppermute(up, "tile", [(i + 1, i) for i in range(TILES - 1)])
-    ahead, behind, scale = call(
-        tables_kernel, [((256, DEEP), BF16), ((256, DEEP), BF16), ((ROW, CB), F32)], 1
-    )(parts)
     weights = footprints[0].reshape(SLOTS, 512)
     column = ((SLOTS, CB), I32)
     names = ((NAMES, CB), I32)
@@ -495,18 +520,17 @@
     sent, flat = call(
         iterate_kernel,
         [((DEPTHS, 24, CB), F32), ((256, CB), F32)],
-        8,
+        9,
         scratch=[
-            pltpu.VMEM((96 * ROW, CB), F32),
-            pltpu.VMEM((96 * ROW, CB), BF16),
             pltpu.VMEM((64 * ROW, CB), F32),
             pltpu.VMEM((64 * ROW, CB), BF16),
             pltpu.VMEM((96, CB), F32),
+            pltpu.VMEM((80, CB), F32),
             pltpu.VMEM((2, 256, CB), F32),
             pltpu.VMEM((80, CB), F32),
             pltpu.VMEM((2 * DEEP, 2 * CB), BF16),
         ],
-    )(own, left, right, sensor, ahead, behind, scale, first)
+    )(own, left, right, sensor, image, ahead, behind, scale, first)
     parts, most = lax.optimization_barrier((swap(sent, "depth"), most))
 
     def share(values, at):

time: 104 us -> 104 us (level)
    pallas_call x3 -> x2, Pallas kernels: 3.38 us -> 3.07 us  [the longest x1 1.75 us: body(): call(iterate_kernel, [((DEPTHS, 24, CB), F32), ((256, CB), F32)], 9, scra...]
where the time goes in v8:
time: 104 us; the launch traced here: 103 us
  blocking collectives  58 us (56%)
  starting transfers between devices  20.2 us (19%)
  waiting for transfers between devices  10.9 us (10%)
  Pallas kernels  8.95 us (9%)
  local copies, waits for them, and re-layouts  3.39 us (3%)
  between operations  1.46 us (1%)
    all_to_all x4, blocking collectives, swap(): return lax.all_to_all(pieces, axis, 0, 0)  58 us
    all_to_all x1, starting transfers between devices, swap(): return lax.all_to_all(pieces, axis, 0, 0)  17.6 us
    all_to_all x1, waiting for transfers between devices, swap(): return lax.all_to_all(pieces, axis, 0, 0)  10.2 us
    pallas_call x1, Pallas kernels, body(): call(prepare_kernel, [((SLOTS, SLOTS), F32), ((8, SLOTS), I32), column, c...  3.08 us
    unnamed x21, local copies, waits for them, and re-layouts  2.35 us
  transfers between devices with their start and end apart: 3, of which 2 were waited for; matrix products, arithmetic and copies ran while one was open for 1% of the time, Pallas kernels for 4%

profile of v8, /device:TPU:1, one launch (start us, length us, event | category | flops | bytes accessed | tf_op | source)
XLA Modules:
  0.0 103.0 jit_solution(1014507295382128727)
XLA Ops:
  0.7 0.7 copy-done.6
  1.3 0.9 copy-done
  2.2 0.1 shard_map.113
  2.4 0.1 pad_add_fusion.where
  2.5 18.2 %all_to_all.37 = f32[16,32,128]{2,1,0:T(8,128)S(1)} all-to-all(f32[16,32,128]{2,1,0:T(8,128)S(1)} %shard_map.113), channel_id=1, replica_groups=mesh['depth'=16,'tile'=32] {'depth'}, dimensions={0} | all-to-all | bytes 524288 | tf_op jit(solution)/shard_map/all_to_all | solution.py:449
  20.6 1.3 %shard_map.114 = (f32[512,128]{1,0:T(8,128)S(1)}, f32[32,128]{1,0:T(8,128)S(1)}, bf16[288,128]{1,0:T(8,128)(2,1)S(1)}, bf16[288,128]{1,0:T(8,128)(2,1)S(1)}, bf1...) custom-call(s32[3]{0:T(128)S(1)} %pad_add_fusion.where, ...), custom_call_target="tpu_custom_call" | custom-call | tf_op jit(solution)/shard_map/pallas_call | solution.py:477
  21.9 1.3 %collective-permute-start = (bf16[288,128]{1,0:T(8,128)(2,1)S(1)}, bf16[288,128]{1,0:T(8,128)(2,1)S(1)}, u32[]{:S(2)}, u32[]{:S(2)}) collective-permute-start(bf16[288,128]{1,0:T(8,128)(2,1)S(1)} %get-tuple-element.91), channel_id=1, source_target_pairs={{0,1},{1,2},{2,3},{3,4},{4,5},{5,6},{6,7},{7,8},{8,9},{9,10},{10,1... | collective-permute-start | bytes 221192 | tf_op jit(solution)/shard_map/ppermute | solution.py:488
  23.2 1.3 %collective-permute-start.1 = (bf16[288,128]{1,0:T(8,128)(2,1)S(1)}, bf16[288,128]{1,0:T(8,128)(2,1)S(1)}, u32[]{:S(2)}, u32[]{:S(2)}) collective-permute-start(bf16[288,128]{1,0:T(8,128)(2,1)S(1)} %get-tuple-element.92), channel_id=1, source_target_pairs={{1,0},{2,1},{3,2},{4,3},{5,4},{6,5},{7,6},{8,7},{9,8},{10,9},{11,1... | collective-permute-start | bytes 221192 | tf_op jit(solution)/shard_map/ppermute | solution.py:489
  24.5 0.0 copy-start.2
  24.6 0.0 copy-start.5
  24.6 0.0 copy-start.8
  24.7 0.0 copy-start.7
  24.7 0.6 copy-done.2
  25.3 0.0 copy-done.3
  25.3 0.0 copy-done.4
  25.3 0.0 copy-done.5
  25.4 3.1 %shard_map.115 = (f32[256,256]{1,0:T(8,128)S(1)}, s32[8,256]{1,0:T(8,128)S(1)}, s32[256,128]{1,0:T(8,128)S(1)}, s32[256,128]{1,0:T(8,128)S(1)}, s32[272,128]{1,0...) custom-call(s32[3]{0:T(128)S(1)} %pad_add_fusion.where, ...), custom_call_target="tpu_custom_call" | custom-call | tf_op jit(solution)/shard_map/pallas_call | solution.py:494
  28.5 0.0 collective-permute-done.left
  28.5 0.7 collective-permute-done.1.right
  29.2 1.8 %shard_map.116 = (f32[16,24,128]{2,1,0:T(8,128)S(1)}, f32[256,128]{1,0:T(8,128)S(1)}) custom-call(f32[512,128]{1,0:T(8,128)S(1)} %get-tuple-element.90.own, bf16[288,128]{1,0:T(8,128)(2,1)S(1)} %collective-permute-done.left, bf16[288,128]{1,0:T(8,128)(2,1)S(1)} %collective-permute-done.1.right, f32[32,128]{1,0:T(8,128)S(1)} %get-tuple-element.93.sensor, ...), custom_call_target="tpu_custom_call" | custom-call | tf_op jit(solution)/shard_map/pallas_call | solution.py:520
  30.9 12.8 %all_to_all.38.parts = f32[16,24,128]{2,1,0:T(8,128)S(1)} all-to-all(f32[16,24,128]{2,1,0:T(8,128)S(1)} %get-tuple-element.106), channel_id=1, replica_groups=mesh['depth'=16,'tile'=32] {'depth'}, dimensions={0} | all-to-all | bytes 393216 | tf_op jit(solution)/shard_map/all_to_all | solution.py:449
  43.7 0.6 shard_map.118
  44.4 17.6 %all-to-all-start.4 = ((f32[32,1,384]{2,1,0:T(1,128)}), f32[32,1,384]{2,1,0:T(1,128)S(1)}, u32[]{:S(2)}, u32[]{:S(2)}) async-start(f32[32,1,384]{2,1,0:T(1,128)} %shard_map.118), calls=%async_computation.4 | async-start | bytes 98304 | tf_op jit(solution)/shard_map/all_to_all | solution.py:449
  62.0 0.5 slice.6
  63.2 1.0 %shard_map.117 = (f32[32,1024]{1,0:T(8,128)}, f32[256,128]{1,0:T(8,128)S(1)}) custom-call(f32[16,24,128]{2,1,0:T(8,128)S(1)} %all_to_all.38.parts, bf16[256,512]{1,0:T(8,128)(2,1)S(1)} %bitcast.22, s32[256,128]{1,0:T(8,128)S(1)} %get-tuple-element.109.b_col), custom_call_target="tpu_custom_call" | custom-call | tf_op jit(solution)/shard_map/pallas_call | solution.py:555
  64.2 10.2 %all-to-all-done.4.parts = f32[32,1,384]{2,1,0:T(1,128)S(1)} async-done(((f32[32,1,384]{2,1,0:T(1,128)}), f32[32,1,384]{2,1,0:T(1,128)S(1)}, u32[]{:S(2)}, u32[]{:S(2)}) %all-to-all-start.4) | async-done | bytes 49184 | tf_op jit(solution)/shard_map/all_to_all | solution.py:449
  74.4 0.8 shard_map.119
  75.2 12.1 %all_to_all.39.parts = f32[16,8,128]{2,1,0:T(8,128)S(1)} all-to-all(f32[16,8,128]{2,1,0:T(8,128)S(1)} %get-tuple-element.124), channel_id=1, replica_groups=mesh['depth'=16,'tile'=32] {'depth'}, dimensions={0} | all-to-all | bytes 131072 | tf_op jit(solution)/shard_map/all_to_all | solution.py:449
  87.3 0.1 shard_map.120
  87.4 15.0 %all_to_all.40.parts = f32[32,1,128]{2,1,0:T(1,128)S(1)} all-to-all(f32[32,1,128]{2,1,0:T(1,128)S(1)} %shard_map.120), channel_id=1, replica_groups=mesh['depth'=16,'tile'=32] {'tile'}, dimensions={0} | all-to-all | bytes 32768 | tf_op jit(solution)/shard_map/all_to_all | solution.py:449
  102.4 0.1 shard_map.121
  102.5 0.5 slice_bitcast_fusion
  (13 shorter events, 0.1 us)
Async XLA Ops:
  0.6 0.7 copy-start.6
  1.3 0.9 copy-start
  2.5 18.2 %copy-start.1 = (f32[32,1024]{1,0:T(8,128)S(1)}, f32[32,1024]{1,0:T(8,128)}, u32[]{:S(2)}) copy-start(f32[32,1024]{1,0:T(8,128)} %measured) | copy-start | bytes 393220
  20.6 3.9 %copy-start.9 = (bf16[1,256,4,128]{3,2,1,0:T(4,128)(2,1)S(1)}, bf16[1,256,4,128]{3,2,1,0:T(4,128)(2,1)}, u32[]{:S(2)}) copy-start(bf16[1,256,4,128]{3,2,1,0:T(4,128)(2,1)} %param.17) | copy-start | bytes 786436
  21.9 6.5 %collective-permute-start = (bf16[288,128]{1,0:T(8,128)(2,1)S(1)}, bf16[288,128]{1,0:T(8,128)(2,1)S(1)}, u32[]{:S(2)}, u32[]{:S(2)}) collective-permute-start(bf16[288,128]{1,0:T(8,128)(2,1)S(1)} %get-tuple-element.91), channel_id=1, source_target_pairs={{0,1},{1,2},{2,3},{3,4},{4,5},{5,6},{6,7},{7,8},{8,9},{9,10},{10,1... | collective-permute-start | bytes 221192 | tf_op jit(solution)/shard_map/ppermute | solution.py:488
  23.2 6.0 %collective-permute-start.1 = (bf16[288,128]{1,0:T(8,128)(2,1)S(1)}, bf16[288,128]{1,0:T(8,128)(2,1)S(1)}, u32[]{:S(2)}, u32[]{:S(2)}) collective-permute-start(bf16[288,128]{1,0:T(8,128)(2,1)S(1)} %get-tuple-element.92), channel_id=1, source_target_pairs={{1,0},{2,1},{3,2},{4,3},{5,4},{6,5},{7,6},{8,7},{9,8},{10,9},{11,1... | collective-permute-start | bytes 221192 | tf_op jit(solution)/shard_map/ppermute | solution.py:489
  24.5 0.8 copy-start.2
  24.6 0.8 copy-start.3
  24.6 0.8 copy-start.4
  24.6 0.8 copy-start.5
  24.6 0.8 copy-start.8
  24.7 0.7 copy-start.7
  44.4 30.0 %all-to-all-start.4 = ((f32[32,1,384]{2,1,0:T(1,128)}), f32[32,1,384]{2,1,0:T(1,128)S(1)}, u32[]{:S(2)}, u32[]{:S(2)}) async-start(f32[32,1,384]{2,1,0:T(1,128)} %shard_map.118), calls=%async_computation.4 | async-start | bytes 98304 | tf_op jit(solution)/shard_map/all_to_all | solution.py:449

commit v9 on v8

--- a/solution.py
+++ b/solution.py
@@ -464,29 +464,9 @@
     d = lax.axis_index("depth")
     t = lax.axis_index("tile")
     where = jnp.stack([d, t, (d * TILES + t) * 16]).astype(I32)
+    table = owner_slot.reshape(64, CB)
     [windows] = call(window_kernel, [((DEPTHS, ROWS, CB), F32)], 2)(volume, point_spread)
-    windows, where = lax.optimization_barrier((windows, where))
-    tied = (swap(windows, "depth"), where, measured, entry_block, entry_neuron, footprints, owner_slot)
-    tied = lax.optimization_barrier(tied + (seed_plane, seed_row, seed_col))
-    parts, where, measured, entry_block, entry_neuron, footprints, owner_slot = tied[:7]
-    seed_plane, seed_row, seed_col = tied[7:]
-    parts = parts.reshape(DEPTHS * ROWS, CB)
-    table = owner_slot.reshape(64, CB)
-    message = ((NEAR * ROW + 4 * HALO, CB), BF16)
-    band = ((256, DEEP), BF16)
-    own, sensor, down, up, ahead, behind, scale, image = call(
-        open_kernel,
-        [((ROWS * ROW, CB), F32), ((ROWS, CB), F32), message, message, band, band, ((ROW, CB), F32), ((48, CB), F32)],
-        3,
-        scalars=(0,),
-        scratch=[
-            pltpu.VMEM((ROWS, COLS + 2 * CB), F32),
-            pltpu.VMEM((64 * ROW, CB), BF16),
-            pltpu.VMEM((2, 256, CB), F32),
-        ],
-    )(where, parts, measured)
-    left = lax.ppermute(down, "tile", [(i, i + 1) for i in range(TILES - 1)])
-    right = lax.ppermute(up, "tile", [(i + 1, i) for i in range(TILES - 1)])
+    parts = swap(windows, "depth").reshape(DEPTHS * ROWS, CB)
     weights = footprints[0].reshape(SLOTS, 512)
     column = ((SLOTS, CB), I32)
     names = ((NAMES, CB), I32)
@@ -517,6 +497,22 @@
         seed_row.reshape(64, CB),
         seed_col.reshape(64, CB),
     )
+    view, first = lax.optimization_barrier((measured, first))
+    message = ((NEAR * ROW + 4 * HALO, CB), BF16)
+    band = ((256, DEEP), BF16)
+    own, sensor, down, up, ahead, behind, scale, image = call(
+        open_kernel,
+        [((ROWS * ROW, CB), F32), ((ROWS, CB), F32), message, message, band, band, ((ROW, CB), F32), ((48, CB), F32)],
+        3,
+        scalars=(0,),
+        scratch=[
+            pltpu.VMEM((ROWS, COLS + 2 * CB), F32),
+            pltpu.VMEM((64 * ROW, CB), BF16),
+            pltpu.VMEM((2, 256, CB), F32),
+        ],
+    )(where, parts, view)
+    left = lax.ppermute(down, "tile", [(i, i + 1) for i in range(TILES - 1)])
+    right = lax.ppermute(up, "tile", [(i + 1, i) for i in range(TILES - 1)])
     sent, flat = call(
         iterate_kernel,
         [((DEPTHS, 24, CB), F32), ((256, CB), F32)],

time: 104 us -> 104 us (level)
  blocking collectives: 58 us -> 40.1 us
  starting transfers between devices: 20.2 us -> 30.3 us
  waiting for transfers between devices: 10.9 us -> 18.9 us
    all_to_all x4 -> x3, blocking collectives: 58 us -> 40.1 us  [swap(): return lax.all_to_all(pieces, axis, 0, 0)]
    all_to_all x1 -> x2, starting transfers between devices: 17.6 us -> 27.7 us  [swap(): return lax.all_to_all(pieces, axis, 0, 0)]
    all_to_all x1 -> x2, waiting for transfers between devices: 10.2 us -> 15 us  [swap(): return lax.all_to_all(pieces, axis, 0, 0)]
    ppermute x1, waiting for transfers between devices: 0.71 us -> 3.86 us  [body(): right = lax.ppermute(up, 'tile', [(i + 1, i) for i in range(TILES - 1)])]
  transfers between devices with their start and end apart: 3 -> 4, of which waited for: 2 -> 4; matrix products, arithmetic and copies ran while one was open for 1% -> 1% of each run, Pallas kernels for 4% -> 4%
where the time goes in v9:
time: 104 us
  blocking collectives  40.1 us (39%)
  starting transfers between devices  30.3 us (29%)
  waiting for transfers between devices  18.9 us (18%)
  Pallas kernels  9.66 us (9%)
  local copies, waits for them, and re-layouts  3.39 us (3%)
  between operations  1.43 us (1%)
    all_to_all x3, blocking collectives, swap(): return lax.all_to_all(pieces, axis, 0, 0)  40.1 us
    all_to_all x2, starting transfers between devices, swap(): return lax.all_to_all(pieces, axis, 0, 0)  27.7 us
    all_to_all x2, waiting for transfers between devices, swap(): return lax.all_to_all(pieces, axis, 0, 0)  15 us
    ppermute x1, waiting for transfers between devices, body(): right = lax.ppermute(up, 'tile', [(i + 1, i) for i in range(TILES - 1)])  3.86 us
    pallas_call x1, Pallas kernels, body(): call(prepare_kernel, [((SLOTS, SLOTS), F32), ((8, SLOTS), I32), column, c...  3.08 us
    unnamed x21, local copies, waits for them, and re-layouts  2.34 us
  transfers between devices with their start and end apart: 4, of which 4 were waited for; matrix products, arithmetic and copies ran while one was open for 1% of the time, Pallas kernels for 4%

profile of v9, /device:TPU:1, one launch (start us, length us, event | category | flops | bytes accessed | tf_op | source)
XLA Modules:
  0.0 103.9 jit_solution(14276438001435647830)
XLA Ops:
  0.6 0.9 copy-done
  1.5 0.7 copy-done.6
  2.2 0.8 shard_map.113
  3.1 10.3 %all-to-all-start.2 = ((f32[16,32,128]{2,1,0:T(8,128)}), f32[16,32,128]{2,1,0:T(8,128)S(1)}, u32[]{:S(2)}, u32[]{:S(2)}) async-start(f32[16,32,128]{2,1,0:T(8,128)} %shard_map.113), calls=%async_computation.2 | async-start | bytes 524288 | tf_op jit(solution)/shard_map/all_to_all | solution.py:449
  13.4 0.0 copy-start.3
  13.4 0.0 copy-start.4
  13.5 0.1 pad_add_fusion.where
  13.6 0.6 copy-done.2
  14.2 0.0 copy-done.3
  14.2 0.0 copy-done.4
  14.2 0.0 copy-done.5
  14.2 0.1 copy-done.7
  14.3 3.1 %shard_map.114 = (f32[256,256]{1,0:T(8,128)S(1)}, s32[8,256]{1,0:T(8,128)S(1)}, s32[256,128]{1,0:T(8,128)S(1)}, s32[256,128]{1,0:T(8,128)S(1)}, s32[272,128]{1,0...) custom-call(s32[3]{0:T(128)S(1)} %pad_add_fusion.where, ...), custom_call_target="tpu_custom_call" | custom-call | tf_op jit(solution)/shard_map/pallas_call | solution.py:474
  17.4 4.8 %all-to-all-done.2 = f32[16,32,128]{2,1,0:T(8,128)S(1)} async-done(((f32[16,32,128]{2,1,0:T(8,128)}), f32[16,32,128]{2,1,0:T(8,128)S(1)}, u32[]{:S(2)}, u32[]{:S(2)}) %all-to-all-start.2) | async-done | bytes 262176 | tf_op jit(solution)/shard_map/all_to_all | solution.py:449
  22.1 1.3 %shard_map.115 = (f32[512,128]{1,0:T(8,128)S(1)}, f32[32,128]{1,0:T(8,128)S(1)}, bf16[288,128]{1,0:T(8,128)(2,1)S(1)}, bf16[288,128]{1,0:T(8,128)(2,1)S(1)}, bf1...) custom-call(s32[3]{0:T(128)S(1)} %pad_add_fusion.where, ...), custom_call_target="tpu_custom_call" | custom-call | tf_op jit(solution)/shard_map/pallas_call | solution.py:503
  23.5 1.3 %collective-permute-start = (bf16[288,128]{1,0:T(8,128)(2,1)S(1)}, bf16[288,128]{1,0:T(8,128)(2,1)S(1)}, u32[]{:S(2)}, u32[]{:S(2)}) collective-permute-start(bf16[288,128]{1,0:T(8,128)(2,1)S(1)} %get-tuple-element.78), channel_id=1, source_target_pairs={{0,1},{1,2},{2,3},{3,4},{4,5},{5,6},{6,7},{7,8},{8,9},{9,10},{10,1... | collective-permute-start | bytes 221192 | tf_op jit(solution)/shard_map/ppermute | solution.py:514
  24.8 1.3 %collective-permute-start.1 = (bf16[288,128]{1,0:T(8,128)(2,1)S(1)}, bf16[288,128]{1,0:T(8,128)(2,1)S(1)}, u32[]{:S(2)}, u32[]{:S(2)}) collective-permute-start(bf16[288,128]{1,0:T(8,128)(2,1)S(1)} %get-tuple-element.79), channel_id=1, source_target_pairs={{1,0},{2,1},{3,2},{4,3},{5,4},{6,5},{7,6},{8,7},{9,8},{10,9},{11,1... | collective-permute-start | bytes 221192 | tf_op jit(solution)/shard_map/ppermute | solution.py:515
  26.1 0.1 collective-permute-done.left
  26.1 3.9 %collective-permute-done.1.right = bf16[288,128]{1,0:T(8,128)(2,1)S(1)} collective-permute-done((bf16[288,128]{1,0:T(8,128)(2,1)S(1)}, bf16[288,128]{1,0:T(8,128)(2,1)S(1)}, u32[]{:S(2)}, u32[]{:S(2)}) %collective-permute-start.1) | collective-permute-done | bytes 73760 | tf_op jit(solution)/shard_map/ppermute | solution.py:515
  30.0 1.8 %shard_map.116 = (f32[16,24,128]{2,1,0:T(8,128)S(1)}, f32[256,128]{1,0:T(8,128)S(1)}) custom-call(f32[512,128]{1,0:T(8,128)S(1)} %get-tuple-element.77.own, bf16[288,128]{1,0:T(8,128)(2,1)S(1)} %collective-permute-done.left, bf16[288,128]{1,0:T(8,128)(2,1)S(1)} %collective-permute-done.1.right, f32[32,128]{1,0:T(8,128)S(1)} %get-tuple-element.80.sensor, ...), custom_call_target="tpu_custom_call" | custom-call | tf_op jit(solution)/shard_map/pallas_call | solution.py:516
  31.8 12.8 %all_to_all.37.parts = f32[16,24,128]{2,1,0:T(8,128)S(1)} all-to-all(f32[16,24,128]{2,1,0:T(8,128)S(1)} %get-tuple-element.86), channel_id=1, replica_groups=mesh['depth'=16,'tile'=32] {'depth'}, dimensions={0} | all-to-all | bytes 393216 | tf_op jit(solution)/shard_map/all_to_all | solution.py:449
  44.6 0.6 shard_map.118
  45.2 17.4 %all-to-all-start.4 = ((f32[32,1,384]{2,1,0:T(1,128)}), f32[32,1,384]{2,1,0:T(1,128)S(1)}, u32[]{:S(2)}, u32[]{:S(2)}) async-start(f32[32,1,384]{2,1,0:T(1,128)} %shard_map.118), calls=%async_computation.4 | async-start | bytes 98304 | tf_op jit(solution)/shard_map/all_to_all | solution.py:449
  62.6 0.5 slice.6
  63.8 1.0 shard_map.117
  64.8 10.2 %all-to-all-done.4.parts = f32[32,1,384]{2,1,0:T(1,128)S(1)} async-done(((f32[32,1,384]{2,1,0:T(1,128)}), f32[32,1,384]{2,1,0:T(1,128)S(1)}, u32[]{:S(2)}, u32[]{:S(2)}) %all-to-all-start.4) | async-done | bytes 49184 | tf_op jit(solution)/shard_map/all_to_all | solution.py:449
  75.0 0.8 shard_map.119
  75.9 12.2 %all_to_all.38.parts = f32[16,8,128]{2,1,0:T(8,128)S(1)} all-to-all(f32[16,8,128]{2,1,0:T(8,128)S(1)} %get-tuple-element.104), channel_id=1, replica_groups=mesh['depth'=16,'tile'=32] {'depth'}, dimensions={0} | all-to-all | bytes 131072 | tf_op jit(solution)/shard_map/all_to_all | solution.py:449
  88.1 0.1 shard_map.120
  88.2 15.0 %all_to_all.39.parts = f32[32,1,128]{2,1,0:T(1,128)S(1)} all-to-all(f32[32,1,128]{2,1,0:T(1,128)S(1)} %shard_map.120), channel_id=1, replica_groups=mesh['depth'=16,'tile'=32] {'tile'}, dimensions={0} | all-to-all | bytes 32768 | tf_op jit(solution)/shard_map/all_to_all | solution.py:449
  103.2 0.1 shard_map.121
  103.3 0.5 slice_bitcast_fusion
  (14 shorter events, 0.1 us)
Async XLA Ops:
  0.6 0.9 copy-start
  1.5 0.7 copy-start.6
  3.1 10.3 %copy-start.9 = (bf16[1,256,4,128]{3,2,1,0:T(4,128)(2,1)S(1)}, bf16[1,256,4,128]{3,2,1,0:T(4,128)(2,1)}, u32[]{:S(2)}) copy-start(bf16[1,256,4,128]{3,2,1,0:T(4,128)(2,1)} %param.17) | copy-start | bytes 786436
  3.1 19.1 %all-to-all-start.2 = ((f32[16,32,128]{2,1,0:T(8,128)}), f32[16,32,128]{2,1,0:T(8,128)S(1)}, u32[]{:S(2)}, u32[]{:S(2)}) async-start(f32[16,32,128]{2,1,0:T(8,128)} %shard_map.113), calls=%async_computation.2 | async-start | bytes 524288 | tf_op jit(solution)/shard_map/all_to_all | solution.py:449
  13.4 0.8 copy-start.2
  13.4 0.8 copy-start.3
  13.4 0.8 copy-start.4
  13.4 0.8 copy-start.5
  13.5 0.7 copy-start.8
  13.6 0.7 copy-start.7
  14.3 7.9 %copy-start.1 = (f32[32,1024]{1,0:T(8,128)S(1)}, f32[32,1024]{1,0:T(8,128)}, u32[]{:S(2)}) copy-start(f32[32,1024]{1,0:T(8,128)} %measured) | copy-start | bytes 393220
  23.5 2.7 %collective-permute-start = (bf16[288,128]{1,0:T(8,128)(2,1)S(1)}, bf16[288,128]{1,0:T(8,128)(2,1)S(1)}, u32[]{:S(2)}, u32[]{:S(2)}) collective-permute-start(bf16[288,128]{1,0:T(8,128)(2,1)S(1)} %get-tuple-element.78), channel_id=1, source_target_pairs={{0,1},{1,2},{2,3},{3,4},{4,5},{5,6},{6,7},{7,8},{8,9},{9,10},{10,1... | collective-permute-start | bytes 221192 | tf_op jit(solution)/shard_map/ppermute | solution.py:514
  24.8 5.3 %collective-permute-start.1 = (bf16[288,128]{1,0:T(8,128)(2,1)S(1)}, bf16[288,128]{1,0:T(8,128)(2,1)S(1)}, u32[]{:S(2)}, u32[]{:S(2)}) collective-permute-start(bf16[288,128]{1,0:T(8,128)(2,1)S(1)} %get-tuple-element.79), channel_id=1, source_target_pairs={{1,0},{2,1},{3,2},{4,3},{5,4},{6,5},{7,6},{8,7},{9,8},{10,9},{11,1... | collective-permute-start | bytes 221192 | tf_op jit(solution)/shard_map/ppermute | solution.py:515
  45.2 29.8 %all-to-all-start.4 = ((f32[32,1,384]{2,1,0:T(1,128)}), f32[32,1,384]{2,1,0:T(1,128)S(1)}, u32[]{:S(2)}, u32[]{:S(2)}) async-start(f32[32,1,384]{2,1,0:T(1,128)} %shard_map.118), calls=%async_computation.4 | async-start | bytes 98304 | tf_op jit(solution)/shard_map/all_to_all | solution.py:449

commit v10 on v8

--- a/solution.py
+++ b/solution.py
@@ -413,30 +413,33 @@
     over = jnp.sum(terms[:, :CB] + terms[:, CB:], axis=1, keepdims=True)
     place = q_col[...]
     lane = iota((SLOTS, CB), 1)
-    target = ((place >> 4) & 3) * 32 + (place & 15)
+    target = ((place >> 5) & 3) * 32 + (place & 15)
     sent = jnp.where(lane == target, proj[...], 0.0) + jnp.where(lane == target + 16, over, 0.0)
-    row_hot = (iota((CB, SLOTS), 0) == (q_row[0:1, :] >> 6)).astype(F32).astype(BF16)
+    spot = q_row[0:1, :]
+    line = ((spot >> 9) * 2 + ((spot >> 4) & 1)) * 4 + ((spot >> 7) & 3)
+    row_hot = (iota((CB, SLOTS), 0) == jnp.where(spot >= 0, line, -1)).astype(F32).astype(BF16)
     parts = split3(sent)
     dense = jnp.dot(row_hot, parts[0], preferred_element_type=F32)
     dense = dense + jnp.dot(row_hot, parts[1], preferred_element_type=F32)
     dense = dense + jnp.dot(row_hot, parts[2], preferred_element_type=F32)
-    for j in range(DEPTHS):
-        out[j] = dense[j * 8 : (j + 1) * 8]
+    for j in range(TILES):
+        out[j] = dense[j * 4 : (j + 1) * 4]
 
 
 def fold_kernel(parts, out):
     total = parts[0]
-    for j in range(1, DEPTHS):
+    for j in range(1, TILES):
         total = total + parts[j]
+    total = jnp.concatenate([total, total], axis=0)
     for m in range(4):
         moved = pltpu.roll(total, (CB - 32 * m) % CB, 1) if m else total
-        for r in range(8):
+        for r in range(4):
             out[4 * r + m] = moved[r : r + 1]
 
 
 def final_kernel(parts, own, out):
     total = parts[0]
-    for j in range(1, TILES):
+    for j in range(1, TILES // 2):
         total = total + parts[j]
     over = pltpu.roll(total, CB - 16, 1)
     initial = own[...]
@@ -445,8 +448,8 @@
     out[...] = jnp.where(real, initial * total, 0.0) / bottom
 
 
-def swap(pieces, axis):
-    return lax.all_to_all(pieces, axis, 0, 0)
+def swap(pieces, axis, groups=None):
+    return lax.all_to_all(pieces, axis, 0, 0, axis_index_groups=groups)
 
 
 def body(
@@ -558,11 +561,15 @@
         3,
         scratch=[pltpu.VMEM((NCB * ROWS, CB), F32)],
     )(parts, weights, b_col)
-    sent, own = call(slots_kernel, [((DEPTHS, 8, CB), F32), ((1, CB), F32)], 8)(
+    sent, own = call(slots_kernel, [((TILES, 4, CB), F32), ((1, CB), F32)], 8)(
         shared, a_row, a_lane, known, gram, q_row, q_col, proj
     )
-    [sent] = call(fold_kernel, [((TILES, 1, CB), F32)], 1)(swap(sent, "depth"))
-    [demixed] = call(final_kernel, [((1, CB), F32)], 2)(swap(sent, "tile"), own)
+    pairs = TILES // 2
+    near = [[d * TILES + 2 * z + x for d in range(DEPTHS) for x in range(2)] for z in range(pairs)]
+    far = [[2 * z + x for z in range(pairs)] for x in range(2)]
+    sent = swap(sent, ("depth", "tile"), near)
+    [sent] = call(fold_kernel, [((pairs, 1, CB), F32)], 1)(sent)
+    [demixed] = call(final_kernel, [((1, CB), F32)], 2)(swap(sent, "tile", far), own)
     return estimate[None], demixed[0, :16]
 
 

time: 104 us -> 102 us (0.981)
  blocking collectives: 58 us -> 56.9 us
    all_to_all x4, blocking collectives: 58 us -> 56.9 us  [swap(): return lax.all_to_all(pieces, axis, 0, 0, axis_index_groups=groups)]
where the time goes in v10:
time: 102 us
  blocking collectives  56.9 us (56%)
  starting transfers between devices  20.2 us (20%)
  waiting for transfers between devices  10.9 us (11%)
  Pallas kernels  8.95 us (9%)
  local copies, waits for them, and re-layouts  3.39 us (3%)
  between operations  1.46 us (1%)
    all_to_all x4, blocking collectives, swap(): return lax.all_to_all(pieces, axis, 0, 0, axis_index_groups=groups)  56.9 us
    all_to_all x1, starting transfers between devices, swap(): return lax.all_to_all(pieces, axis, 0, 0, axis_index_groups=groups)  17.6 us
    all_to_all x1, waiting for transfers between devices, swap(): return lax.all_to_all(pieces, axis, 0, 0, axis_index_groups=groups)  10.2 us
    pallas_call x1, Pallas kernels, body(): call(prepare_kernel, [((SLOTS, SLOTS), F32), ((8, SLOTS), I32), column, c...  3.08 us
    unnamed x21, local copies, waits for them, and re-layouts  2.35 us
  transfers between devices with their start and end apart: 3, of which 2 were waited for; matrix products, arithmetic and copies ran while one was open for 1% of the time, Pallas kernels for 4%

profile of v10, /device:TPU:1, one launch (start us, length us, event | category | flops | bytes accessed | tf_op | source)
XLA Modules:
  0.0 101.9 jit_solution(694983831315907333)
XLA Ops:
  0.7 0.7 copy-done.6
  1.3 0.9 copy-done
  2.2 0.1 shard_map.113
  2.4 0.1 pad_add_fusion.where
  2.5 18.2 %all_to_all.37 = f32[16,32,128]{2,1,0:T(8,128)S(1)} all-to-all(f32[16,32,128]{2,1,0:T(8,128)S(1)} %shard_map.113), channel_id=1, replica_groups=mesh['depth'=16,'tile'=32] {'depth'}, dimensions={0} | all-to-all | bytes 524288 | tf_op jit(solution)/shard_map/all_to_all | solution.py:452
  20.6 1.3 %shard_map.114 = (f32[512,128]{1,0:T(8,128)S(1)}, f32[32,128]{1,0:T(8,128)S(1)}, bf16[288,128]{1,0:T(8,128)(2,1)S(1)}, bf16[288,128]{1,0:T(8,128)(2,1)S(1)}, bf1...) custom-call(s32[3]{0:T(128)S(1)} %pad_add_fusion.where, ...), custom_call_target="tpu_custom_call" | custom-call | tf_op jit(solution)/shard_map/pallas_call | solution.py:480
  21.9 1.3 %collective-permute-start = (bf16[288,128]{1,0:T(8,128)(2,1)S(1)}, bf16[288,128]{1,0:T(8,128)(2,1)S(1)}, u32[]{:S(2)}, u32[]{:S(2)}) collective-permute-start(bf16[288,128]{1,0:T(8,128)(2,1)S(1)} %get-tuple-element.91), channel_id=1, source_target_pairs={{0,1},{1,2},{2,3},{3,4},{4,5},{5,6},{6,7},{7,8},{8,9},{9,10},{10,1... | collective-permute-start | bytes 221192 | tf_op jit(solution)/shard_map/ppermute | solution.py:491
  23.2 1.3 %collective-permute-start.1 = (bf16[288,128]{1,0:T(8,128)(2,1)S(1)}, bf16[288,128]{1,0:T(8,128)(2,1)S(1)}, u32[]{:S(2)}, u32[]{:S(2)}) collective-permute-start(bf16[288,128]{1,0:T(8,128)(2,1)S(1)} %get-tuple-element.92), channel_id=1, source_target_pairs={{1,0},{2,1},{3,2},{4,3},{5,4},{6,5},{7,6},{8,7},{9,8},{10,9},{11,1... | collective-permute-start | bytes 221192 | tf_op jit(solution)/shard_map/ppermute | solution.py:492
  24.5 0.0 copy-start.2
  24.6 0.0 copy-start.3
  24.6 0.0 copy-start.4
  24.6 0.0 copy-start.5
  24.7 0.6 copy-done.2
  25.3 0.0 copy-done.3
  25.3 0.0 copy-done.4
  25.3 0.0 copy-done.5
  25.4 3.1 %shard_map.115 = (f32[256,256]{1,0:T(8,128)S(1)}, s32[8,256]{1,0:T(8,128)S(1)}, s32[256,128]{1,0:T(8,128)S(1)}, s32[256,128]{1,0:T(8,128)S(1)}, s32[272,128]{1,0...) custom-call(s32[3]{0:T(128)S(1)} %pad_add_fusion.where, ...), custom_call_target="tpu_custom_call" | custom-call | tf_op jit(solution)/shard_map/pallas_call | solution.py:497
  28.5 0.0 collective-permute-done.left
  28.5 0.7 collective-permute-done.1.right
  29.2 1.8 %shard_map.116 = (f32[16,24,128]{2,1,0:T(8,128)S(1)}, f32[256,128]{1,0:T(8,128)S(1)}) custom-call(f32[512,128]{1,0:T(8,128)S(1)} %get-tuple-element.90.own, bf16[288,128]{1,0:T(8,128)(2,1)S(1)} %collective-permute-done.left, bf16[288,128]{1,0:T(8,128)(2,1)S(1)} %collective-permute-done.1.right, f32[32,128]{1,0:T(8,128)S(1)} %get-tuple-element.93.sensor, ...), custom_call_target="tpu_custom_call" | custom-call | tf_op jit(solution)/shard_map/pallas_call | solution.py:523
  30.9 12.8 %all_to_all.38.parts = f32[16,24,128]{2,1,0:T(8,128)S(1)} all-to-all(f32[16,24,128]{2,1,0:T(8,128)S(1)} %get-tuple-element.106), channel_id=1, replica_groups=mesh['depth'=16,'tile'=32] {'depth'}, dimensions={0} | all-to-all | bytes 393216 | tf_op jit(solution)/shard_map/all_to_all | solution.py:452
  43.7 0.6 shard_map.118
  44.4 17.6 %all-to-all-start.4 = ((f32[32,1,384]{2,1,0:T(1,128)}), f32[32,1,384]{2,1,0:T(1,128)S(1)}, u32[]{:S(2)}, u32[]{:S(2)}) async-start(f32[32,1,384]{2,1,0:T(1,128)} %shard_map.118), calls=%async_computation.4 | async-start | bytes 98304 | tf_op jit(solution)/shard_map/all_to_all | solution.py:452
  62.0 0.5 slice.6
  63.2 1.0 %shard_map.117 = (f32[32,1024]{1,0:T(8,128)}, f32[256,128]{1,0:T(8,128)S(1)}) custom-call(f32[16,24,128]{2,1,0:T(8,128)S(1)} %all_to_all.38.parts, bf16[256,512]{1,0:T(8,128)(2,1)S(1)} %bitcast.22, s32[256,128]{1,0:T(8,128)S(1)} %get-tuple-element.109.b_col), custom_call_target="tpu_custom_call" | custom-call | tf_op jit(solution)/shard_map/pallas_call | solution.py:558
  64.2 10.2 %all-to-all-done.4.parts = f32[32,1,384]{2,1,0:T(1,128)S(1)} async-done(((f32[32,1,384]{2,1,0:T(1,128)}), f32[32,1,384]{2,1,0:T(1,128)S(1)}, u32[]{:S(2)}, u32[]{:S(2)}) %all-to-all-start.4) | async-done | bytes 49184 | tf_op jit(solution)/shard_map/all_to_all | solution.py:452
  74.4 0.8 shard_map.119
  75.2 12.2 %all_to_all.39.parts = f32[32,4,128]{2,1,0:T(4,128)S(1)} all-to-all(f32[32,4,128]{2,1,0:T(4,128)S(1)} %get-tuple-element.124), channel_id=1, replica_groups={{0,1,32,33,64,65,96,97,128,129,160,161,192,193,224,225,256,257,288,289,..., dimensions={0} | all-to-all | bytes 131072 | tf_op jit(solution)/shard_map/all_to_all | solution.py:452
  87.4 0.1 shard_map.120
  87.5 13.8 %all_to_all.40.parts = f32[16,1,128]{2,1,0:T(1,128)S(1)} all-to-all(f32[16,1,128]{2,1,0:T(1,128)S(1)} %shard_map.120), channel_id=1, replica_groups={{0,2,4,6,8,10,12,14,16,18,20,22,24,26,28,30},{1,3,5,7,9,11,13,15,17,19,..., dimensions={0} | all-to-all | bytes 16384 | tf_op jit(solution)/shard_map/all_to_all | solution.py:452
  101.3 0.1 shard_map.121
  101.4 0.5 slice_bitcast_fusion
  (13 shorter events, 0.1 us)
Async XLA Ops:
  0.6 0.7 copy-start.6
  1.3 0.9 copy-start
  2.5 18.2 %copy-start.1 = (f32[32,1024]{1,0:T(8,128)S(1)}, f32[32,1024]{1,0:T(8,128)}, u32[]{:S(2)}) copy-start(f32[32,1024]{1,0:T(8,128)} %measured) | copy-start | bytes 393220
  20.6 3.9 %copy-start.9 = (bf16[1,256,4,128]{3,2,1,0:T(4,128)(2,1)S(1)}, bf16[1,256,4,128]{3,2,1,0:T(4,128)(2,1)}, u32[]{:S(2)}) copy-start(bf16[1,256,4,128]{3,2,1,0:T(4,128)(2,1)} %param.17) | copy-start | bytes 786436
  21.9 6.5 %collective-permute-start = (bf16[288,128]{1,0:T(8,128)(2,1)S(1)}, bf16[288,128]{1,0:T(8,128)(2,1)S(1)}, u32[]{:S(2)}, u32[]{:S(2)}) collective-permute-start(bf16[288,128]{1,0:T(8,128)(2,1)S(1)} %get-tuple-element.91), channel_id=1, source_target_pairs={{0,1},{1,2},{2,3},{3,4},{4,5},{5,6},{6,7},{7,8},{8,9},{9,10},{10,1... | collective-permute-start | bytes 221192 | tf_op jit(solution)/shard_map/ppermute | solution.py:491
  23.2 6.0 %collective-permute-start.1 = (bf16[288,128]{1,0:T(8,128)(2,1)S(1)}, bf16[288,128]{1,0:T(8,128)(2,1)S(1)}, u32[]{:S(2)}, u32[]{:S(2)}) collective-permute-start(bf16[288,128]{1,0:T(8,128)(2,1)S(1)} %get-tuple-element.92), channel_id=1, source_target_pairs={{1,0},{2,1},{3,2},{4,3},{5,4},{6,5},{7,6},{8,7},{9,8},{10,9},{11,1... | collective-permute-start | bytes 221192 | tf_op jit(solution)/shard_map/ppermute | solution.py:492
  24.5 0.8 copy-start.2
  24.6 0.8 copy-start.3
  24.6 0.8 copy-start.4
  24.6 0.8 copy-start.5
  24.6 0.8 copy-start.8
  24.7 0.7 copy-start.7
  44.4 30.0 %all-to-all-start.4 = ((f32[32,1,384]{2,1,0:T(1,128)}), f32[32,1,384]{2,1,0:T(1,128)S(1)}, u32[]{:S(2)}, u32[]{:S(2)}) async-start(f32[32,1,384]{2,1,0:T(1,128)} %shard_map.118), calls=%async_computation.4 | async-start | bytes 98304 | tf_op jit(solution)/shard_map/all_to_all | solution.py:452

commit v11 on v10

--- a/solution.py
+++ b/solution.py
@@ -69,8 +69,8 @@
 
 
 def prepare_kernel(
-    where, block, neuron, weights, owner, s_plane, s_row, s_col,
-    gram, q_row, q_col, b_col, a_row, a_lane, rank, code, first, most,
+    where, block, neuron, weights, owner, s_row,
+    gram, q_row, q_col, b_col, a_row, a_lane, most,
 ):
     foot = weights[...]
     product = lax.dot_general(foot, foot, (((1,), (1,)), ((), ())), preferred_element_type=F32)
@@ -85,8 +85,7 @@
         hit = jnp.sum(jnp.where(table == where[2] + i, number.astype(F32), 0.0), axis=0, keepdims=True)
         own = jnp.where(iota((16, CB), 0) == i, lane_sum(hit), own)
     names = jnp.concatenate([column_of(neuron[...].astype(F32)), own], axis=0).astype(I32)
-    row, col = s_row[...], s_col[...]
-    tile, window = row >> 5, col >> 6
+    tile = s_row[...] >> 5
     tables = [tile, table >> 7, table & 127]
     tables = jnp.concatenate([x.astype(F32) for x in tables], axis=1).astype(BF16)
     hot = (iota((NAMES, 64), 1) == (names[:, :64] >> 7)).astype(F32).astype(BF16)
@@ -120,6 +119,11 @@
         turn = turn + (position >= i * CAP).astype(I32)
     a_row[...] = jnp.where(names >= 0, turn * TILES + n_tile, -1)
     a_lane[...] = position - turn * CAP
+
+
+def lists_kernel(where, s_plane, s_row, s_col, rank, code, first):
+    row, col = s_row[...], s_col[...]
+    tile, window = row >> 5, col >> 6
     local = tile == where[1]
     mask = local.astype(F32)
     before = (iota((CB, CB), 0) < iota((CB, CB), 1)).astype(F32).astype(BF16)
@@ -490,36 +494,9 @@
     )(where, parts, measured)
     left = lax.ppermute(down, "tile", [(i, i + 1) for i in range(TILES - 1)])
     right = lax.ppermute(up, "tile", [(i + 1, i) for i in range(TILES - 1)])
-    weights = footprints[0].reshape(SLOTS, 512)
-    column = ((SLOTS, CB), I32)
-    names = ((NAMES, CB), I32)
+    lines = [x.reshape(64, CB) for x in (seed_plane, seed_row, seed_col)]
     square = ((64, CB), I32)
-    gram, q_row, q_col, b_col, a_row, a_lane, rank, code, first, most = call(
-        prepare_kernel,
-        [
-            ((SLOTS, SLOTS), F32),
-            ((8, SLOTS), I32),
-            column,
-            column,
-            names,
-            names,
-            square,
-            square,
-            ((8, CB), I32),
-            ((8, CB), I32),
-        ],
-        8,
-        scalars=(0,),
-    )(
-        where,
-        entry_block,
-        entry_neuron,
-        weights,
-        table,
-        seed_plane.reshape(64, CB),
-        seed_row.reshape(64, CB),
-        seed_col.reshape(64, CB),
-    )
+    rank, code, first = call(lists_kernel, [square, square, ((8, CB), I32)], 4, scalars=(0,))(where, *lines)
     sent, flat = call(
         iterate_kernel,
         [((DEPTHS, 24, CB), F32), ((256, CB), F32)],
@@ -534,7 +511,17 @@
             pltpu.VMEM((2 * DEEP, 2 * CB), BF16),
         ],
     )(own, left, right, sensor, image, ahead, behind, scale, first)
-    parts, most = lax.optimization_barrier((swap(sent, "depth"), most))
+    later = (swap(sent, "depth"), entry_block, entry_neuron, table, lines[1])
+    parts, entry_block, entry_neuron, table, seed_rows = lax.optimization_barrier(later)
+    weights = footprints[0].reshape(SLOTS, 512)
+    column = ((SLOTS, CB), I32)
+    names = ((NAMES, CB), I32)
+    gram, q_row, q_col, b_col, a_row, a_lane, most = call(
+        prepare_kernel,
+        [((SLOTS, SLOTS), F32), ((8, SLOTS), I32), column, column, names, names, ((8, CB), I32)],
+        6,
+        scalars=(0,),
+    )(where, entry_block, entry_neuron, weights, table, seed_rows)
 
     def share(values, at):
         [values] = call(gather_kernel(at), [((TILES, 1, CAP), F32)], 1)(values)

time: 102 us -> 103 us (level)
    all_to_all x1, waiting for transfers between devices: 10.2 us -> 7.17 us  [swap(): return lax.all_to_all(pieces, axis, 0, 0, axis_index_groups=groups)]
    ppermute x1, waiting for transfers between devices: 0.71 us -> 3.07 us  [body(): right = lax.ppermute(up, 'tile', [(i + 1, i) for i in range(TILES - 1)])]
    pallas_call x0 -> x1, Pallas kernels: none -> 1.54 us  [body(): call(lists_kernel, [square, square, ((8, CB), I32)], 4, scalars=(0,))]
  transfers between devices with their start and end apart: 3 -> 3, of which waited for: 2 -> 2; matrix products, arithmetic and copies ran while one was open for 1% -> 1% of each run, Pallas kernels for 4% -> 5%
where the time goes in v11:
time: 103 us
  blocking collectives  57.8 us (56%)
  starting transfers between devices  20 us (19%)
  waiting for transfers between devices  10.2 us (10%)
  Pallas kernels  9.64 us (9%)
  local copies, waits for them, and re-layouts  3.38 us (3%)
  between operations  1.47 us (1%)
    all_to_all x4, blocking collectives, swap(): return lax.all_to_all(pieces, axis, 0, 0, axis_index_groups=groups)  57.8 us
    all_to_all x1, starting transfers between devices, swap(): return lax.all_to_all(pieces, axis, 0, 0, axis_index_groups=groups)  17.4 us
    all_to_all x1, waiting for transfers between devices, swap(): return lax.all_to_all(pieces, axis, 0, 0, axis_index_groups=groups)  7.17 us
    ppermute x1, waiting for transfers between devices, body(): right = lax.ppermute(up, 'tile', [(i + 1, i) for i in range(TILES - 1)])  3.07 us
    unnamed x21, local copies, waits for them, and re-layouts  2.33 us
    pallas_call x1, Pallas kernels, body(): call(prepare_kernel, [((SLOTS, SLOTS), F32), ((8, SLOTS), I32), column, c...  2.23 us
  transfers between devices with their start and end apart: 3, of which 2 were waited for; matrix products, arithmetic and copies ran while one was open for 1% of the time, Pallas kernels for 5%

profile of v11, /device:TPU:1, one launch (start us, length us, event | category | flops | bytes accessed | tf_op | source)
XLA Modules:
  0.0 102.6 jit_solution(16784639977628730425)
XLA Ops:
  0.6 0.0 copy-start.6
  0.6 0.7 copy-done.6
  1.3 0.9 copy-done
  2.2 0.1 shard_map.113
  2.4 0.1 pad_add_fusion.where
  2.5 18.2 %all_to_all.37 = f32[16,32,128]{2,1,0:T(8,128)S(1)} all-to-all(f32[16,32,128]{2,1,0:T(8,128)S(1)} %shard_map.113), channel_id=1, replica_groups=mesh['depth'=16,'tile'=32] {'depth'}, dimensions={0} | all-to-all | bytes 524288 | tf_op jit(solution)/shard_map/all_to_all | solution.py:456
  20.6 0.0 copy-done.2
  20.6 1.3 %shard_map.114 = (f32[512,128]{1,0:T(8,128)S(1)}, f32[32,128]{1,0:T(8,128)S(1)}, bf16[288,128]{1,0:T(8,128)(2,1)S(1)}, bf16[288,128]{1,0:T(8,128)(2,1)S(1)}, bf1...) custom-call(s32[3]{0:T(128)S(1)} %pad_add_fusion.where, ...), custom_call_target="tpu_custom_call" | custom-call | tf_op jit(solution)/shard_map/pallas_call | solution.py:484
  22.0 1.3 %collective-permute-start = (bf16[288,128]{1,0:T(8,128)(2,1)S(1)}, bf16[288,128]{1,0:T(8,128)(2,1)S(1)}, u32[]{:S(2)}, u32[]{:S(2)}) collective-permute-start(bf16[288,128]{1,0:T(8,128)(2,1)S(1)} %get-tuple-element.94), channel_id=1, source_target_pairs={{0,1},{1,2},{2,3},{3,4},{4,5},{5,6},{6,7},{7,8},{8,9},{9,10},{10,1... | collective-permute-start | bytes 221192 | tf_op jit(solution)/shard_map/ppermute | solution.py:495
  23.3 1.3 %collective-permute-start.1 = (bf16[288,128]{1,0:T(8,128)(2,1)S(1)}, bf16[288,128]{1,0:T(8,128)(2,1)S(1)}, u32[]{:S(2)}, u32[]{:S(2)}) collective-permute-start(bf16[288,128]{1,0:T(8,128)(2,1)S(1)} %get-tuple-element.95), channel_id=1, source_target_pairs={{1,0},{2,1},{3,2},{4,3},{5,4},{6,5},{7,6},{8,7},{9,8},{10,9},{11,1... | collective-permute-start | bytes 221192 | tf_op jit(solution)/shard_map/ppermute | solution.py:496
  24.6 0.0 copy-done.1
  24.6 1.5 %shard_map.115 = (s32[64,128]{1,0:T(8,128)S(1)}, s32[64,128]{1,0:T(8,128)S(1)}, s32[8,128]{1,0:T(8,128)S(1)}) custom-call(s32[3]{0:T(128)S(1)} %pad_add_fusion.where, s32[64,128]{1,0:T(8,128)S(1)} %bitcast.26, s32[64,128]{1,0:T(8,128)S(1)} %bitcast.24, s32[64,128]{1,0:T(8,128)S(1)} %bitcast.27), custom_call_target="tpu_custom_call" | custom-call | tf_op jit(solution)/shard_map/pallas_call | solution.py:499
  26.1 0.0 collective-permute-done.left
  26.1 3.1 %collective-permute-done.1.right = bf16[288,128]{1,0:T(8,128)(2,1)S(1)} collective-permute-done((bf16[288,128]{1,0:T(8,128)(2,1)S(1)}, bf16[288,128]{1,0:T(8,128)(2,1)S(1)}, u32[]{:S(2)}, u32[]{:S(2)}) %collective-permute-start.1) | collective-permute-done | bytes 73760 | tf_op jit(solution)/shard_map/ppermute | solution.py:496
  29.2 1.7 %shard_map.116 = (f32[16,24,128]{2,1,0:T(8,128)S(1)}, f32[256,128]{1,0:T(8,128)S(1)}) custom-call(f32[512,128]{1,0:T(8,128)S(1)} %get-tuple-element.93.own, bf16[288,128]{1,0:T(8,128)(2,1)S(1)} %collective-permute-done.left, bf16[288,128]{1,0:T(8,128)(2,1)S(1)} %collective-permute-done.1.right, f32[32,128]{1,0:T(8,128)S(1)} %get-tuple-element.96.sensor, ...), custom_call_target="tpu_custom_call" | custom-call | tf_op jit(solution)/shard_map/pallas_call | solution.py:500
  31.0 12.8 %all_to_all.38.parts = f32[16,24,128]{2,1,0:T(8,128)S(1)} all-to-all(f32[16,24,128]{2,1,0:T(8,128)S(1)} %get-tuple-element.105), channel_id=1, replica_groups=mesh['depth'=16,'tile'=32] {'depth'}, dimensions={0} | all-to-all | bytes 393216 | tf_op jit(solution)/shard_map/all_to_all | solution.py:456
  43.8 0.6 shard_map.119
  44.4 17.4 %all-to-all-start.4 = ((f32[32,1,384]{2,1,0:T(1,128)}), f32[32,1,384]{2,1,0:T(1,128)S(1)}, u32[]{:S(2)}, u32[]{:S(2)}) async-start(f32[32,1,384]{2,1,0:T(1,128)} %shard_map.119), calls=%async_computation.4 | async-start | bytes 98304 | tf_op jit(solution)/shard_map/all_to_all | solution.py:456
  61.8 0.0 copy-start.5
  61.8 0.0 copy-start.8
  61.9 0.0 copy-start.7
  61.9 0.7 copy-done.5
  62.6 2.2 %shard_map.117 = (f32[256,256]{1,0:T(8,128)S(1)}, s32[8,256]{1,0:T(8,128)S(1)}, s32[256,128]{1,0:T(8,128)S(1)}, s32[256,128]{1,0:T(8,128)S(1)}, s32[272,128]{1,0...) custom-call(s32[3]{0:T(128)S(1)} %pad_add_fusion.where, s32[1,256]{1,0:T(1,128)S(1)} %copy-done.7, ...), custom_call_target="tpu_custom_call" | custom-call | tf_op jit(solution)/shard_map/pallas_call | solution.py:519
  64.8 0.5 slice.6
  66.0 1.0 %shard_map.118 = (f32[32,1024]{1,0:T(8,128)}, f32[256,128]{1,0:T(8,128)S(1)}) custom-call(f32[16,24,128]{2,1,0:T(8,128)S(1)} %all_to_all.38.parts, bf16[256,512]{1,0:T(8,128)(2,1)S(1)} %bitcast.22, s32[256,128]{1,0:T(8,128)S(1)} %get-tuple-element.115.b_col), custom_call_target="tpu_custom_call" | custom-call | tf_op jit(solution)/shard_map/pallas_call | solution.py:545
  67.0 7.2 %all-to-all-done.4.parts = f32[32,1,384]{2,1,0:T(1,128)S(1)} async-done(((f32[32,1,384]{2,1,0:T(1,128)}), f32[32,1,384]{2,1,0:T(1,128)S(1)}, u32[]{:S(2)}, u32[]{:S(2)}) %all-to-all-start.4) | async-done | bytes 49184 | tf_op jit(solution)/shard_map/all_to_all | solution.py:456
  74.2 0.8 shard_map.120
  75.0 12.2 %all_to_all.39.parts = f32[32,4,128]{2,1,0:T(4,128)S(1)} all-to-all(f32[32,4,128]{2,1,0:T(4,128)S(1)} %get-tuple-element.130), channel_id=1, replica_groups={{0,1,32,33,64,65,96,97,128,129,160,161,192,193,224,225,256,257,288,289,..., dimensions={0} | all-to-all | bytes 131072 | tf_op jit(solution)/shard_map/all_to_all | solution.py:456
  87.2 0.1 shard_map.121
  87.4 14.6 %all_to_all.40.parts = f32[16,1,128]{2,1,0:T(1,128)S(1)} all-to-all(f32[16,1,128]{2,1,0:T(1,128)S(1)} %shard_map.121), channel_id=1, replica_groups={{0,2,4,6,8,10,12,14,16,18,20,22,24,26,28,30},{1,3,5,7,9,11,13,15,17,19,..., dimensions={0} | all-to-all | bytes 16384 | tf_op jit(solution)/shard_map/all_to_all | solution.py:456
  102.0 0.1 shard_map.122
  102.1 0.5 slice_bitcast_fusion
  (14 shorter events, 0.1 us)
Async XLA Ops:
  0.6 0.7 copy-start.6
  1.3 0.9 copy-start
  2.5 18.2 %copy-start.2 = (f32[32,1024]{1,0:T(8,128)S(1)}, f32[32,1024]{1,0:T(8,128)}, u32[]{:S(2)}) copy-start(f32[32,1024]{1,0:T(8,128)} %measured) | copy-start | bytes 393220
  20.6 3.9 %copy-start.1 = (s32[8192]{0:T(1024)S(1)}, s32[8192]{0:T(1024)}, u32[]{:S(2)}) copy-start(s32[8192]{0:T(1024)} %param.19) | copy-start | bytes 98308
  20.6 3.9 %copy-start.3 = (s32[8192]{0:T(1024)S(1)}, s32[8192]{0:T(1024)}, u32[]{:S(2)}) copy-start(s32[8192]{0:T(1024)} %param.18) | copy-start | bytes 98308
  20.6 4.0 %copy-start.4 = (s32[8192]{0:T(1024)S(1)}, s32[8192]{0:T(1024)}, u32[]{:S(2)}) copy-start(s32[8192]{0:T(1024)} %param.20) | copy-start | bytes 98308
  22.0 4.2 %collective-permute-start = (bf16[288,128]{1,0:T(8,128)(2,1)S(1)}, bf16[288,128]{1,0:T(8,128)(2,1)S(1)}, u32[]{:S(2)}, u32[]{:S(2)}) collective-permute-start(bf16[288,128]{1,0:T(8,128)(2,1)S(1)} %get-tuple-element.94), channel_id=1, source_target_pairs={{0,1},{1,2},{2,3},{3,4},{4,5},{5,6},{6,7},{7,8},{8,9},{9,10},{10,1... | collective-permute-start | bytes 221192 | tf_op jit(solution)/shard_map/ppermute | solution.py:495
  23.3 6.0 %collective-permute-start.1 = (bf16[288,128]{1,0:T(8,128)(2,1)S(1)}, bf16[288,128]{1,0:T(8,128)(2,1)S(1)}, u32[]{:S(2)}, u32[]{:S(2)}) collective-permute-start(bf16[288,128]{1,0:T(8,128)(2,1)S(1)} %get-tuple-element.95), channel_id=1, source_target_pairs={{1,0},{2,1},{3,2},{4,3},{5,4},{6,5},{7,6},{8,7},{9,8},{10,9},{11,1... | collective-permute-start | bytes 221192 | tf_op jit(solution)/shard_map/ppermute | solution.py:496
  43.8 18.0 %copy-start.9 = (bf16[1,256,4,128]{3,2,1,0:T(4,128)(2,1)S(1)}, bf16[1,256,4,128]{3,2,1,0:T(4,128)(2,1)}, u32[]{:S(2)}) copy-start(bf16[1,256,4,128]{3,2,1,0:T(4,128)(2,1)} %param.17) | copy-start | bytes 786436
  44.4 29.8 %all-to-all-start.4 = ((f32[32,1,384]{2,1,0:T(1,128)}), f32[32,1,384]{2,1,0:T(1,128)S(1)}, u32[]{:S(2)}, u32[]{:S(2)}) async-start(f32[32,1,384]{2,1,0:T(1,128)} %shard_map.119), calls=%async_computation.4 | async-start | bytes 98304 | tf_op jit(solution)/shard_map/all_to_all | solution.py:456
  61.8 0.8 copy-start.5
  61.8 0.8 copy-start.8
  61.9 0.7 copy-start.7

commit v12 on v11

--- a/solution.py
+++ b/solution.py
@@ -97,23 +97,24 @@
     place = jnp.where(names[:SLOTS] >= 0, place, -1.0)
     q_col[...] = place.astype(I32)
     q_row[...] = jnp.transpose(place)[0:8, :].astype(I32)
-    both = jnp.zeros((TILES, 1), F32)
-    for r in range(0, 64, 8):
-        tiles = jnp.zeros((TILES, CB), F32)
-        for i in range(r, r + 8):
-            tiles = tiles + (iota((TILES, CB), 0) == tile[i : i + 1, :]).astype(F32)
-        both = both + lane_sum(tiles)
-    top = jnp.max(both, axis=0, keepdims=True)
+    held = jnp.zeros((TILES, CB), F32)
+    for r in range(64):
+        here = lane_sum((iota((TILES, CB), 0) == tile[r : r + 1, :]).astype(F32))
+        held = jnp.where(iota((TILES, CB), 1) == r, here, held)
+    top = jnp.max(lane_sum(held), axis=0, keepdims=True)
     most[...] = jnp.broadcast_to(top, (8, CB)).astype(I32)
-    wide = jnp.concatenate([both, jnp.zeros((CB - TILES, 1), F32)], axis=0)
-    held = jnp.transpose(jnp.broadcast_to(wide, (CB, CB)))[0:1, :]
-    earlier = lane_sum(jnp.where(iota((NAMES, CB), 1) < n_tile, held, 0.0))
-    keys = tile * NEURONS + number
-    high = jnp.broadcast_to(n_tile * NEURONS, (NAMES, CB)) + names
-    count = jnp.zeros((NAMES, CB), F32)
-    for r in range(64):
-        count = count + jnp.where(keys[r : r + 1, :] < high, 1.0, 0.0)
-    position = jnp.broadcast_to(lane_sum(count) - earlier, (NAMES, CB)).astype(I32)
+    before = (iota((CB, CB), 0) < iota((CB, CB), 1)).astype(F32).astype(BF16)
+    earlier = jnp.dot(held.astype(BF16), before, preferred_element_type=F32)
+    row_hot = (iota((NAMES, CB), 1) == (names >> 7)).astype(F32).astype(BF16)
+    counts = jnp.zeros((NAMES, TILES), F32)
+    for part in split2(earlier):
+        counts = counts + lax.dot_general(
+            row_hot, part, (((1,), (1,)), ((), ())), preferred_element_type=F32
+        )
+    count = lane_sum(jnp.where(iota((NAMES, TILES), 1) == n_tile, counts, 0.0))
+    inside = (found[:, :CB] == picked[0]) & (iota((NAMES, CB), 1) < (names & 127))
+    count = count + lane_sum(jnp.where(inside, 1.0, 0.0))
+    position = jnp.broadcast_to(count, (NAMES, CB)).astype(I32)
     turn = jnp.zeros((NAMES, CB), I32)
     for i in range(1, (NEURONS + CAP - 1) // CAP):
         turn = turn + (position >= i * CAP).astype(I32)

time: 103 us -> 103 us (level)
  transfers between devices with their start and end apart: 3 -> 3, of which waited for: 2 -> 2; matrix products, arithmetic and copies ran while one was open for 1% -> 1% of each run, Pallas kernels for 5% -> 4%
where the time goes in v12:
time: 103 us; the launch traced here: 102 us
  blocking collectives  57.3 us (56%)
  starting transfers between devices  20 us (19%)
  waiting for transfers between devices  10.7 us (10%)
  Pallas kernels  9.21 us (9%)
  local copies, waits for them, and re-layouts  3.38 us (3%)
  between operations  1.47 us (1%)
    all_to_all x4, blocking collectives, swap(): return lax.all_to_all(pieces, axis, 0, 0, axis_index_groups=groups)  57.3 us
    all_to_all x1, starting transfers between devices, swap(): return lax.all_to_all(pieces, axis, 0, 0, axis_index_groups=groups)  17.4 us
    all_to_all x1, waiting for transfers between devices, swap(): return lax.all_to_all(pieces, axis, 0, 0, axis_index_groups=groups)  7.6 us
    ppermute x1, waiting for transfers between devices, body(): right = lax.ppermute(up, 'tile', [(i + 1, i) for i in range(TILES - 1)])  3.07 us
    unnamed x21, local copies, waits for them, and re-layouts  2.33 us
  transfers between devices with their start and end apart: 3, of which 2 were waited for; matrix products, arithmetic and copies ran while one was open for 1% of the time, Pallas kernels for 4%

profile of v12, /device:TPU:1, one launch (start us, length us, event | category | flops | bytes accessed | tf_op | source)
XLA Modules:
  0.0 102.2 jit_solution(7245430921779442810)
XLA Ops:
  0.6 0.0 copy-start.6
  0.6 0.7 copy-done.6
  1.3 0.9 copy-done
  2.2 0.1 shard_map.113
  2.4 0.1 pad_add_fusion.where
  2.5 18.2 %all_to_all.37 = f32[16,32,128]{2,1,0:T(8,128)S(1)} all-to-all(f32[16,32,128]{2,1,0:T(8,128)S(1)} %shard_map.113), channel_id=1, replica_groups=mesh['depth'=16,'tile'=32] {'depth'}, dimensions={0} | all-to-all | bytes 524288 | tf_op jit(solution)/shard_map/all_to_all | solution.py:457
  20.6 0.0 copy-done.2
  20.6 1.3 %shard_map.114 = (f32[512,128]{1,0:T(8,128)S(1)}, f32[32,128]{1,0:T(8,128)S(1)}, bf16[288,128]{1,0:T(8,128)(2,1)S(1)}, bf16[288,128]{1,0:T(8,128)(2,1)S(1)}, bf1...) custom-call(s32[3]{0:T(128)S(1)} %pad_add_fusion.where, ...), custom_call_target="tpu_custom_call" | custom-call | tf_op jit(solution)/shard_map/pallas_call | solution.py:485
  22.0 1.3 %collective-permute-start = (bf16[288,128]{1,0:T(8,128)(2,1)S(1)}, bf16[288,128]{1,0:T(8,128)(2,1)S(1)}, u32[]{:S(2)}, u32[]{:S(2)}) collective-permute-start(bf16[288,128]{1,0:T(8,128)(2,1)S(1)} %get-tuple-element.94), channel_id=1, source_target_pairs={{0,1},{1,2},{2,3},{3,4},{4,5},{5,6},{6,7},{7,8},{8,9},{9,10},{10,1... | collective-permute-start | bytes 221192 | tf_op jit(solution)/shard_map/ppermute | solution.py:496
  23.3 1.3 %collective-permute-start.1 = (bf16[288,128]{1,0:T(8,128)(2,1)S(1)}, bf16[288,128]{1,0:T(8,128)(2,1)S(1)}, u32[]{:S(2)}, u32[]{:S(2)}) collective-permute-start(bf16[288,128]{1,0:T(8,128)(2,1)S(1)} %get-tuple-element.95), channel_id=1, source_target_pairs={{1,0},{2,1},{3,2},{4,3},{5,4},{6,5},{7,6},{8,7},{9,8},{10,9},{11,1... | collective-permute-start | bytes 221192 | tf_op jit(solution)/shard_map/ppermute | solution.py:497
  24.6 0.0 copy-done.1
  24.6 1.5 %shard_map.115 = (s32[64,128]{1,0:T(8,128)S(1)}, s32[64,128]{1,0:T(8,128)S(1)}, s32[8,128]{1,0:T(8,128)S(1)}) custom-call(s32[3]{0:T(128)S(1)} %pad_add_fusion.where, s32[64,128]{1,0:T(8,128)S(1)} %bitcast.26, s32[64,128]{1,0:T(8,128)S(1)} %bitcast.24, s32[64,128]{1,0:T(8,128)S(1)} %bitcast.27), custom_call_target="tpu_custom_call" | custom-call | tf_op jit(solution)/shard_map/pallas_call | solution.py:500
  26.1 0.0 collective-permute-done.left
  26.1 3.1 %collective-permute-done.1.right = bf16[288,128]{1,0:T(8,128)(2,1)S(1)} collective-permute-done((bf16[288,128]{1,0:T(8,128)(2,1)S(1)}, bf16[288,128]{1,0:T(8,128)(2,1)S(1)}, u32[]{:S(2)}, u32[]{:S(2)}) %collective-permute-start.1) | collective-permute-done | bytes 73760 | tf_op jit(solution)/shard_map/ppermute | solution.py:497
  29.2 1.7 %shard_map.116 = (f32[16,24,128]{2,1,0:T(8,128)S(1)}, f32[256,128]{1,0:T(8,128)S(1)}) custom-call(f32[512,128]{1,0:T(8,128)S(1)} %get-tuple-element.93.own, bf16[288,128]{1,0:T(8,128)(2,1)S(1)} %collective-permute-done.left, bf16[288,128]{1,0:T(8,128)(2,1)S(1)} %collective-permute-done.1.right, f32[32,128]{1,0:T(8,128)S(1)} %get-tuple-element.96.sensor, ...), custom_call_target="tpu_custom_call" | custom-call | tf_op jit(solution)/shard_map/pallas_call | solution.py:501
  31.0 12.8 %all_to_all.38.parts = f32[16,24,128]{2,1,0:T(8,128)S(1)} all-to-all(f32[16,24,128]{2,1,0:T(8,128)S(1)} %get-tuple-element.105), channel_id=1, replica_groups=mesh['depth'=16,'tile'=32] {'depth'}, dimensions={0} | all-to-all | bytes 393216 | tf_op jit(solution)/shard_map/all_to_all | solution.py:457
  43.8 0.6 shard_map.119
  44.4 17.4 %all-to-all-start.4 = ((f32[32,1,384]{2,1,0:T(1,128)}), f32[32,1,384]{2,1,0:T(1,128)S(1)}, u32[]{:S(2)}, u32[]{:S(2)}) async-start(f32[32,1,384]{2,1,0:T(1,128)} %shard_map.119), calls=%async_computation.4 | async-start | bytes 98304 | tf_op jit(solution)/shard_map/all_to_all | solution.py:457
  61.8 0.0 copy-start.5
  61.8 0.0 copy-start.8
  61.9 0.0 copy-start.7
  61.9 0.7 copy-done.5
  62.6 1.8 %shard_map.117 = (f32[256,256]{1,0:T(8,128)S(1)}, s32[8,256]{1,0:T(8,128)S(1)}, s32[256,128]{1,0:T(8,128)S(1)}, s32[256,128]{1,0:T(8,128)S(1)}, s32[272,128]{1,0...) custom-call(s32[3]{0:T(128)S(1)} %pad_add_fusion.where, s32[1,256]{1,0:T(1,128)S(1)} %copy-done.7, ...), custom_call_target="tpu_custom_call" | custom-call | tf_op jit(solution)/shard_map/pallas_call | solution.py:520
  64.4 0.5 slice.6
  65.6 1.0 %shard_map.118 = (f32[32,1024]{1,0:T(8,128)}, f32[256,128]{1,0:T(8,128)S(1)}) custom-call(f32[16,24,128]{2,1,0:T(8,128)S(1)} %all_to_all.38.parts, bf16[256,512]{1,0:T(8,128)(2,1)S(1)} %bitcast.22, s32[256,128]{1,0:T(8,128)S(1)} %get-tuple-element.115.b_col), custom_call_target="tpu_custom_call" | custom-call | tf_op jit(solution)/shard_map/pallas_call | solution.py:546
  66.6 7.6 %all-to-all-done.4.parts = f32[32,1,384]{2,1,0:T(1,128)S(1)} async-done(((f32[32,1,384]{2,1,0:T(1,128)}), f32[32,1,384]{2,1,0:T(1,128)S(1)}, u32[]{:S(2)}, u32[]{:S(2)}) %all-to-all-start.4) | async-done | bytes 49184 | tf_op jit(solution)/shard_map/all_to_all | solution.py:457
  74.2 0.8 shard_map.120
  75.0 12.2 %all_to_all.39.parts = f32[32,4,128]{2,1,0:T(4,128)S(1)} all-to-all(f32[32,4,128]{2,1,0:T(4,128)S(1)} %get-tuple-element.130), channel_id=1, replica_groups={{0,1,32,33,64,65,96,97,128,129,160,161,192,193,224,225,256,257,288,289,..., dimensions={0} | all-to-all | bytes 131072 | tf_op jit(solution)/shard_map/all_to_all | solution.py:457
  87.2 0.1 shard_map.121
  87.4 14.2 %all_to_all.40.parts = f32[16,1,128]{2,1,0:T(1,128)S(1)} all-to-all(f32[16,1,128]{2,1,0:T(1,128)S(1)} %shard_map.121), channel_id=1, replica_groups={{0,2,4,6,8,10,12,14,16,18,20,22,24,26,28,30},{1,3,5,7,9,11,13,15,17,19,..., dimensions={0} | all-to-all | bytes 16384 | tf_op jit(solution)/shard_map/all_to_all | solution.py:457
  101.5 0.1 shard_map.122
  101.6 0.5 slice_bitcast_fusion
  (14 shorter events, 0.1 us)
Async XLA Ops:
  0.6 0.7 copy-start.6
  1.3 0.9 copy-start
  2.5 18.2 %copy-start.2 = (f32[32,1024]{1,0:T(8,128)S(1)}, f32[32,1024]{1,0:T(8,128)}, u32[]{:S(2)}) copy-start(f32[32,1024]{1,0:T(8,128)} %measured) | copy-start | bytes 393220
  20.6 3.9 %copy-start.1 = (s32[8192]{0:T(1024)S(1)}, s32[8192]{0:T(1024)}, u32[]{:S(2)}) copy-start(s32[8192]{0:T(1024)} %param.19) | copy-start | bytes 98308
  20.6 3.9 %copy-start.3 = (s32[8192]{0:T(1024)S(1)}, s32[8192]{0:T(1024)}, u32[]{:S(2)}) copy-start(s32[8192]{0:T(1024)} %param.18) | copy-start | bytes 98308
  20.6 4.0 %copy-start.4 = (s32[8192]{0:T(1024)S(1)}, s32[8192]{0:T(1024)}, u32[]{:S(2)}) copy-start(s32[8192]{0:T(1024)} %param.20) | copy-start | bytes 98308
  22.0 4.2 %collective-permute-start = (bf16[288,128]{1,0:T(8,128)(2,1)S(1)}, bf16[288,128]{1,0:T(8,128)(2,1)S(1)}, u32[]{:S(2)}, u32[]{:S(2)}) collective-permute-start(bf16[288,128]{1,0:T(8,128)(2,1)S(1)} %get-tuple-element.94), channel_id=1, source_target_pairs={{0,1},{1,2},{2,3},{3,4},{4,5},{5,6},{6,7},{7,8},{8,9},{9,10},{10,1... | collective-permute-start | bytes 221192 | tf_op jit(solution)/shard_map/ppermute | solution.py:496
  23.3 6.0 %collective-permute-start.1 = (bf16[288,128]{1,0:T(8,128)(2,1)S(1)}, bf16[288,128]{1,0:T(8,128)(2,1)S(1)}, u32[]{:S(2)}, u32[]{:S(2)}) collective-permute-start(bf16[288,128]{1,0:T(8,128)(2,1)S(1)} %get-tuple-element.95), channel_id=1, source_target_pairs={{1,0},{2,1},{3,2},{4,3},{5,4},{6,5},{7,6},{8,7},{9,8},{10,9},{11,1... | collective-permute-start | bytes 221192 | tf_op jit(solution)/shard_map/ppermute | solution.py:497
  43.8 18.0 %copy-start.9 = (bf16[1,256,4,128]{3,2,1,0:T(4,128)(2,1)S(1)}, bf16[1,256,4,128]{3,2,1,0:T(4,128)(2,1)}, u32[]{:S(2)}) copy-start(bf16[1,256,4,128]{3,2,1,0:T(4,128)(2,1)} %param.17) | copy-start | bytes 786436
  44.4 29.8 %all-to-all-start.4 = ((f32[32,1,384]{2,1,0:T(1,128)}), f32[32,1,384]{2,1,0:T(1,128)S(1)}, u32[]{:S(2)}, u32[]{:S(2)}) async-start(f32[32,1,384]{2,1,0:T(1,128)} %shard_map.119), calls=%async_computation.4 | async-start | bytes 98304 | tf_op jit(solution)/shard_map/all_to_all | solution.py:457
  61.8 0.8 copy-start.5
  61.8 0.8 copy-start.8
  61.9 0.7 copy-start.7

commit v13 on v12

--- a/solution.py
+++ b/solution.py
@@ -102,7 +102,10 @@
         here = lane_sum((iota((TILES, CB), 0) == tile[r : r + 1, :]).astype(F32))
         held = jnp.where(iota((TILES, CB), 1) == r, here, held)
     top = jnp.max(lane_sum(held), axis=0, keepdims=True)
-    most[...] = jnp.broadcast_to(top, (8, CB)).astype(I32)
+    turns = jnp.zeros((1, 1), I32)
+    for i in range((NEURONS + CAP - 1) // CAP):
+        turns = turns + (top > i * CAP).astype(I32)
+    most[...] = jnp.broadcast_to(turns, (8, CB))
     before = (iota((CB, CB), 0) < iota((CB, CB), 1)).astype(F32).astype(BF16)
     earlier = jnp.dot(held.astype(BF16), before, preferred_element_type=F32)
     row_hot = (iota((NAMES, CB), 1) == (names >> 7)).astype(F32).astype(BF16)
@@ -540,9 +543,8 @@
         )
         return look(turn, share(swap(values, "depth"), 0), known)
 
-    rounds = (most[0, 0] + CAP - 1) // CAP
     shared, none = lax.optimization_barrier((share(parts, 16), jnp.zeros((NAMES, CB), F32)))
-    known = lax.fori_loop(1, rounds, another, none)
+    known = lax.fori_loop(1, most[0, 0], another, none)
     estimate, proj = call(
         home_kernel,
         [((ROWS, COLS), F32), ((SLOTS, CB), F32)],

time: 103 us -> 103 us (level)
  no operation moved by 1% of the time
where the time goes in v13:
time: 103 us; the launch traced here: 102 us
  blocking collectives  57 us (55%)
  starting transfers between devices  20 us (19%)
  waiting for transfers between devices  11.3 us (11%)
  Pallas kernels  9.2 us (9%)
  local copies, waits for them, and re-layouts  3.46 us (3%)
    all_to_all x4, blocking collectives, swap(): return lax.all_to_all(pieces, axis, 0, 0, axis_index_groups=groups)  57 us
    all_to_all x1, starting transfers between devices, swap(): return lax.all_to_all(pieces, axis, 0, 0, axis_index_groups=groups)  17.4 us
    all_to_all x1, waiting for transfers between devices, swap(): return lax.all_to_all(pieces, axis, 0, 0, axis_index_groups=groups)  8.19 us
    ppermute x1, waiting for transfers between devices, body(): right = lax.ppermute(up, 'tile', [(i + 1, i) for i in range(TILES - 1)])  3.07 us
    unnamed x21, local copies, waits for them, and re-layouts  2.33 us
  transfers between devices with their start and end apart: 3, of which 2 were waited for; matrix products, arithmetic and copies ran while one was open for 1% of the time, Pallas kernels for 4%

profile of v13, /device:TPU:1, one launch (start us, length us, event | category | flops | bytes accessed | tf_op | source)
XLA Modules:
  0.0 102.5 jit_solution(3920245022801300742)
XLA Ops:
  0.6 0.7 copy-done.6
  1.3 0.9 copy-done
  2.2 0.1 shard_map.113
  2.4 0.1 pad_add_fusion.where
  2.5 18.2 %all_to_all.37 = f32[16,32,128]{2,1,0:T(8,128)S(1)} all-to-all(f32[16,32,128]{2,1,0:T(8,128)S(1)} %shard_map.113), channel_id=1, replica_groups=mesh['depth'=16,'tile'=32] {'depth'}, dimensions={0} | all-to-all | bytes 524288 | tf_op jit(solution)/shard_map/all_to_all | solution.py:460
  20.6 0.0 copy-done.2
  20.6 1.3 %shard_map.114 = (f32[512,128]{1,0:T(8,128)S(1)}, f32[32,128]{1,0:T(8,128)S(1)}, bf16[288,128]{1,0:T(8,128)(2,1)S(1)}, bf16[288,128]{1,0:T(8,128)(2,1)S(1)}, bf1...) custom-call(s32[3]{0:T(128)S(1)} %pad_add_fusion.where, ...), custom_call_target="tpu_custom_call" | custom-call | tf_op jit(solution)/shard_map/pallas_call | solution.py:488
  22.0 1.3 %collective-permute-start = (bf16[288,128]{1,0:T(8,128)(2,1)S(1)}, bf16[288,128]{1,0:T(8,128)(2,1)S(1)}, u32[]{:S(2)}, u32[]{:S(2)}) collective-permute-start(bf16[288,128]{1,0:T(8,128)(2,1)S(1)} %get-tuple-element.94), channel_id=1, source_target_pairs={{0,1},{1,2},{2,3},{3,4},{4,5},{5,6},{6,7},{7,8},{8,9},{9,10},{10,1... | collective-permute-start | bytes 221192 | tf_op jit(solution)/shard_map/ppermute | solution.py:499
  23.3 1.3 %collective-permute-start.1 = (bf16[288,128]{1,0:T(8,128)(2,1)S(1)}, bf16[288,128]{1,0:T(8,128)(2,1)S(1)}, u32[]{:S(2)}, u32[]{:S(2)}) collective-permute-start(bf16[288,128]{1,0:T(8,128)(2,1)S(1)} %get-tuple-element.95), channel_id=1, source_target_pairs={{1,0},{2,1},{3,2},{4,3},{5,4},{6,5},{7,6},{8,7},{9,8},{10,9},{11,1... | collective-permute-start | bytes 221192 | tf_op jit(solution)/shard_map/ppermute | solution.py:500
  24.6 1.5 %shard_map.115 = (s32[64,128]{1,0:T(8,128)S(1)}, s32[64,128]{1,0:T(8,128)S(1)}, s32[8,128]{1,0:T(8,128)S(1)}) custom-call(s32[3]{0:T(128)S(1)} %pad_add_fusion.where, s32[64,128]{1,0:T(8,128)S(1)} %bitcast.25, s32[64,128]{1,0:T(8,128)S(1)} %bitcast.23, s32[64,128]{1,0:T(8,128)S(1)} %bitcast.26), custom_call_target="tpu_custom_call" | custom-call | tf_op jit(solution)/shard_map/pallas_call | solution.py:503
  26.1 0.0 collective-permute-done.left
  26.1 3.1 %collective-permute-done.1.right = bf16[288,128]{1,0:T(8,128)(2,1)S(1)} collective-permute-done((bf16[288,128]{1,0:T(8,128)(2,1)S(1)}, bf16[288,128]{1,0:T(8,128)(2,1)S(1)}, u32[]{:S(2)}, u32[]{:S(2)}) %collective-permute-start.1) | collective-permute-done | bytes 73760 | tf_op jit(solution)/shard_map/ppermute | solution.py:500
  29.2 1.7 %shard_map.116 = (f32[16,24,128]{2,1,0:T(8,128)S(1)}, f32[256,128]{1,0:T(8,128)S(1)}) custom-call(f32[512,128]{1,0:T(8,128)S(1)} %get-tuple-element.93.own, bf16[288,128]{1,0:T(8,128)(2,1)S(1)} %collective-permute-done.left, bf16[288,128]{1,0:T(8,128)(2,1)S(1)} %collective-permute-done.1.right, f32[32,128]{1,0:T(8,128)S(1)} %get-tuple-element.96.sensor, ...), custom_call_target="tpu_custom_call" | custom-call | tf_op jit(solution)/shard_map/pallas_call | solution.py:504
  31.0 12.8 %all_to_all.38.parts = f32[16,24,128]{2,1,0:T(8,128)S(1)} all-to-all(f32[16,24,128]{2,1,0:T(8,128)S(1)} %get-tuple-element.105), channel_id=1, replica_groups=mesh['depth'=16,'tile'=32] {'depth'}, dimensions={0} | all-to-all | bytes 393216 | tf_op jit(solution)/shard_map/all_to_all | solution.py:460
  43.8 0.6 shard_map.119
  44.4 17.4 %all-to-all-start.4 = ((f32[32,1,384]{2,1,0:T(1,128)}), f32[32,1,384]{2,1,0:T(1,128)S(1)}, u32[]{:S(2)}, u32[]{:S(2)}) async-start(f32[32,1,384]{2,1,0:T(1,128)} %shard_map.119), calls=%async_computation.4 | async-start | bytes 98304 | tf_op jit(solution)/shard_map/all_to_all | solution.py:460
  61.8 0.0 copy-start.5
  61.8 0.0 copy-start.8
  61.9 0.0 copy-start.7
  61.9 0.7 copy-done.5
  62.6 0.0 copy-done.7
  62.6 1.8 %shard_map.117 = (f32[256,256]{1,0:T(8,128)S(1)}, s32[8,256]{1,0:T(8,128)S(1)}, s32[256,128]{1,0:T(8,128)S(1)}, s32[256,128]{1,0:T(8,128)S(1)}, s32[272,128]{1,0...) custom-call(s32[3]{0:T(128)S(1)} %pad_add_fusion.where, s32[1,256]{1,0:T(1,128)S(1)} %copy-done.7, ...), custom_call_target="tpu_custom_call" | custom-call | tf_op jit(solution)/shard_map/pallas_call | solution.py:523
  64.4 1.0 %shard_map.118 = (f32[32,1024]{1,0:T(8,128)}, f32[256,128]{1,0:T(8,128)S(1)}) custom-call(f32[16,24,128]{2,1,0:T(8,128)S(1)} %all_to_all.38.parts, bf16[256,512]{1,0:T(8,128)(2,1)S(1)} %bitcast.21, s32[256,128]{1,0:T(8,128)S(1)} %get-tuple-element.115.b_col), custom_call_target="tpu_custom_call" | custom-call | tf_op jit(solution)/shard_map/pallas_call | solution.py:548
  65.4 0.6 slice.6
  66.0 8.2 %all-to-all-done.4.parts = f32[32,1,384]{2,1,0:T(1,128)S(1)} async-done(((f32[32,1,384]{2,1,0:T(1,128)}), f32[32,1,384]{2,1,0:T(1,128)S(1)}, u32[]{:S(2)}, u32[]{:S(2)}) %all-to-all-start.4) | async-done | bytes 49184 | tf_op jit(solution)/shard_map/all_to_all | solution.py:460
  74.2 0.7 while.10
  74.9 0.8 shard_map.120
  75.7 12.2 %all_to_all.39.parts = f32[32,4,128]{2,1,0:T(4,128)S(1)} all-to-all(f32[32,4,128]{2,1,0:T(4,128)S(1)} %get-tuple-element.130), channel_id=1, replica_groups={{0,1,32,33,64,65,96,97,128,129,160,161,192,193,224,225,256,257,288,289,..., dimensions={0} | all-to-all | bytes 131072 | tf_op jit(solution)/shard_map/all_to_all | solution.py:460
  87.9 0.1 shard_map.121
  88.0 13.8 %all_to_all.40.parts = f32[16,1,128]{2,1,0:T(1,128)S(1)} all-to-all(f32[16,1,128]{2,1,0:T(1,128)S(1)} %shard_map.121), channel_id=1, replica_groups={{0,2,4,6,8,10,12,14,16,18,20,22,24,26,28,30},{1,3,5,7,9,11,13,15,17,19,..., dimensions={0} | all-to-all | bytes 16384 | tf_op jit(solution)/shard_map/all_to_all | solution.py:460
  101.9 0.1 shard_map.122
  101.9 0.5 slice_bitcast_fusion
  (14 shorter events, 0.1 us)
Async XLA Ops:
  0.6 0.7 copy-start.6
  1.3 0.9 copy-start
  2.5 18.2 %copy-start.2 = (f32[32,1024]{1,0:T(8,128)S(1)}, f32[32,1024]{1,0:T(8,128)}, u32[]{:S(2)}) copy-start(f32[32,1024]{1,0:T(8,128)} %measured) | copy-start | bytes 393220
  20.6 3.9 %copy-start.1 = (s32[8192]{0:T(1024)S(1)}, s32[8192]{0:T(1024)}, u32[]{:S(2)}) copy-start(s32[8192]{0:T(1024)} %param.19) | copy-start | bytes 98308
  20.6 3.9 %copy-start.3 = (s32[8192]{0:T(1024)S(1)}, s32[8192]{0:T(1024)}, u32[]{:S(2)}) copy-start(s32[8192]{0:T(1024)} %param.18) | copy-start | bytes 98308
  20.6 4.0 %copy-start.4 = (s32[8192]{0:T(1024)S(1)}, s32[8192]{0:T(1024)}, u32[]{:S(2)}) copy-start(s32[8192]{0:T(1024)} %param.20) | copy-start | bytes 98308
  22.0 4.2 %collective-permute-start = (bf16[288,128]{1,0:T(8,128)(2,1)S(1)}, bf16[288,128]{1,0:T(8,128)(2,1)S(1)}, u32[]{:S(2)}, u32[]{:S(2)}) collective-permute-start(bf16[288,128]{1,0:T(8,128)(2,1)S(1)} %get-tuple-element.94), channel_id=1, source_target_pairs={{0,1},{1,2},{2,3},{3,4},{4,5},{5,6},{6,7},{7,8},{8,9},{9,10},{10,1... | collective-permute-start | bytes 221192 | tf_op jit(solution)/shard_map/ppermute | solution.py:499
  23.3 6.0 %collective-permute-start.1 = (bf16[288,128]{1,0:T(8,128)(2,1)S(1)}, bf16[288,128]{1,0:T(8,128)(2,1)S(1)}, u32[]{:S(2)}, u32[]{:S(2)}) collective-permute-start(bf16[288,128]{1,0:T(8,128)(2,1)S(1)} %get-tuple-element.95), channel_id=1, source_target_pairs={{1,0},{2,1},{3,2},{4,3},{5,4},{6,5},{7,6},{8,7},{9,8},{10,9},{11,1... | collective-permute-start | bytes 221192 | tf_op jit(solution)/shard_map/ppermute | solution.py:500
  43.8 18.0 %copy-start.9 = (bf16[1,256,4,128]{3,2,1,0:T(4,128)(2,1)S(1)}, bf16[1,256,4,128]{3,2,1,0:T(4,128)(2,1)}, u32[]{:S(2)}) copy-start(bf16[1,256,4,128]{3,2,1,0:T(4,128)(2,1)} %param.17) | copy-start | bytes 786436
  44.4 29.8 %all-to-all-start.4 = ((f32[32,1,384]{2,1,0:T(1,128)}), f32[32,1,384]{2,1,0:T(1,128)S(1)}, u32[]{:S(2)}, u32[]{:S(2)}) async-start(f32[32,1,384]{2,1,0:T(1,128)} %shard_map.119), calls=%async_computation.4 | async-start | bytes 98304 | tf_op jit(solution)/shard_map/all_to_all | solution.py:460
  61.8 0.8 copy-start.5
  61.8 0.8 copy-start.8
  61.9 0.7 copy-start.7

commit v14 on v13

--- a/solution.py
+++ b/solution.py
@@ -543,8 +543,9 @@
         )
         return look(turn, share(swap(values, "depth"), 0), known)
 
+    rounds = jnp.minimum(most[0, 0], (NEURONS + CAP - 1) // CAP)
     shared, none = lax.optimization_barrier((share(parts, 16), jnp.zeros((NAMES, CB), F32)))
-    known = lax.fori_loop(1, most[0, 0], another, none)
+    known = lax.fori_loop(1, rounds, another, none)
     estimate, proj = call(
         home_kernel,
         [((ROWS, COLS), F32), ((SLOTS, CB), F32)],

time: 103 us -> 103 us (level)
  no operation moved by 1% of the time
where the time goes in v14:
time: 103 us; the launch traced here: 102 us
  blocking collectives  57.3 us (56%)
  starting transfers between devices  20 us (19%)
  waiting for transfers between devices  10.8 us (10%)
  Pallas kernels  9.2 us (9%)
  local copies, waits for them, and re-layouts  3.38 us (3%)
  between operations  1.39 us (1%)
    all_to_all x4, blocking collectives, swap(): return lax.all_to_all(pieces, axis, 0, 0, axis_index_groups=groups)  57.3 us
    all_to_all x1, starting transfers between devices, swap(): return lax.all_to_all(pieces, axis, 0, 0, axis_index_groups=groups)  17.4 us
    all_to_all x1, waiting for transfers between devices, swap(): return lax.all_to_all(pieces, axis, 0, 0, axis_index_groups=groups)  7.69 us
    ppermute x1, waiting for transfers between devices, body(): right = lax.ppermute(up, 'tile', [(i + 1, i) for i in range(TILES - 1)])  3.07 us
    unnamed x21, local copies, waits for them, and re-layouts  2.33 us
  transfers between devices with their start and end apart: 3, of which 2 were waited for; matrix products, arithmetic and copies ran while one was open for 1% of the time, Pallas kernels for 4%

profile of v14, /device:TPU:1, one launch (start us, length us, event | category | flops | bytes accessed | tf_op | source)
XLA Modules:
  0.0 102.1 jit_solution(1450609294334522559)
XLA Ops:
  0.6 0.0 copy-start.6
  0.6 0.7 copy-done.6
  1.3 0.9 copy-done
  2.2 0.1 shard_map.113
  2.4 0.1 pad_add_fusion.where
  2.5 18.2 %all_to_all.37 = f32[16,32,128]{2,1,0:T(8,128)S(1)} all-to-all(f32[16,32,128]{2,1,0:T(8,128)S(1)} %shard_map.113), channel_id=1, replica_groups=mesh['depth'=16,'tile'=32] {'depth'}, dimensions={0} | all-to-all | bytes 524288 | tf_op jit(solution)/shard_map/all_to_all | solution.py:460
  20.6 0.0 copy-done.2
  20.6 1.3 %shard_map.114 = (f32[512,128]{1,0:T(8,128)S(1)}, f32[32,128]{1,0:T(8,128)S(1)}, bf16[288,128]{1,0:T(8,128)(2,1)S(1)}, bf16[288,128]{1,0:T(8,128)(2,1)S(1)}, bf1...) custom-call(s32[3]{0:T(128)S(1)} %pad_add_fusion.where, ...), custom_call_target="tpu_custom_call" | custom-call | tf_op jit(solution)/shard_map/pallas_call | solution.py:488
  22.0 1.3 %collective-permute-start = (bf16[288,128]{1,0:T(8,128)(2,1)S(1)}, bf16[288,128]{1,0:T(8,128)(2,1)S(1)}, u32[]{:S(2)}, u32[]{:S(2)}) collective-permute-start(bf16[288,128]{1,0:T(8,128)(2,1)S(1)} %get-tuple-element.94), channel_id=1, source_target_pairs={{0,1},{1,2},{2,3},{3,4},{4,5},{5,6},{6,7},{7,8},{8,9},{9,10},{10,1... | collective-permute-start | bytes 221192 | tf_op jit(solution)/shard_map/ppermute | solution.py:499
  23.3 1.3 %collective-permute-start.1 = (bf16[288,128]{1,0:T(8,128)(2,1)S(1)}, bf16[288,128]{1,0:T(8,128)(2,1)S(1)}, u32[]{:S(2)}, u32[]{:S(2)}) collective-permute-start(bf16[288,128]{1,0:T(8,128)(2,1)S(1)} %get-tuple-element.95), channel_id=1, source_target_pairs={{1,0},{2,1},{3,2},{4,3},{5,4},{6,5},{7,6},{8,7},{9,8},{10,9},{11,1... | collective-permute-start | bytes 221192 | tf_op jit(solution)/shard_map/ppermute | solution.py:500
  24.6 1.5 %shard_map.115 = (s32[64,128]{1,0:T(8,128)S(1)}, s32[64,128]{1,0:T(8,128)S(1)}, s32[8,128]{1,0:T(8,128)S(1)}) custom-call(s32[3]{0:T(128)S(1)} %pad_add_fusion.where, s32[64,128]{1,0:T(8,128)S(1)} %bitcast.25, s32[64,128]{1,0:T(8,128)S(1)} %bitcast.23, s32[64,128]{1,0:T(8,128)S(1)} %bitcast.26), custom_call_target="tpu_custom_call" | custom-call | tf_op jit(solution)/shard_map/pallas_call | solution.py:503
  26.1 0.0 collective-permute-done.left
  26.1 3.1 %collective-permute-done.1.right = bf16[288,128]{1,0:T(8,128)(2,1)S(1)} collective-permute-done((bf16[288,128]{1,0:T(8,128)(2,1)S(1)}, bf16[288,128]{1,0:T(8,128)(2,1)S(1)}, u32[]{:S(2)}, u32[]{:S(2)}) %collective-permute-start.1) | collective-permute-done | bytes 73760 | tf_op jit(solution)/shard_map/ppermute | solution.py:500
  29.2 1.7 %shard_map.116 = (f32[16,24,128]{2,1,0:T(8,128)S(1)}, f32[256,128]{1,0:T(8,128)S(1)}) custom-call(f32[512,128]{1,0:T(8,128)S(1)} %get-tuple-element.93.own, bf16[288,128]{1,0:T(8,128)(2,1)S(1)} %collective-permute-done.left, bf16[288,128]{1,0:T(8,128)(2,1)S(1)} %collective-permute-done.1.right, f32[32,128]{1,0:T(8,128)S(1)} %get-tuple-element.96.sensor, ...), custom_call_target="tpu_custom_call" | custom-call | tf_op jit(solution)/shard_map/pallas_call | solution.py:504
  31.0 12.8 %all_to_all.38.parts = f32[16,24,128]{2,1,0:T(8,128)S(1)} all-to-all(f32[16,24,128]{2,1,0:T(8,128)S(1)} %get-tuple-element.105), channel_id=1, replica_groups=mesh['depth'=16,'tile'=32] {'depth'}, dimensions={0} | all-to-all | bytes 393216 | tf_op jit(solution)/shard_map/all_to_all | solution.py:460
  43.8 0.6 shard_map.119
  44.4 17.4 %all-to-all-start.4 = ((f32[32,1,384]{2,1,0:T(1,128)}), f32[32,1,384]{2,1,0:T(1,128)S(1)}, u32[]{:S(2)}, u32[]{:S(2)}) async-start(f32[32,1,384]{2,1,0:T(1,128)} %shard_map.119), calls=%async_computation.4 | async-start | bytes 98304 | tf_op jit(solution)/shard_map/all_to_all | solution.py:460
  61.8 0.0 copy-start.5
  61.8 0.0 copy-start.8
  61.9 0.0 copy-start.7
  61.9 0.7 copy-done.5
  62.6 0.0 copy-done.7
  62.6 1.8 %shard_map.117 = (f32[256,256]{1,0:T(8,128)S(1)}, s32[8,256]{1,0:T(8,128)S(1)}, s32[256,128]{1,0:T(8,128)S(1)}, s32[256,128]{1,0:T(8,128)S(1)}, s32[272,128]{1,0...) custom-call(s32[3]{0:T(128)S(1)} %pad_add_fusion.where, s32[1,256]{1,0:T(1,128)S(1)} %copy-done.7, ...), custom_call_target="tpu_custom_call" | custom-call | tf_op jit(solution)/shard_map/pallas_call | solution.py:523
  64.4 1.0 %shard_map.118 = (f32[32,1024]{1,0:T(8,128)}, f32[256,128]{1,0:T(8,128)S(1)}) custom-call(f32[16,24,128]{2,1,0:T(8,128)S(1)} %all_to_all.38.parts, bf16[256,512]{1,0:T(8,128)(2,1)S(1)} %bitcast.21, s32[256,128]{1,0:T(8,128)S(1)} %get-tuple-element.115.b_col), custom_call_target="tpu_custom_call" | custom-call | tf_op jit(solution)/shard_map/pallas_call | solution.py:549
  65.4 0.5 slice.6
  66.5 7.7 %all-to-all-done.4.parts = f32[32,1,384]{2,1,0:T(1,128)S(1)} async-done(((f32[32,1,384]{2,1,0:T(1,128)}), f32[32,1,384]{2,1,0:T(1,128)S(1)}, u32[]{:S(2)}, u32[]{:S(2)}) %all-to-all-start.4) | async-done | bytes 49184 | tf_op jit(solution)/shard_map/all_to_all | solution.py:460
  74.2 0.8 shard_map.120
  75.0 12.2 %all_to_all.39.parts = f32[32,4,128]{2,1,0:T(4,128)S(1)} all-to-all(f32[32,4,128]{2,1,0:T(4,128)S(1)} %get-tuple-element.130), channel_id=1, replica_groups={{0,1,32,33,64,65,96,97,128,129,160,161,192,193,224,225,256,257,288,289,..., dimensions={0} | all-to-all | bytes 131072 | tf_op jit(solution)/shard_map/all_to_all | solution.py:460
  87.3 0.1 shard_map.121
  87.4 14.1 %all_to_all.40.parts = f32[16,1,128]{2,1,0:T(1,128)S(1)} all-to-all(f32[16,1,128]{2,1,0:T(1,128)S(1)} %shard_map.121), channel_id=1, replica_groups={{0,2,4,6,8,10,12,14,16,18,20,22,24,26,28,30},{1,3,5,7,9,11,13,15,17,19,..., dimensions={0} | all-to-all | bytes 16384 | tf_op jit(solution)/shard_map/all_to_all | solution.py:460
  101.5 0.1 shard_map.122
  101.6 0.5 slice_bitcast_fusion
  (14 shorter events, 0.1 us)
Async XLA Ops:
  0.6 0.7 copy-start.6
  1.3 0.9 copy-start
  2.5 18.2 %copy-start.2 = (f32[32,1024]{1,0:T(8,128)S(1)}, f32[32,1024]{1,0:T(8,128)}, u32[]{:S(2)}) copy-start(f32[32,1024]{1,0:T(8,128)} %measured) | copy-start | bytes 393220
  20.6 3.9 %copy-start.1 = (s32[8192]{0:T(1024)S(1)}, s32[8192]{0:T(1024)}, u32[]{:S(2)}) copy-start(s32[8192]{0:T(1024)} %param.19) | copy-start | bytes 98308
  20.6 3.9 %copy-start.3 = (s32[8192]{0:T(1024)S(1)}, s32[8192]{0:T(1024)}, u32[]{:S(2)}) copy-start(s32[8192]{0:T(1024)} %param.18) | copy-start | bytes 98308
  20.6 4.0 %copy-start.4 = (s32[8192]{0:T(1024)S(1)}, s32[8192]{0:T(1024)}, u32[]{:S(2)}) copy-start(s32[8192]{0:T(1024)} %param.20) | copy-start | bytes 98308
  22.0 4.2 %collective-permute-start = (bf16[288,128]{1,0:T(8,128)(2,1)S(1)}, bf16[288,128]{1,0:T(8,128)(2,1)S(1)}, u32[]{:S(2)}, u32[]{:S(2)}) collective-permute-start(bf16[288,128]{1,0:T(8,128)(2,1)S(1)} %get-tuple-element.94), channel_id=1, source_target_pairs={{0,1},{1,2},{2,3},{3,4},{4,5},{5,6},{6,7},{7,8},{8,9},{9,10},{10,1... | collective-permute-start | bytes 221192 | tf_op jit(solution)/shard_map/ppermute | solution.py:499
  23.3 6.0 %collective-permute-start.1 = (bf16[288,128]{1,0:T(8,128)(2,1)S(1)}, bf16[288,128]{1,0:T(8,128)(2,1)S(1)}, u32[]{:S(2)}, u32[]{:S(2)}) collective-permute-start(bf16[288,128]{1,0:T(8,128)(2,1)S(1)} %get-tuple-element.95), channel_id=1, source_target_pairs={{1,0},{2,1},{3,2},{4,3},{5,4},{6,5},{7,6},{8,7},{9,8},{10,9},{11,1... | collective-permute-start | bytes 221192 | tf_op jit(solution)/shard_map/ppermute | solution.py:500
  43.8 18.0 %copy-start.9 = (bf16[1,256,4,128]{3,2,1,0:T(4,128)(2,1)S(1)}, bf16[1,256,4,128]{3,2,1,0:T(4,128)(2,1)}, u32[]{:S(2)}) copy-start(bf16[1,256,4,128]{3,2,1,0:T(4,128)(2,1)} %param.17) | copy-start | bytes 786436
  44.4 29.8 %all-to-all-start.4 = ((f32[32,1,384]{2,1,0:T(1,128)}), f32[32,1,384]{2,1,0:T(1,128)S(1)}, u32[]{:S(2)}, u32[]{:S(2)}) async-start(f32[32,1,384]{2,1,0:T(1,128)} %shard_map.119), calls=%async_computation.4 | async-start | bytes 98304 | tf_op jit(solution)/shard_map/all_to_all | solution.py:460
  61.8 0.8 copy-start.5
  61.8 0.8 copy-start.8
  61.9 0.7 copy-start.7

commit v15 on v10

--- a/solution.py
+++ b/solution.py
@@ -98,23 +98,24 @@
     place = jnp.where(names[:SLOTS] >= 0, place, -1.0)
     q_col[...] = place.astype(I32)
     q_row[...] = jnp.transpose(place)[0:8, :].astype(I32)
-    both = jnp.zeros((TILES, 1), F32)
-    for r in range(0, 64, 8):
-        tiles = jnp.zeros((TILES, CB), F32)
-        for i in range(r, r + 8):
-            tiles = tiles + (iota((TILES, CB), 0) == tile[i : i + 1, :]).astype(F32)
-        both = both + lane_sum(tiles)
-    top = jnp.max(both, axis=0, keepdims=True)
+    held = jnp.zeros((TILES, CB), F32)
+    for r in range(64):
+        here = lane_sum((iota((TILES, CB), 0) == tile[r : r + 1, :]).astype(F32))
+        held = jnp.where(iota((TILES, CB), 1) == r, here, held)
+    top = jnp.max(lane_sum(held), axis=0, keepdims=True)
     most[...] = jnp.broadcast_to(top, (8, CB)).astype(I32)
-    wide = jnp.concatenate([both, jnp.zeros((CB - TILES, 1), F32)], axis=0)
-    held = jnp.transpose(jnp.broadcast_to(wide, (CB, CB)))[0:1, :]
-    earlier = lane_sum(jnp.where(iota((NAMES, CB), 1) < n_tile, held, 0.0))
-    keys = tile * NEURONS + number
-    high = jnp.broadcast_to(n_tile * NEURONS, (NAMES, CB)) + names
-    count = jnp.zeros((NAMES, CB), F32)
-    for r in range(64):
-        count = count + jnp.where(keys[r : r + 1, :] < high, 1.0, 0.0)
-    position = jnp.broadcast_to(lane_sum(count) - earlier, (NAMES, CB)).astype(I32)
+    before = (iota((CB, CB), 0) < iota((CB, CB), 1)).astype(F32).astype(BF16)
+    earlier = jnp.dot(held.astype(BF16), before, preferred_element_type=F32)
+    row_hot = (iota((NAMES, CB), 1) == (names >> 7)).astype(F32).astype(BF16)
+    counts = jnp.zeros((NAMES, TILES), F32)
+    for part in split2(earlier):
+        counts = counts + lax.dot_general(
+            row_hot, part, (((1,), (1,)), ((), ())), preferred_element_type=F32
+        )
+    count = lane_sum(jnp.where(iota((NAMES, TILES), 1) == n_tile, counts, 0.0))
+    inside = (found[:, :CB] == picked[0]) & (iota((NAMES, CB), 1) < (names & 127))
+    count = count + lane_sum(jnp.where(inside, 1.0, 0.0))
+    position = jnp.broadcast_to(count, (NAMES, CB)).astype(I32)
     turn = jnp.zeros((NAMES, CB), I32)
     for i in range(1, (NEURONS + CAP - 1) // CAP):
         turn = turn + (position >= i * CAP).astype(I32)

time: 102 us -> 102 us (level)
  waiting for transfers between devices: 10.9 us -> 12 us
  Pallas kernels: 8.95 us -> 7.88 us
    ppermute x1, waiting for transfers between devices: 0.71 us -> 1.8 us  [body(): right = lax.ppermute(up, 'tile', [(i + 1, i) for i in range(TILES - 1)])]
    pallas_call x1, Pallas kernels: 3.08 us -> 2.01 us  [body(): call(prepare_kernel, [((SLOTS, SLOTS), F32), ((8, SLOTS), I32), column, c...]
  transfers between devices with their start and end apart: 3 -> 3, of which waited for: 2 -> 2; matrix products, arithmetic and copies ran while one was open for 1% -> 1% of each run, Pallas kernels for 4% -> 3%
where the time goes in v15:
time: 102 us
  blocking collectives  57 us (56%)
  starting transfers between devices  20 us (20%)
  waiting for transfers between devices  12 us (12%)
  Pallas kernels  7.88 us (8%)
  local copies, waits for them, and re-layouts  3.39 us (3%)
  between operations  1.46 us (1%)
    all_to_all x4, blocking collectives, swap(): return lax.all_to_all(pieces, axis, 0, 0, axis_index_groups=groups)  57 us
    all_to_all x1, starting transfers between devices, swap(): return lax.all_to_all(pieces, axis, 0, 0, axis_index_groups=groups)  17.4 us
    all_to_all x1, waiting for transfers between devices, swap(): return lax.all_to_all(pieces, axis, 0, 0, axis_index_groups=groups)  10.2 us
    unnamed x21, local copies, waits for them, and re-layouts  2.35 us
  transfers between devices with their start and end apart: 3, of which 2 were waited for; matrix products, arithmetic and copies ran while one was open for 1% of the time, Pallas kernels for 3%

profile of v15, /device:TPU:1, one launch (start us, length us, event | category | flops | bytes accessed | tf_op | source)
XLA Modules:
  0.0 101.8 jit_solution(12646147589816739291)
XLA Ops:
  0.7 0.7 copy-done.6
  1.3 0.9 copy-done
  2.2 0.1 shard_map.113
  2.4 0.1 pad_add_fusion.where
  2.5 18.2 %all_to_all.37 = f32[16,32,128]{2,1,0:T(8,128)S(1)} all-to-all(f32[16,32,128]{2,1,0:T(8,128)S(1)} %shard_map.113), channel_id=1, replica_groups=mesh['depth'=16,'tile'=32] {'depth'}, dimensions={0} | all-to-all | bytes 524288 | tf_op jit(solution)/shard_map/all_to_all | solution.py:453
  20.6 1.3 %shard_map.114 = (f32[512,128]{1,0:T(8,128)S(1)}, f32[32,128]{1,0:T(8,128)S(1)}, bf16[288,128]{1,0:T(8,128)(2,1)S(1)}, bf16[288,128]{1,0:T(8,128)(2,1)S(1)}, bf1...) custom-call(s32[3]{0:T(128)S(1)} %pad_add_fusion.where, ...), custom_call_target="tpu_custom_call" | custom-call | tf_op jit(solution)/shard_map/pallas_call | solution.py:481
  21.9 1.3 %collective-permute-start = (bf16[288,128]{1,0:T(8,128)(2,1)S(1)}, bf16[288,128]{1,0:T(8,128)(2,1)S(1)}, u32[]{:S(2)}, u32[]{:S(2)}) collective-permute-start(bf16[288,128]{1,0:T(8,128)(2,1)S(1)} %get-tuple-element.91), channel_id=1, source_target_pairs={{0,1},{1,2},{2,3},{3,4},{4,5},{5,6},{6,7},{7,8},{8,9},{9,10},{10,1... | collective-permute-start | bytes 221192 | tf_op jit(solution)/shard_map/ppermute | solution.py:492
  23.2 1.3 %collective-permute-start.1 = (bf16[288,128]{1,0:T(8,128)(2,1)S(1)}, bf16[288,128]{1,0:T(8,128)(2,1)S(1)}, u32[]{:S(2)}, u32[]{:S(2)}) collective-permute-start(bf16[288,128]{1,0:T(8,128)(2,1)S(1)} %get-tuple-element.92), channel_id=1, source_target_pairs={{1,0},{2,1},{3,2},{4,3},{5,4},{6,5},{7,6},{8,7},{9,8},{10,9},{11,1... | collective-permute-start | bytes 221192 | tf_op jit(solution)/shard_map/ppermute | solution.py:493
  24.5 0.0 copy-start.2
  24.6 0.0 copy-start.3
  24.6 0.0 copy-start.4
  24.6 0.0 copy-start.5
  24.7 0.6 copy-done.2
  25.3 0.0 copy-done.3
  25.3 0.0 copy-done.4
  25.3 0.0 copy-done.5
  25.4 2.0 %shard_map.115 = (f32[256,256]{1,0:T(8,128)S(1)}, s32[8,256]{1,0:T(8,128)S(1)}, s32[256,128]{1,0:T(8,128)S(1)}, s32[256,128]{1,0:T(8,128)S(1)}, s32[272,128]{1,0...) custom-call(s32[3]{0:T(128)S(1)} %pad_add_fusion.where, ...), custom_call_target="tpu_custom_call" | custom-call | tf_op jit(solution)/shard_map/pallas_call | solution.py:498
  27.4 0.0 collective-permute-done.left
  27.4 1.8 %collective-permute-done.1.right = bf16[288,128]{1,0:T(8,128)(2,1)S(1)} collective-permute-done((bf16[288,128]{1,0:T(8,128)(2,1)S(1)}, bf16[288,128]{1,0:T(8,128)(2,1)S(1)}, u32[]{:S(2)}, u32[]{:S(2)}) %collective-permute-start.1) | collective-permute-done | bytes 73760 | tf_op jit(solution)/shard_map/ppermute | solution.py:493
  29.2 1.8 %shard_map.116 = (f32[16,24,128]{2,1,0:T(8,128)S(1)}, f32[256,128]{1,0:T(8,128)S(1)}) custom-call(f32[512,128]{1,0:T(8,128)S(1)} %get-tuple-element.90.own, bf16[288,128]{1,0:T(8,128)(2,1)S(1)} %collective-permute-done.left, bf16[288,128]{1,0:T(8,128)(2,1)S(1)} %collective-permute-done.1.right, f32[32,128]{1,0:T(8,128)S(1)} %get-tuple-element.93.sensor, ...), custom_call_target="tpu_custom_call" | custom-call | tf_op jit(solution)/shard_map/pallas_call | solution.py:524
  30.9 12.8 %all_to_all.38.parts = f32[16,24,128]{2,1,0:T(8,128)S(1)} all-to-all(f32[16,24,128]{2,1,0:T(8,128)S(1)} %get-tuple-element.106), channel_id=1, replica_groups=mesh['depth'=16,'tile'=32] {'depth'}, dimensions={0} | all-to-all | bytes 393216 | tf_op jit(solution)/shard_map/all_to_all | solution.py:453
  43.7 0.6 shard_map.118
  44.4 17.4 %all-to-all-start.4 = ((f32[32,1,384]{2,1,0:T(1,128)}), f32[32,1,384]{2,1,0:T(1,128)S(1)}, u32[]{:S(2)}, u32[]{:S(2)}) async-start(f32[32,1,384]{2,1,0:T(1,128)} %shard_map.118), calls=%async_computation.4 | async-start | bytes 98304 | tf_op jit(solution)/shard_map/all_to_all | solution.py:453
  61.8 0.5 slice.6
  63.0 1.0 %shard_map.117 = (f32[32,1024]{1,0:T(8,128)}, f32[256,128]{1,0:T(8,128)S(1)}) custom-call(f32[16,24,128]{2,1,0:T(8,128)S(1)} %all_to_all.38.parts, bf16[256,512]{1,0:T(8,128)(2,1)S(1)} %bitcast.22, s32[256,128]{1,0:T(8,128)S(1)} %get-tuple-element.109.b_col), custom_call_target="tpu_custom_call" | custom-call | tf_op jit(solution)/shard_map/pallas_call | solution.py:559
  64.0 10.2 %all-to-all-done.4.parts = f32[32,1,384]{2,1,0:T(1,128)S(1)} async-done(((f32[32,1,384]{2,1,0:T(1,128)}), f32[32,1,384]{2,1,0:T(1,128)S(1)}, u32[]{:S(2)}, u32[]{:S(2)}) %all-to-all-start.4) | async-done | bytes 49184 | tf_op jit(solution)/shard_map/all_to_all | solution.py:453
  74.2 0.8 shard_map.119
  75.0 12.2 %all_to_all.39.parts = f32[32,4,128]{2,1,0:T(4,128)S(1)} all-to-all(f32[32,4,128]{2,1,0:T(4,128)S(1)} %get-tuple-element.124), channel_id=1, replica_groups={{0,1,32,33,64,65,96,97,128,129,160,161,192,193,224,225,256,257,288,289,..., dimensions={0} | all-to-all | bytes 131072 | tf_op jit(solution)/shard_map/all_to_all | solution.py:453
  87.2 0.1 shard_map.120
  87.4 13.8 %all_to_all.40.parts = f32[16,1,128]{2,1,0:T(1,128)S(1)} all-to-all(f32[16,1,128]{2,1,0:T(1,128)S(1)} %shard_map.120), channel_id=1, replica_groups={{0,2,4,6,8,10,12,14,16,18,20,22,24,26,28,30},{1,3,5,7,9,11,13,15,17,19,..., dimensions={0} | all-to-all | bytes 16384 | tf_op jit(solution)/shard_map/all_to_all | solution.py:453
  101.2 0.1 shard_map.121
  101.3 0.5 slice_bitcast_fusion
  (13 shorter events, 0.1 us)
Async XLA Ops:
  0.6 0.7 copy-start.6
  1.3 0.9 copy-start
  2.5 18.2 %copy-start.1 = (f32[32,1024]{1,0:T(8,128)S(1)}, f32[32,1024]{1,0:T(8,128)}, u32[]{:S(2)}) copy-start(f32[32,1024]{1,0:T(8,128)} %measured) | copy-start | bytes 393220
  20.6 3.9 %copy-start.9 = (bf16[1,256,4,128]{3,2,1,0:T(4,128)(2,1)S(1)}, bf16[1,256,4,128]{3,2,1,0:T(4,128)(2,1)}, u32[]{:S(2)}) copy-start(bf16[1,256,4,128]{3,2,1,0:T(4,128)(2,1)} %param.17) | copy-start | bytes 786436
  21.9 5.5 %collective-permute-start = (bf16[288,128]{1,0:T(8,128)(2,1)S(1)}, bf16[288,128]{1,0:T(8,128)(2,1)S(1)}, u32[]{:S(2)}, u32[]{:S(2)}) collective-permute-start(bf16[288,128]{1,0:T(8,128)(2,1)S(1)} %get-tuple-element.91), channel_id=1, source_target_pairs={{0,1},{1,2},{2,3},{3,4},{4,5},{5,6},{6,7},{7,8},{8,9},{9,10},{10,1... | collective-permute-start | bytes 221192 | tf_op jit(solution)/shard_map/ppermute | solution.py:492
  23.2 6.0 %collective-permute-start.1 = (bf16[288,128]{1,0:T(8,128)(2,1)S(1)}, bf16[288,128]{1,0:T(8,128)(2,1)S(1)}, u32[]{:S(2)}, u32[]{:S(2)}) collective-permute-start(bf16[288,128]{1,0:T(8,128)(2,1)S(1)} %get-tuple-element.92), channel_id=1, source_target_pairs={{1,0},{2,1},{3,2},{4,3},{5,4},{6,5},{7,6},{8,7},{9,8},{10,9},{11,1... | collective-permute-start | bytes 221192 | tf_op jit(solution)/shard_map/ppermute | solution.py:493
  24.5 0.8 copy-start.2
  24.6 0.8 copy-start.3
  24.6 0.8 copy-start.4
  24.6 0.8 copy-start.5
  24.6 0.8 copy-start.8
  24.7 0.7 copy-start.7
  44.4 29.8 %all-to-all-start.4 = ((f32[32,1,384]{2,1,0:T(1,128)}), f32[32,1,384]{2,1,0:T(1,128)S(1)}, u32[]{:S(2)}, u32[]{:S(2)}) async-start(f32[32,1,384]{2,1,0:T(1,128)} %shard_map.118), calls=%async_computation.4 | async-start | bytes 98304 | tf_op jit(solution)/shard_map/all_to_all | solution.py:453
